TPU v7x, 32 devices: a whole 2x2x4 slice. The times are simulated.
32 devices in a mesh: group: 8 (over z, y), mp: 4 (over x, core).
Axes of the slice: x: 2, y: 2, z: 4, core: 2. Of those that a mesh axis runs over, the one named last changes fastest.
Arguments:
- tokens: bfloat16 [16, 1024, 1152], P('group', 'mp'), may hold values from -6 to 6
- cotangent: bfloat16 [16, 1024, 1152], P('group', 'mp'), may hold values from -6 to 6
- key_mask: int32 [16, 1024], P('group'), may hold values from 0 to 1, as said below
- group_bucket: int32 [8], P('group'), may hold values from 0 to 15
- group_count: int32 [8], P('group'), may hold values from 1 to 2, as said below
- time_table: float32 [16, 1152], replicated, may hold values from -6 to 6
- ln_params: float32 [2, 4, 1152], replicated, may hold values from -1.5 to 2.1, as said below
- ln_first: float32 [2, 4, 1152], replicated, may hold values from -96 to 96
- ln_second: float32 [2, 4, 1152], replicated, may hold values from 128 to 1024
- rel_table: float32 [2, 16, 2, 63], replicated, may hold values from -5 to 5
- rel_first: float32 [2, 16, 2, 63], replicated, may hold values from -20 to 20
- rel_second: float32 [2, 16, 2, 63], replicated, may hold values from 6.4 to 25.6
- qkv_weight: float32 [2, 1152, 3, 1152], P(None, 'group', None, 'mp')
- qkv_first: float32 [2, 1152, 3, 1152], P(None, 'group', None, 'mp'), may hold values from -96 to 96
- qkv_second: float32 [2, 1152, 3, 1152], P(None, 'group', None, 'mp'), may hold values from 128 to 1024
- time_weight: float32 [2, 1152, 2, 1152], P(None, 'group', None, 'mp')
- time_first: float32 [2, 1152, 2, 1152], P(None, 'group', None, 'mp'), may hold values from -96 to 96
- time_second: float32 [2, 1152, 2, 1152], P(None, 'group', None, 'mp'), may hold values from 128 to 1024
- out_weight: float32 [2, 1152, 1152], P(None, 'mp', 'group')
- out_first: float32 [2, 1152, 1152], P(None, 'mp', 'group'), may hold values from -96 to 96
- out_second: float32 [2, 1152, 1152], P(None, 'mp', 'group'), may hold values from 128 to 1024
- up_weight: float32 [2, 1152, 4608], P(None, 'group', 'mp')
- up_first: float32 [2, 1152, 4608], P(None, 'group', 'mp'), may hold values from -96 to 96
- up_second: float32 [2, 1152, 4608], P(None, 'group', 'mp'), may hold values from 128 to 1024
- down_weight: float32 [2, 4608, 1152], P(None, 'mp', 'group')
- down_first: float32 [2, 4608, 1152], P(None, 'mp', 'group'), may hold values from -96 to 96
- down_second: float32 [2, 4608, 1152], P(None, 'mp', 'group'), may hold values from 128 to 1024
Outputs:
- block_out: bfloat16 [16, 1024, 1152], P('group', 'mp')
- tokens_grad: bfloat16 [16, 1024, 1152], P('group', 'mp')
- ln_new: float32 [2, 4, 1152], replicated
- ln_first_new: float32 [2, 4, 1152], replicated
- ln_second_new: float32 [2, 4, 1152], replicated
- rel_new: float32 [2, 16, 2, 63], replicated
- rel_first_new: float32 [2, 16, 2, 63], replicated
- rel_second_new: float32 [2, 16, 2, 63], replicated
- qkv_new: float32 [2, 1152, 3, 1152], P(None, 'group', None, 'mp')
- qkv_first_new: float32 [2, 1152, 3, 1152], P(None, 'group', None, 'mp')
- qkv_second_new: float32 [2, 1152, 3, 1152], P(None, 'group', None, 'mp')
- qkv_copy: bfloat16 [2, 1152, 3, 1152], P(None, 'group', None, 'mp')
- time_new: float32 [2, 1152, 2, 1152], P(None, 'group', None, 'mp')
- time_first_new: float32 [2, 1152, 2, 1152], P(None, 'group', None, 'mp')
- time_second_new: float32 [2, 1152, 2, 1152], P(None, 'group', None, 'mp')
- time_copy: bfloat16 [2, 1152, 2, 1152], P(None, 'group', None, 'mp')
- out_new: float32 [2, 1152, 1152], P(None, 'mp', 'group')
- out_first_new: float32 [2, 1152, 1152], P(None, 'mp', 'group')
- out_second_new: float32 [2, 1152, 1152], P(None, 'mp', 'group')
- out_copy: bfloat16 [2, 1152, 1152], P(None, 'mp', 'group')
- up_new: float32 [2, 1152, 4608], P(None, 'group', 'mp')
- up_first_new: float32 [2, 1152, 4608], P(None, 'group', 'mp')
- up_second_new: float32 [2, 1152, 4608], P(None, 'group', 'mp')
- up_copy: bfloat16 [2, 1152, 4608], P(None, 'group', 'mp')
- down_new: float32 [2, 4608, 1152], P(None, 'mp', 'group')
- down_first_new: float32 [2, 4608, 1152], P(None, 'mp', 'group')
- down_second_new: float32 [2, 4608, 1152], P(None, 'mp', 'group')
- down_copy: bfloat16 [2, 4608, 1152], P(None, 'mp', 'group')
- matrix_stats: float32 [3, 2, 5], replicated
Inputs may be any that keep to these rules, and one draw needn't show every extreme that they name: Group g's live images are its first group_count[g] slots; in every draw some group has all 2 slots live and another only one. `key_mask`: an image's live keys are its first 256 positions or all 1024 of them; in every group some live image has all positions live. `ln_params`: rows 0 and 2 of each layer are positive gains, rows 1 and 3 are shifts.
All inputs are finite; a program needn't handle non-finite values.
Results may differ from a plain program's by a relative error of at most 0.02.
Values may be sent and summed in bfloat16 or wider, within the bound.
No kernel may reach another device: no remote copies, remote signals or barrier semaphores. Data moves between devices by JAX's collectives and lax.ppermute only.
A program may use at most 320 MiB of HBM per device.

v0:
```python
import jax
import jax.numpy as jnp
from jax import lax
from jax.sharding import PartitionSpec as P

STEP = 5


highest = lax.Precision.HIGHEST
norm_epsilon = 1e-05
adam_epsilon = 1e-06
beta_first = 0.5
beta_second = 0.5
decay_rate = 0.01
learn_rate = 0.5


def layer_norm(inputs, norm_gain, norm_shift):
    average = jnp.mean(inputs, axis=-1, keepdims=True)
    centred = inputs - average
    scaling = lax.rsqrt(jnp.mean(centred * centred, axis=-1, keepdims=True) + norm_epsilon)
    normed = centred * scaling
    return (normed * norm_gain + norm_shift, normed, scaling)


def norm_back(gradient, normed, scaling, norm_gain):
    scaled = gradient * norm_gain
    centred_grad = scaled - jnp.mean(scaled, axis=-1, keepdims=True)
    centred_grad = centred_grad - normed * jnp.mean(scaled * normed, axis=-1, keepdims=True)
    return centred_grad * scaling


def offset_onehot(grid_side):
    places = jnp.arange(grid_side)
    offset = places[:, None] - places[None, :] + grid_side - 1
    return (offset[:, :, None] == jnp.arange(2 * grid_side - 1)[None, None, :]).astype(jnp.float32)


def gelu_slope(pre_act, gradient):
    return jax.vjp(lambda argument: jax.nn.gelu(argument, approximate=True), pre_act)[1](gradient)[
        0
    ]


def lamb_moments(param, first, second, gradient):
    first_new = beta_first * first + (1.0 - beta_first) * gradient
    second_new = beta_second * second + (1.0 - beta_second) * gradient * gradient
    corrected = first_new / (1.0 - beta_first**STEP)
    update = (
        corrected / (jnp.sqrt(second_new / (1.0 - beta_second**STEP)) + adam_epsilon)
        + decay_rate * param
    )
    return (first_new, second_new, update)


def block_scores(queries, keyset, live_keys, row_bias, col_bias, offset):
    head_count = queries.shape[1]
    grid_side = row_bias.shape[1]
    query_rows = queries.shape[0] // grid_side
    key_rows = keyset.shape[0] // grid_side
    products = jnp.einsum("qhd,khd->hqk", queries, keyset, preferred_element_type=jnp.float32)
    first_row = offset // grid_side
    row_part = row_bias[:, first_row : first_row + query_rows, :key_rows]
    rel_bias = (row_part[:, :, None, :, None] + col_bias[:, None, :, None, :]).reshape(
        head_count, queries.shape[0], keyset.shape[0]
    )
    scores = products * queries.shape[2] ** (-0.5) + rel_bias
    return jnp.where(live_keys[None, None, :] > 0, scores, -1e30)


def attend_image(queries, keyset, values, live_keys, row_bias, col_bias, block_rows):
    outputs = []
    log_sums = []
    for offset in range(0, queries.shape[0], block_rows):
        scores = block_scores(
            queries[offset : offset + block_rows], keyset, live_keys, row_bias, col_bias, offset
        )
        row_max = jnp.max(scores, axis=-1, keepdims=True)
        weights_exp = jnp.exp(scores - row_max)
        row_total = jnp.sum(weights_exp, axis=-1, keepdims=True)
        softmax_out = (weights_exp / row_total).astype(jnp.bfloat16)
        attended = jnp.einsum(
            "hqk,khd->qhd", softmax_out, values, preferred_element_type=jnp.float32
        )
        outputs.append(attended.astype(jnp.bfloat16))
        log_sums.append((row_max + jnp.log(row_total))[:, :, 0])
    return (jnp.concatenate(outputs, axis=0), jnp.concatenate(log_sums, axis=1))


def attend_back(
    queries,
    keyset,
    values,
    live_keys,
    grad_out,
    log_sums,
    row_bias,
    col_bias,
    key_count,
    block_rows,
):
    head_count = queries.shape[1]
    grid_side = row_bias.shape[1]
    key_rows = key_count // grid_side
    query_rows = block_rows // grid_side
    scaling = queries.shape[2] ** (-0.5)
    grad_keys = jnp.zeros((key_count,) + queries.shape[1:], jnp.float32)
    grad_values = jnp.zeros_like(grad_keys)
    grad_rows = jnp.zeros((head_count, grid_side, grid_side), jnp.float32)
    grad_cols = jnp.zeros_like(grad_rows)
    grad_parts = []
    for offset in range(0, queries.shape[0], block_rows):
        query_block = queries[offset : offset + block_rows]
        scores = block_scores(query_block, keyset, live_keys, row_bias, col_bias, offset)
        softmax_full = jnp.exp(scores - log_sums[:, offset : offset + block_rows, None])
        grad_block = grad_out[offset : offset + block_rows]
        grad_values = grad_values + jnp.einsum(
            "hqk,qhd->khd",
            softmax_full.astype(jnp.bfloat16),
            grad_block,
            preferred_element_type=jnp.float32,
        )
        grad_probs = jnp.einsum(
            "qhd,khd->hqk", grad_block, values, preferred_element_type=jnp.float32
        )
        grad_scores = (
            softmax_full * (grad_probs - jnp.sum(grad_probs * softmax_full, axis=-1, keepdims=True))
        ).astype(jnp.bfloat16)
        grad_parts.append(
            jnp.einsum("hqk,khd->qhd", grad_scores, keyset, preferred_element_type=jnp.float32)
            * scaling
        )
        grad_keys = (
            grad_keys
            + jnp.einsum(
                "hqk,qhd->khd", grad_scores, query_block, preferred_element_type=jnp.float32
            )
            * scaling
        )
        grid_grads = grad_scores.astype(jnp.float32).reshape(
            head_count, query_rows, grid_side, key_rows, grid_side
        )
        first_row = offset // grid_side
        grad_rows = grad_rows.at[:, first_row : first_row + query_rows, :key_rows].add(
            jnp.sum(grid_grads, axis=(2, 4))
        )
        grad_cols = grad_cols + jnp.sum(grid_grads, axis=(1, 3))
    padding = ((0, queries.shape[0] - key_count), (0, 0), (0, 0))
    return (
        jnp.concatenate(grad_parts, axis=0),
        jnp.pad(grad_keys, padding),
        jnp.pad(grad_values, padding),
        grad_rows,
        grad_cols,
    )


def shards(
    tokens,
    cotangent,
    key_mask,
    group_bucket,
    group_count,
    time_table,
    ln_params,
    ln_first,
    ln_second,
    rel_table,
    rel_first,
    rel_second,
    qkv_weight,
    qkv_first,
    qkv_second,
    time_weight,
    time_first,
    time_second,
    out_weight,
    out_first,
    out_second,
    up_weight,
    up_first,
    up_second,
    down_weight,
    down_first,
    down_second,
):
    slot_count = tokens.shape[0]
    seq_len = key_mask.shape[1]
    layers = ln_params.shape[0]
    local_heads = rel_table.shape[1] // lax.axis_size("mp")
    local_width = qkv_weight.shape[3]
    head_size = local_width // local_heads
    grid_side = (rel_table.shape[3] + 1) // 2
    block_rows = min(512, seq_len)
    head_start = lax.axis_index("mp") * local_heads
    onehot = offset_onehot(grid_side)
    bucket_hit = (jnp.arange(time_table.shape[0]) == group_bucket[0]).astype(jnp.float32)
    time_row = jnp.dot(bucket_hit, time_table, precision=highest).astype(jnp.bfloat16)

    def whole_rows(part_rows):
        return lax.all_gather(part_rows, "mp", axis=1, tiled=True)

    def row_sums(partial_value):
        return lax.psum_scatter(
            partial_value.astype(jnp.bfloat16), "mp", scatter_dimension=1, tiled=True
        ).astype(jnp.float32)

    def branch_out(activation, w_part):
        return row_sums(
            jnp.einsum("snf,fd->snd", activation, w_part, preferred_element_type=jnp.float32)
        )

    def head_bias(layer_index):
        rel_part = lax.dynamic_slice_in_dim(rel_table[layer_index], head_start, local_heads, 0)
        row_bias = jnp.einsum("abr,hr->hab", onehot, rel_part[:, 0], precision=highest)
        col_bias = jnp.einsum("abr,hr->hab", onehot, rel_part[:, 1], precision=highest)
        return (row_bias, col_bias)

    state = tokens.astype(jnp.float32)
    saved = []
    kept_weights = []
    for layer_index in range(layers):
        fetched = (
            lax.all_gather(
                qkv_weight[layer_index].astype(jnp.bfloat16), "group", axis=0, tiled=True
            ),
            lax.all_gather(
                time_weight[layer_index].astype(jnp.bfloat16), "group", axis=0, tiled=True
            ),
            lax.all_gather(
                out_weight[layer_index].astype(jnp.bfloat16), "group", axis=1, tiled=True
            ),
            lax.all_gather(
                up_weight[layer_index].astype(jnp.bfloat16), "group", axis=0, tiled=True
            ),
            lax.all_gather(
                down_weight[layer_index].astype(jnp.bfloat16), "group", axis=1, tiled=True
            ),
        )
        w_qkv, w_time, w_out, w_up, w_down = fetched
        norm_params = ln_params[layer_index]
        first_norm, normed_one, scaling_one = layer_norm(state, norm_params[0], norm_params[1])
        gathered_one = whole_rows(first_norm.astype(jnp.bfloat16))
        time_shift = jnp.einsum("d,dcf->cf", time_row, w_time, preferred_element_type=jnp.float32)
        project = jnp.einsum(
            "snd,dcf->sncf", gathered_one, w_qkv, preferred_element_type=jnp.float32
        )
        head_shape = (slot_count, seq_len, local_heads, head_size)
        queries = (project[:, :, 0] + time_shift[0]).astype(jnp.bfloat16).reshape(head_shape)
        keyset = project[:, :, 1].astype(jnp.bfloat16).reshape(head_shape)
        values = (project[:, :, 2] + time_shift[1]).astype(jnp.bfloat16).reshape(head_shape)
        row_bias, col_bias = head_bias(layer_index)

        def image_forward(members):

            def run_keys(key_count):
                return attend_image(
                    members[0], members[1], members[2], members[3], row_bias, col_bias, block_rows
                )

            return run_keys(seq_len)

        attended, log_sums = lax.map(image_forward, (queries, keyset, values, key_mask))
        mixed = attended.reshape(slot_count, seq_len, local_width)
        middle = state + branch_out(mixed, w_out)
        second_norm, normed_two, scaling_two = layer_norm(middle, norm_params[2], norm_params[3])
        gathered_two = whole_rows(second_norm.astype(jnp.bfloat16))
        pre_act = jnp.einsum("snd,df->snf", gathered_two, w_up, preferred_element_type=jnp.float32)
        active = jax.nn.gelu(pre_act, approximate=True).astype(jnp.bfloat16)
        state = middle + branch_out(active, w_down)
        saved.append(
            (
                normed_one,
                scaling_one,
                gathered_one,
                queries,
                keyset,
                values,
                log_sums,
                mixed,
                normed_two,
                scaling_two,
                gathered_two,
                pre_act,
                active,
            )
        )
        kept_weights.append(None)
    block_out = state.astype(jnp.bfloat16)
    slot_live = (jnp.arange(slot_count) < group_count[0]).astype(jnp.float32)
    gradient = cotangent.astype(jnp.float32) * slot_live[:, None, None]
    matrix_grads = [None] * layers
    norm_grads = [None] * layers
    rel_grads = [None] * layers
    for layer_index in reversed(range(layers)):
        (
            normed_one,
            scaling_one,
            gathered_one,
            queries,
            keyset,
            values,
            log_sums,
            mixed,
            normed_two,
            scaling_two,
            gathered_two,
            pre_act,
            active,
        ) = saved[layer_index]
        w_qkv = lax.all_gather(
            qkv_weight[layer_index].astype(jnp.bfloat16), "group", axis=0, tiled=True
        )
        w_time = lax.all_gather(
            time_weight[layer_index].astype(jnp.bfloat16), "group", axis=0, tiled=True
        )
        w_out = lax.all_gather(
            out_weight[layer_index].astype(jnp.bfloat16), "group", axis=1, tiled=True
        )
        w_up = lax.all_gather(
            up_weight[layer_index].astype(jnp.bfloat16), "group", axis=0, tiled=True
        )
        w_down = lax.all_gather(
            down_weight[layer_index].astype(jnp.bfloat16), "group", axis=1, tiled=True
        )
        norm_params = ln_params[layer_index]
        down_rows = whole_rows(gradient.astype(jnp.bfloat16))
        grad_down = jnp.einsum("snf,snd->fd", active, down_rows, preferred_element_type=jnp.float32)
        grad_active = jnp.einsum(
            "snd,fd->snf", down_rows, w_down, preferred_element_type=jnp.float32
        )
        grad_pre = gelu_slope(pre_act, grad_active).astype(jnp.bfloat16)
        grad_up = jnp.einsum(
            "snd,snf->df", gathered_two, grad_pre, preferred_element_type=jnp.float32
        )
        grad_two = row_sums(
            jnp.einsum("snf,df->snd", grad_pre, w_up, preferred_element_type=jnp.float32)
        )
        gain_two = jnp.sum(grad_two * normed_two, axis=(0, 1))
        shift_two = jnp.sum(grad_two, axis=(0, 1))
        gradient = gradient + norm_back(grad_two, normed_two, scaling_two, norm_params[2])
        out_rows = whole_rows(gradient.astype(jnp.bfloat16))
        grad_out = jnp.einsum("snf,snd->fd", mixed, out_rows, preferred_element_type=jnp.float32)
        grad_mixed = jnp.einsum(
            "snd,fd->snf", out_rows, w_out, preferred_element_type=jnp.float32
        ).astype(jnp.bfloat16)
        grad_mixed = grad_mixed.reshape(queries.shape)
        row_bias, col_bias = head_bias(layer_index)

        def image_back(members):

            def run_keys(key_count):
                return attend_back(
                    members[0],
                    members[1],
                    members[2],
                    members[3],
                    members[4],
                    members[5],
                    row_bias,
                    col_bias,
                    key_count,
                    block_rows,
                )

            return run_keys(seq_len)

        grad_query, grad_keys, grad_values, grad_rows, grad_cols = lax.map(
            image_back, (queries, keyset, values, key_mask, grad_mixed, log_sums)
        )
        flat_shape = (slot_count, seq_len, local_width)
        grad_query = grad_query.astype(jnp.bfloat16).reshape(flat_shape)
        grad_keys = grad_keys.astype(jnp.bfloat16).reshape(flat_shape)
        grad_values = grad_values.astype(jnp.bfloat16).reshape(flat_shape)
        grad_project = jnp.stack([grad_query, grad_keys, grad_values], axis=2)
        grad_qkv = jnp.einsum(
            "snd,sncf->dcf", gathered_one, grad_project, preferred_element_type=jnp.float32
        )
        shift_sums = jnp.stack(
            [
                jnp.sum(grad_query.astype(jnp.float32), axis=(0, 1)),
                jnp.sum(grad_values.astype(jnp.float32), axis=(0, 1)),
            ]
        )
        grad_time = time_row.astype(jnp.float32)[:, None, None] * shift_sums[None]
        grad_one = row_sums(
            jnp.einsum("sncf,dcf->snd", grad_project, w_qkv, preferred_element_type=jnp.float32)
        )
        gain_one = jnp.sum(grad_one * normed_one, axis=(0, 1))
        shift_one = jnp.sum(grad_one, axis=(0, 1))
        gradient = gradient + norm_back(grad_one, normed_one, scaling_one, norm_params[0])
        matrix_grads[layer_index] = (
            lax.psum_scatter(grad_qkv, "group", scatter_dimension=0, tiled=True),
            lax.psum_scatter(grad_time, "group", scatter_dimension=0, tiled=True),
            lax.psum_scatter(grad_out, "group", scatter_dimension=1, tiled=True),
            lax.psum_scatter(grad_up, "group", scatter_dimension=0, tiled=True),
            lax.psum_scatter(grad_down, "group", scatter_dimension=1, tiled=True),
        )
        norm_grads[layer_index] = jnp.stack([gain_one, shift_one, gain_two, shift_two])
        table_rows = jnp.einsum(
            "abr,hab->hr", onehot, jnp.sum(grad_rows, axis=0), precision=highest
        )
        table_cols = jnp.einsum(
            "abr,hab->hr", onehot, jnp.sum(grad_cols, axis=0), precision=highest
        )
        rel_grads[layer_index] = jnp.stack([table_rows, table_cols], axis=1)
    rel_whole = lax.dynamic_update_slice_in_dim(
        jnp.zeros(rel_table.shape, jnp.float32), jnp.stack(rel_grads), head_start, 1
    )
    first_mp = (lax.axis_index("mp") == 0).astype(jnp.float32)
    count_term = first_mp * group_count[0].astype(jnp.float32)
    norm_sum, rel_sum, count_sum = lax.psum(
        (jnp.stack(norm_grads), rel_whole, count_term), ("group", "mp")
    )
    inverse = 1.0 / count_sum
    tokens_grad = (gradient * inverse).astype(jnp.bfloat16)
    ln_first_new, ln_second_new, ln_update = lamb_moments(
        ln_params, ln_first, ln_second, norm_sum * inverse
    )
    ln_ratio = jnp.sqrt(jnp.sum(ln_params * ln_params, axis=-1, keepdims=True)) / jnp.sqrt(
        jnp.sum(ln_update * ln_update, axis=-1, keepdims=True)
    )
    ln_new = ln_params - learn_rate * ln_ratio * ln_update
    rel_first_new, rel_second_new, rel_update = lamb_moments(
        rel_table, rel_first, rel_second, rel_sum * inverse
    )
    rel_ratio = jnp.sqrt(jnp.sum(rel_table * rel_table, axis=(1, 2, 3), keepdims=True)) / jnp.sqrt(
        jnp.sum(rel_update * rel_update, axis=(1, 2, 3), keepdims=True)
    )
    rel_new = rel_table - learn_rate * rel_ratio * rel_update
    masters = (qkv_weight, time_weight, out_weight, up_weight, down_weight)
    first_olds = (qkv_first, time_first, out_first, up_first, down_first)
    second_olds = (qkv_second, time_second, out_second, up_second, down_second)
    sectioned = []
    squares = []
    for matrix_index in range(5):
        master = masters[matrix_index]
        reduced = (
            jnp.stack([matrix_grads[layer_index][matrix_index] for layer_index in range(layers)])
            * inverse
        )
        first_new, second_new, update = lamb_moments(
            master, first_olds[matrix_index], second_olds[matrix_index], reduced
        )
        summed_axes = tuple(range(1, master.ndim))
        squares.append(
            jnp.stack(
                [
                    jnp.sum(master * master, axis=summed_axes),
                    jnp.sum(update * update, axis=summed_axes),
                ]
            )
        )
        sectioned.append((first_new, second_new, update))
    totals = lax.psum(jnp.stack(squares, axis=2), ("group", "mp"))
    weight_norm = jnp.sqrt(totals[0])
    update_norm = jnp.sqrt(totals[1])
    trust_ratio = weight_norm / update_norm
    results = []
    for matrix_index in range(5):
        master = masters[matrix_index]
        first_new, second_new, update = sectioned[matrix_index]
        factor = (learn_rate * trust_ratio[:, matrix_index]).reshape(
            (layers,) + (1,) * (master.ndim - 1)
        )
        renewed = master - factor * update
        results.extend([renewed, first_new, second_new, renewed.astype(jnp.bfloat16)])
    matrix_stats = jnp.stack([weight_norm, update_norm, trust_ratio])
    return (
        block_out,
        tokens_grad,
        ln_new,
        ln_first_new,
        ln_second_new,
        rel_new,
        rel_first_new,
        rel_second_new,
        results[0],
        results[1],
        results[2],
        results[3],
        results[4],
        results[5],
        results[6],
        results[7],
        results[8],
        results[9],
        results[10],
        results[11],
        results[12],
        results[13],
        results[14],
        results[15],
        results[16],
        results[17],
        results[18],
        results[19],
        matrix_stats,
    )


def solution(mesh):
    in_specs = (
        P("group", "mp", None),
        P("group", "mp", None),
        P("group", None),
        P("group"),
        P("group"),
        P(),
        P(),
        P(),
        P(),
        P(),
        P(),
        P(),
        P(None, "group", None, "mp"),
        P(None, "group", None, "mp"),
        P(None, "group", None, "mp"),
        P(None, "group", None, "mp"),
        P(None, "group", None, "mp"),
        P(None, "group", None, "mp"),
        P(None, "mp", "group"),
        P(None, "mp", "group"),
        P(None, "mp", "group"),
        P(None, "group", "mp"),
        P(None, "group", "mp"),
        P(None, "group", "mp"),
        P(None, "mp", "group"),
        P(None, "mp", "group"),
        P(None, "mp", "group"),
    )
    out_specs = (
        P("group", "mp", None),
        P("group", "mp", None),
        P(),
        P(),
        P(),
        P(),
        P(),
        P(),
        P(None, "group", None, "mp"),
        P(None, "group", None, "mp"),
        P(None, "group", None, "mp"),
        P(None, "group", None, "mp"),
        P(None, "group", None, "mp"),
        P(None, "group", None, "mp"),
        P(None, "group", None, "mp"),
        P(None, "group", None, "mp"),
        P(None, "mp", "group"),
        P(None, "mp", "group"),
        P(None, "mp", "group"),
        P(None, "mp", "group"),
        P(None, "group", "mp"),
        P(None, "group", "mp"),
        P(None, "group", "mp"),
        P(None, "group", "mp"),
        P(None, "mp", "group"),
        P(None, "mp", "group"),
        P(None, "mp", "group"),
        P(None, "mp", "group"),
        P(),
    )
    return jax.shard_map(shards, mesh=mesh, in_specs=in_specs, out_specs=out_specs, check_vma=False)
```

profile of v0, /device:TPU:0, one launch (start us, length us, event | category | flops | bytes accessed | tf_op | source)
XLA Modules:
  0.0 3118.0 jit_solution(15085448324163622412)
XLA Ops:
  20.8 37.6 %all-gather.2 = bf16[1,288,1152]{1,2,0:T(8,128)(2,1)} all-gather(bf16[1,288,144]{1,2,0:T(8,128)(2,1)S(1)} %get-tuple-element.1056), channel_id=4, replica_groups=mesh['group'=8,'mp'=4] {'group'}, dimensions={2}, use_global_device_ids=true | all-gather | bytes 746496 | tf_op jit(solution)/shard_map/all_gather | solution.py:230
  69.0 55.5 %all-gather.43.cloned.1.call-done = bf16[1,1152,3,288]{3,1,2,0:T(8,128)(2,1)} async-done(((bf16[1,144,3,288]{3,1,2,0:T(8,128)(2,1)}), bf16[1,1152,3,288]{3,1,2,0:T(8,128)(2,1)}) %all-gather.43.cloned.1.call-update) | async-done | bytes 1990672 | tf_op jit(solution)/shard_map/all_gather | solution.py:224
  124.5 38.2 %all-gather.27.cloned.1.call-done = bf16[2,1024,1152]{2,1,0:T(8,128)(2,1)} async-done(((bf16[2,256,1152]{2,1,0:T(8,128)(2,1)}), bf16[2,1024,1152]{2,1,0:T(8,128)(2,1)}) %all-gather.27.cloned.1.call-update) | async-done | bytes 4718608 | tf_op jit(solution)/shard_map/all_gather | solution.py:201
  174.1 187.8 %while.68 = (s32[]{:T(128)}, bf16[2,1024,4,72]{1,3,2,0:T(8,128)(2,1)}, f32[2,4,1024]{2,1,0:T(4,128)S(1)}, bf16[2,1024,4,72]{1,3,2,0:T(8,128)(2,1)}, s32[2,1024]{...) while((s32[]{:T(128)}, ...), condition=%wide.region_7.8_spmd, body=%wide.region_2.7_spmd.sunk | while | flops 1251378176 | bytes 141272848 | solution.py:263
  174.3 22.1 broadcast_add_fusion.12
  196.4 26.1 add.1068
  231.6 26.1 add.1070
  268.0 22.1 broadcast_add_fusion.12
  290.1 26.1 add.1068
  325.3 26.1 add.1070
  371.8 45.7 %reduce-scatter.17.cloned.1.call-done = bf16[2,256,1152]{2,1,0:T(8,128)(2,1)} async-done(((bf16[2,1024,1152]{2,1,0:T(8,128)(2,1)}), bf16[2,256,1152]{2,1,0:T(8,128)(2,1)}) %reduce-scatter.17.cloned.1.call-update) | async-done | bytes 1179664 | tf_op jit(solution)/shard_map/reduce_scatter | solution.py:204
  424.0 51.4 %all-gather.47.cloned.1.call-done = bf16[1,1152,1152]{2,1,0:T(8,128)(2,1)} async-done(((bf16[1,144,1152]{2,1,0:T(8,128)(2,1)}), bf16[1,1152,1152]{2,1,0:T(8,128)(2,1)}) %all-gather.47.cloned.1.call-update) | async-done | bytes 2654224 | tf_op jit(solution)/shard_map/all_gather | solution.py:233
  475.4 38.1 %all-gather.29.cloned.1.call-done = bf16[2,1024,1152]{2,1,0:T(8,128)(2,1)} async-done(((bf16[2,256,1152]{2,1,0:T(8,128)(2,1)}), bf16[2,1024,1152]{2,1,0:T(8,128)(2,1)}) %all-gather.29.cloned.1.call-update) | async-done | bytes 4718608 | tf_op jit(solution)/shard_map/all_gather | solution.py:201
  525.1 46.4 %all-gather.49.cloned.1.call-done = bf16[1,1152,1152]{1,2,0:T(8,128)(2,1)} async-done(((bf16[1,1152,144]{1,2,0:T(8,128)(2,1)}), bf16[1,1152,1152]{1,2,0:T(8,128)(2,1)}) %all-gather.49.cloned.1.call-update) | async-done | bytes 2654224 | tf_op jit(solution)/shard_map/all_gather | solution.py:236
  586.3 44.8 %reduce-scatter.19.cloned.1.call-done = bf16[2,256,1152]{2,1,0:T(8,128)(2,1)} async-done(((bf16[2,1024,1152]{2,1,0:T(8,128)(2,1)}), bf16[2,256,1152]{2,1,0:T(8,128)(2,1)}) %reduce-scatter.19.cloned.1.call-update) | async-done | bytes 1179664 | tf_op jit(solution)/shard_map/reduce_scatter | solution.py:204
  638.4 35.9 %all-gather.7 = bf16[1,288,1152]{1,2,0:T(8,128)(2,1)} all-gather(bf16[1,288,144]{1,2,0:T(8,128)(2,1)S(1)} %copy-done.90), channel_id=9, replica_groups=mesh['group'=8,'mp'=4] {'group'}, dimensions={2}, use_global_device_ids=true | all-gather | bytes 746496 | tf_op jit(solution)/shard_map/all_gather | solution.py:230
  687.2 54.7 %all-gather.51.cloned.1.call-done = bf16[1,1152,3,288]{3,1,2,0:T(8,128)(2,1)} async-done(((bf16[1,144,3,288]{3,1,2,0:T(8,128)(2,1)}), bf16[1,1152,3,288]{3,1,2,0:T(8,128)(2,1)}) %all-gather.51.cloned.1.call-update) | async-done | bytes 1990672 | tf_op jit(solution)/shard_map/all_gather | solution.py:224
  741.9 38.2 %all-gather.31.cloned.1.call-done = bf16[2,1024,1152]{2,1,0:T(8,128)(2,1)} async-done(((bf16[2,256,1152]{2,1,0:T(8,128)(2,1)}), bf16[2,1024,1152]{2,1,0:T(8,128)(2,1)}) %all-gather.31.cloned.1.call-update) | async-done | bytes 4718608 | tf_op jit(solution)/shard_map/all_gather | solution.py:201
  791.6 187.8 %while.69 = (s32[]{:T(128)}, bf16[2,1024,4,72]{1,3,2,0:T(8,128)(2,1)}, f32[2,4,1024]{2,1,0:T(4,128)S(1)}, bf16[2,1024,4,72]{1,3,2,0:T(8,128)(2,1)}, s32[2,1024]{...) while((s32[]{:T(128)}, ...), condition=%wide.region_19.20_spmd, body=%wide.region_14.19_spmd.sunk | while | flops 1251378176 | bytes 141272848 | solution.py:263
  791.8 22.0 broadcast_add_fusion.13
  813.8 26.1 add.1076
  849.0 26.1 add.1078
  885.5 22.0 broadcast_add_fusion.13
  907.5 26.1 add.1076
  942.7 26.1 add.1078
  986.7 47.2 %reduce-scatter.21.cloned.1.call-done = bf16[2,256,1152]{2,1,0:T(8,128)(2,1)} async-done(((bf16[2,1024,1152]{2,1,0:T(8,128)(2,1)}), bf16[2,256,1152]{2,1,0:T(8,128)(2,1)}) %reduce-scatter.21.cloned.1.call-update) | async-done | bytes 1179664 | tf_op jit(solution)/shard_map/reduce_scatter | solution.py:204
  1043.2 48.8 %all-gather.55.cloned.1.call-done = bf16[1,1152,1152]{2,1,0:T(8,128)(2,1)} async-done(((bf16[1,144,1152]{2,1,0:T(8,128)(2,1)}), bf16[1,1152,1152]{2,1,0:T(8,128)(2,1)}) %all-gather.55.cloned.1.call-update) | async-done | bytes 2654224 | tf_op jit(solution)/shard_map/all_gather | solution.py:233
  1092.0 38.1 %all-gather.33.cloned.1.call-done = bf16[2,1024,1152]{2,1,0:T(8,128)(2,1)} async-done(((bf16[2,256,1152]{2,1,0:T(8,128)(2,1)}), bf16[2,1024,1152]{2,1,0:T(8,128)(2,1)}) %all-gather.33.cloned.1.call-update) | async-done | bytes 4718608 | tf_op jit(solution)/shard_map/all_gather | solution.py:201
  1141.7 46.3 %all-gather.57.cloned.1.call-done = bf16[1,1152,1152]{1,2,0:T(8,128)(2,1)} async-done(((bf16[1,1152,144]{1,2,0:T(8,128)(2,1)}), bf16[1,1152,1152]{1,2,0:T(8,128)(2,1)}) %all-gather.57.cloned.1.call-update) | async-done | bytes 2654224 | tf_op jit(solution)/shard_map/all_gather | solution.py:236
  1188.0 38.1 %all-gather.35.cloned.1.call-done = bf16[2,1024,1152]{2,1,0:T(8,128)(2,1)} async-done(((bf16[2,256,1152]{2,1,0:T(8,128)(2,1)}), bf16[2,1024,1152]{2,1,0:T(8,128)(2,1)}) %all-gather.35.cloned.1.call-update) | async-done | bytes 4718608 | tf_op jit(solution)/shard_map/all_gather | solution.py:201
  1251.2 47.9 %reduce-scatter.25.cloned.1.call-done = bf16[2,256,1152]{2,1,0:T(8,128)(2,1)} async-done(((bf16[2,1024,1152]{2,1,0:T(8,128)(2,1)}), bf16[2,256,1152]{2,1,0:T(8,128)(2,1)}) %reduce-scatter.25.cloned.1.call-update) | async-done | bytes 1179664 | tf_op jit(solution)/shard_map/reduce_scatter | solution.py:204
  1306.6 37.6 %all-gather.37.cloned.1.call-done = bf16[2,1024,1152]{2,1,0:T(8,128)(2,1)} async-done(((bf16[2,256,1152]{2,1,0:T(8,128)(2,1)}), bf16[2,1024,1152]{2,1,0:T(8,128)(2,1)}) %all-gather.37.cloned.1.call-update) | async-done | bytes 4718608 | tf_op jit(solution)/shard_map/all_gather | solution.py:201
  1352.8 352.9 %while.70 = (s32[]{:T(128)}, bf16[2,1024,4,72]{1,3,2,0:T(8,128)(2,1)}, bf16[2,1024,4,72]{1,3,2,0:T(8,128)(2,1)}, bf16[2,1024,4,72]{1,3,2,0:T(8,128)(2,1)}, f32[2...) while((s32[]{:T(128)}, ...), condition=%wide.region_34.35_spmd, body=%wide.region_27.34_spmd.sunk | while | flops 3077067776 | bytes 385031264 | solution.py:368
  1353.1 22.2 broadcast_add_fusion.14
  1375.2 26.1 add.1088
  1411.1 26.1 add.1090
  1460.4 21.0 reshape.783
  1494.7 21.0 reshape.782
  1529.2 22.2 broadcast_add_fusion.14
  1551.4 26.1 add.1088
  1587.3 26.1 add.1090
  1636.6 21.0 reshape.783
  1670.9 21.0 reshape.782
  1730.9 34.0 %reduce-scatter.27.cloned.1.call-done = bf16[2,256,1152]{2,1,0:T(8,128)(2,1)} async-done(((bf16[2,1024,1152]{2,1,0:T(8,128)(2,1)}), bf16[2,256,1152]{2,1,0:T(8,128)(2,1)}) %reduce-scatter.27.cloned.1.call-update) | async-done | bytes 1179664 | tf_op jit(solution)/shard_map/reduce_scatter | solution.py:204
  1768.0 47.3 %reduce-scatter.23.cloned.1.call-done = bf16[2,256,1152]{2,1,0:T(8,128)(2,1)} async-done(((bf16[2,1024,1152]{2,1,0:T(8,128)(2,1)}), bf16[2,256,1152]{2,1,0:T(8,128)(2,1)}) %reduce-scatter.23.cloned.1.call-update) | async-done | bytes 1179664 | tf_op jit(solution)/shard_map/reduce_scatter | solution.py:204
  1820.9 37.6 %all-gather.39.cloned.1.call-done = bf16[2,1024,1152]{2,1,0:T(8,128)(2,1)} async-done(((bf16[2,256,1152]{2,1,0:T(8,128)(2,1)}), bf16[2,1024,1152]{2,1,0:T(8,128)(2,1)}) %all-gather.39.cloned.1.call-update) | async-done | bytes 4718608 | tf_op jit(solution)/shard_map/all_gather | solution.py:201
  1883.5 47.9 %reduce-scatter.29.cloned.1.call-done = bf16[2,256,1152]{2,1,0:T(8,128)(2,1)} async-done(((bf16[2,1024,1152]{2,1,0:T(8,128)(2,1)}), bf16[2,256,1152]{2,1,0:T(8,128)(2,1)}) %reduce-scatter.29.cloned.1.call-update) | async-done | bytes 1179664 | tf_op jit(solution)/shard_map/reduce_scatter | solution.py:204
  2017.3 360.6 %while.71 = (s32[]{:T(128)}, bf16[2,1024,4,72]{1,3,2,0:T(8,128)(2,1)}, bf16[2,1024,4,72]{1,3,2,0:T(8,128)(2,1)}, bf16[2,1024,4,72]{1,3,2,0:T(8,128)(2,1)}, f32[2...) while((s32[]{:T(128)}, ...), condition=%wide.region_48.49_spmd, body=%wide.region_41.48_spmd.sunk | while | flops 3077067776 | bytes 380312640 | solution.py:368
  2017.8 22.3 broadcast_add_fusion.15
  2040.0 26.2 add.1100
  2077.1 26.2 add.1102
  2128.6 21.0 reshape.785
  2162.9 21.0 reshape.784
  2197.4 22.4 broadcast_add_fusion.15
  2219.8 26.2 add.1100
  2257.1 26.2 add.1102
  2343.2 21.0 reshape.784
  2420.6 39.7 %psum.28 = f32[]{:T(128)} all-reduce(f32[]{:T(128)S(6)} %mul.879), channel_id=1, replica_groups=mesh['group'=8,'mp'=4] {'group','mp'}, use_global_device_ids=true, to_apply=%region_52.53 | all-reduce | flops 1 | bytes 8 | tf_op jit(solution)/shard_map/psum | solution.py:412
  2475.4 68.4 %reduce-scatter.37.cloned.1.call-done = f32[288,144]{0,1:T(8,128)} async-done(((f32[288,1152]{0,1:T(8,128)}), f32[288,144]{0,1:T(8,128)}) %reduce-scatter.37.cloned.1.call-update) | async-done | bytes 165904 | tf_op jit(solution)/shard_map/reduce_scatter | solution.py:395
  2546.5 235.2 %all-reduce.8.cloned.1.call-done = (f32[1152,2,288]{2,1,0:T(2,128)}, f32[1152,2,288]{2,1,0:T(2,128)}) async-done(((f32[1152,2,288]{2,1,0:T(2,128)}, f32[1152,2,288]{2,1,0:T(2,128)}), (f32[1152,2,288]{2,1,0:T(2,128)}, f32[1152,2,288]{2,1,0:T(2,128)})) %all-reduce.8.cloned.1.call-update) | async-done | bytes 5308432
  2791.4 97.0 %reduce-scatter.35.cloned.1.call-done = f32[144,3,288]{2,0,1:T(8,128)} async-done(((f32[1152,3,288]{2,0,1:T(8,128)}), f32[144,3,288]{2,0,1:T(8,128)}) %reduce-scatter.35.cloned.1.call-update) | async-done | bytes 497680 | tf_op jit(solution)/shard_map/reduce_scatter | solution.py:393
  2888.4 107.9 %reduce-scatter.33.cloned.1.call-done = f32[144,3,288]{2,0,1:T(8,128)} async-done(((f32[1152,3,288]{2,0,1:T(8,128)}), f32[144,3,288]{2,0,1:T(8,128)}) %reduce-scatter.33.cloned.1.call-update) | async-done | bytes 497680 | tf_op jit(solution)/shard_map/reduce_scatter | solution.py:393
  3001.7 44.5 %reduce-scatter.31.cloned.1.call-done = bf16[2,256,1152]{2,1,0:T(8,128)(2,1)} async-done(((bf16[2,1024,1152]{2,1,0:T(8,128)(2,1)}), bf16[2,256,1152]{2,1,0:T(8,128)(2,1)}) %reduce-scatter.31.cloned.1.call-update) | async-done | bytes 1179664 | tf_op jit(solution)/shard_map/reduce_scatter | solution.py:204
  3048.9 41.0 %all-reduce.4 = (f32[2,4,1152]{2,1,0:T(4,128)S(1)}, f32[2,16,2,63]{3,2,1,0:T(2,128)}, f32[2,2,5]{2,1,0:T(2,128)S(1)}) all-reduce(f32[2,4,1152]{2,1,0:T(4,128)S(1)} %pad_maximum_fusion.6, f32[2,16,2,63]{3,2,1,0:T(2,128)S(1)} %copy_dynamic-update-slice_fusion, f32[2,2,5]{2,1,0:T(2,128)S(1)} %stack.269), channel_id=1, replica_groups=mesh['group'=8,'mp'=4] {'group','mp'}, use_global_device_ids=true, to_apply=%region_62.63 | all-reduce | flops 13268 | bytes 106144 | tf_op jit(solution)/shard_map/psum | solution.py:412
  (813 shorter events, 762.7 us)
Async XLA Ops:
  7.2 59.8 %all-gather.45.cloned.1.call-start = ((), (), s32[]{:S(2)}) async-start(), calls=%async_computation.41 | async-start | bytes 1990656 | tf_op jit(solution)/shard_map/all_gather | solution.py:227
  9.6 114.9 %all-gather.43.cloned.1.call-start = ((), (), s32[]{:S(2)}) async-start(), calls=%async_computation.40 | async-start | bytes 2985984 | tf_op jit(solution)/shard_map/all_gather | solution.py:224
  12.0 150.7 %all-gather.27.cloned.1.call-start = ((), (), s32[]{:S(2)}) async-start(), calls=%async_computation.16 | async-start | bytes 5898240 | tf_op jit(solution)/shard_map/all_gather | solution.py:201
  15.6 401.9 %reduce-scatter.17.cloned.1.call-start = ((), (), s32[]{:S(2)}) async-start(), calls=%async_computation.17 | async-start | bytes 5898240 | tf_op jit(solution)/shard_map/reduce_scatter | solution.py:204
  17.0 51.8 %copy-start.121 = (bf16[1152,1,1]{0,1,2:T(2,128)(2,1)}, bf16[1152,1,1]{0,1,2:T(2,128)(2,1)S(1)}, u32[]{:S(2)}) copy-start(bf16[1152,1,1]{0,1,2:T(2,128)(2,1)S(1)} %reshape.722) | copy-start | bytes 6916
  369.5 48.0 %copy-start.14 = (bf16[2,256,1152]{2,1,0:T(8,128)(2,1)S(1)}, bf16[2,256,1152]{2,1,0:T(8,128)(2,1)}, u32[]{:S(2)}) copy-start(bf16[2,256,1152]{2,1,0:T(8,128)(2,1)} %param.43) | copy-start | bytes 3538948
  369.5 105.9 %all-gather.47.cloned.1.call-start = ((), (), s32[]{:S(2)}) async-start(), calls=%async_computation.42 | async-start | bytes 2985984 | tf_op jit(solution)/shard_map/all_gather | solution.py:233
  371.8 48.1 %copy-start.100 = (f32[1152]{0:T(1024)S(1)}, f32[1152]{0:T(1024)}, u32[]{:S(2)}) copy-start(f32[1152]{0:T(1024)} %get-tuple-element.853) | copy-start | bytes 13828
  371.8 48.1 %copy-start.131 = (f32[1152]{0:T(1024)S(1)}, f32[1152]{0:T(1024)}, u32[]{:S(2)}) copy-start(f32[1152]{0:T(1024)} %get-tuple-element.852) | copy-start | bytes 13828
  371.8 141.7 %all-gather.29.cloned.1.call-start = ((), (), s32[]{:S(2)}) async-start(), calls=%async_computation.18 | async-start | bytes 5898240 | tf_op jit(solution)/shard_map/all_gather | solution.py:201
  421.6 150.0 %all-gather.49.cloned.1.call-start = ((), (), s32[]{:S(2)}) async-start(), calls=%async_computation.43 | async-start | bytes 2985984 | tf_op jit(solution)/shard_map/all_gather | solution.py:236
  423.9 207.2 %reduce-scatter.19.cloned.1.call-start = ((), (), s32[]{:S(2)}) async-start(), calls=%async_computation.19 | async-start | bytes 5898240 | tf_op jit(solution)/shard_map/reduce_scatter | solution.py:204
  584.5 100.6 %all-gather.53.cloned.1.call-start = ((), (), s32[]{:S(2)}) async-start(), calls=%async_computation.45 | async-start | bytes 1990656 | tf_op jit(solution)/shard_map/all_gather | solution.py:227
  585.3 156.6 %all-gather.51.cloned.1.call-start = ((), (), s32[]{:S(2)}) async-start(), calls=%async_computation.44 | async-start | bytes 2985984 | tf_op jit(solution)/shard_map/all_gather | solution.py:224
  585.9 194.2 %all-gather.31.cloned.1.call-start = ((), (), s32[]{:S(2)}) async-start(), calls=%async_computation.20 | async-start | bytes 5898240 | tf_op jit(solution)/shard_map/all_gather | solution.py:201
  635.9 49.3 %copy-start.122 = (bf16[1152,1,1]{0,1,2:T(2,128)(2,1)S(1)}, bf16[1152,1,1]{0,1,2:T(2,128)(2,1)}, u32[]{:S(2)}) copy-start(bf16[1152,1,1]{0,1,2:T(2,128)(2,1)} %copy-done.121) | copy-start | bytes 6916
  635.9 398.0 %reduce-scatter.21.cloned.1.call-start = ((), (), s32[]{:S(2)}) async-start(), calls=%async_computation.21 | async-start | bytes 5898240 | tf_op jit(solution)/shard_map/reduce_scatter | solution.py:204
  985.9 106.0 %all-gather.55.cloned.1.call-start = ((), (), s32[]{:S(2)}) async-start(), calls=%async_computation.46 | async-start | bytes 2985984 | tf_op jit(solution)/shard_map/all_gather | solution.py:233
  986.7 143.4 %all-gather.33.cloned.1.call-start = ((), (), s32[]{:S(2)}) async-start(), calls=%async_computation.22 | async-start | bytes 5898240 | tf_op jit(solution)/shard_map/all_gather | solution.py:201
  1036.3 266.8 %copy-start.107 = (f32[2,256]{1,0:T(2,128)}, f32[2,256]{1,0:T(2,128)S(1)}, u32[]{:S(2)}) copy-start(f32[2,256]{1,0:T(2,128)S(1)} %broadcast_multiply_fusion.10) | copy-start | bytes 6148
  1036.6 266.4 %copy-start.114 = (f32[2,256]{1,0:T(2,128)}, f32[2,256]{1,0:T(2,128)S(1)}, u32[]{:S(2)}) copy-start(f32[2,256]{1,0:T(2,128)S(1)} %add_rsqrt_fusion) | copy-start | bytes 6148
  1039.1 148.8 %all-gather.57.cloned.1.call-start = ((), (), s32[]{:S(2)}) async-start(), calls=%async_computation.47 | async-start | bytes 2985984 | tf_op jit(solution)/shard_map/all_gather | solution.py:236
  1039.7 186.4 %all-gather.35.cloned.1.call-start = ((), (), s32[]{:S(2)}) async-start(), calls=%async_computation.24 | async-start | bytes 5898240 | tf_op jit(solution)/shard_map/all_gather | solution.py:201
  1040.4 262.6 %copy-start.157 = (f32[2]{0:T(128)}, f32[2]{0:T(128)S(1)}, u32[]{:S(2)}) copy-start(f32[2]{0:T(128)S(1)} %compare_convert_fusion) | copy-start | bytes 28
  1043.1 256.0 %reduce-scatter.25.cloned.1.call-start = ((), (), s32[]{:S(2)}) async-start(), calls=%async_computation.25 | async-start | bytes 5898240 | tf_op jit(solution)/shard_map/reduce_scatter | solution.py:204
  1251.2 93.0 %all-gather.37.cloned.1.call-start = ((), (), s32[]{:S(2)}) async-start(), calls=%async_computation.26 | async-start | bytes 5898240 | tf_op jit(solution)/shard_map/all_gather | solution.py:201
  1306.6 458.3 %reduce-scatter.27.cloned.1.call-start = ((), (), s32[]{:S(2)}) async-start(), calls=%async_computation.27 | async-start | bytes 5898240 | tf_op jit(solution)/shard_map/reduce_scatter | solution.py:204
  1353.0 48.3 %copy-start.17 = (bf16[2,1024,4,72]{1,3,2,0:T(8,128)(2,1)}, bf16[2,1024,4,72]{1,3,2,0:T(8,128)(2,1)S(1)}, u32[]{:S(2)}) copy-start(bf16[2,1024,4,72]{1,3,2,0:T(8,128)(2,1)S(1)} %get-tuple-element.1568) | copy-start | bytes 3538948 | tf_op jit(solution)/shard_map/while
  1353.0 84.2 %copy-start.11 = (bf16[2,1024,4,72]{1,3,2,0:T(8,128)(2,1)}, bf16[2,1024,4,72]{1,3,2,0:T(8,128)(2,1)S(1)}, u32[]{:S(2)}) copy-start(bf16[2,1024,4,72]{1,3,2,0:T(8,128)(2,1)S(1)} %get-tuple-element.1566) | copy-start | bytes 3538948 | tf_op jit(solution)/shard_map/while
  1529.1 48.3 %copy-start.17 = (bf16[2,1024,4,72]{1,3,2,0:T(8,128)(2,1)}, bf16[2,1024,4,72]{1,3,2,0:T(8,128)(2,1)S(1)}, u32[]{:S(2)}) copy-start(bf16[2,1024,4,72]{1,3,2,0:T(8,128)(2,1)S(1)} %get-tuple-element.1568) | copy-start | bytes 3538948 | tf_op jit(solution)/shard_map/while
  1529.1 84.2 %copy-start.11 = (bf16[2,1024,4,72]{1,3,2,0:T(8,128)(2,1)}, bf16[2,1024,4,72]{1,3,2,0:T(8,128)(2,1)S(1)}, u32[]{:S(2)}) copy-start(bf16[2,1024,4,72]{1,3,2,0:T(8,128)(2,1)S(1)} %get-tuple-element.1566) | copy-start | bytes 3538948 | tf_op jit(solution)/shard_map/while
  1716.9 98.4 %reduce-scatter.23.cloned.1.call-start = ((), (), s32[]{:S(2)}) async-start(), calls=%async_computation.23 | async-start | bytes 5898240 | tf_op jit(solution)/shard_map/reduce_scatter | solution.py:204
  1730.8 84.5 %copy-start.99 = (f32[1152]{0:T(1024)S(1)}, f32[1152]{0:T(1024)}, u32[]{:S(2)}) copy-start(f32[1152]{0:T(1024)} %get-tuple-element.848) | copy-start | bytes 13828
  1730.8 84.5 %copy-start.108 = (f32[2,256]{1,0:T(2,128)S(1)}, f32[2,256]{1,0:T(2,128)}, u32[]{:S(2)}) copy-start(f32[2,256]{1,0:T(2,128)} %copy-done.107) | copy-start | bytes 6148
  1730.8 84.5 %copy-start.115 = (f32[2,256]{1,0:T(2,128)S(1)}, f32[2,256]{1,0:T(2,128)}, u32[]{:S(2)}) copy-start(f32[2,256]{1,0:T(2,128)} %copy-done.114) | copy-start | bytes 6148
  1730.8 84.5 %copy-start.145 = (f32[2,256]{1,0:T(2,128)S(1)}, f32[2,256]{1,0:T(2,128)}, u32[]{:S(2)}) copy-start(f32[2,256]{1,0:T(2,128)} %copy-done.144) | copy-start | bytes 6148
  1730.9 84.5 %copy-start.147 = (f32[2,256]{1,0:T(2,128)S(1)}, f32[2,256]{1,0:T(2,128)}, u32[]{:S(2)}) copy-start(f32[2,256]{1,0:T(2,128)} %copy-done.146) | copy-start | bytes 6148
  1730.9 84.5 %copy-start.158 = (f32[2]{0:T(128)S(1)}, f32[2]{0:T(128)}, u32[]{:S(2)}) copy-start(f32[2]{0:T(128)} %copy-done.157) | copy-start | bytes 28
  1730.9 127.5 %all-gather.39.cloned.1.call-start = ((), (), s32[]{:S(2)}) async-start(), calls=%async_computation.28 | async-start | bytes 5898240 | tf_op jit(solution)/shard_map/all_gather | solution.py:201
  1820.8 53.9 %copy-start.159 = (bf16[1,1152,1152]{2,1,0:T(8,128)(2,1)S(1)}, bf16[1,1152,1152]{2,1,0:T(8,128)(2,1)}, u32[]{:S(2)}) copy-start(bf16[1,1152,1152]{2,1,0:T(8,128)(2,1)} %all-gather.47.cloned.1.call-done) | copy-start | bytes 7962628
  1820.8 110.6 %reduce-scatter.29.cloned.1.call-start = ((), (), s32[]{:S(2)}) async-start(), calls=%async_computation.29 | async-start | bytes 5898240 | tf_op jit(solution)/shard_map/reduce_scatter | solution.py:204
  1883.4 48.0 %copy-start.15 = (bf16[2,256,1152]{2,1,0:T(8,128)(2,1)S(1)}, bf16[2,256,1152]{2,1,0:T(8,128)(2,1)}, u32[]{:S(2)}) copy-start(bf16[2,256,1152]{2,1,0:T(8,128)(2,1)} %param.43) | copy-start | bytes 3538948
  1883.4 48.0 %copy-start.25 = (bf16[2,256,1152]{2,1,0:T(8,128)(2,1)S(1)}, bf16[2,256,1152]{2,1,0:T(8,128)(2,1)}, u32[]{:S(2)}) copy-start(bf16[2,256,1152]{2,1,0:T(8,128)(2,1)} %reduce-scatter.17.cloned.1.call-done) | copy-start | bytes 3538948
  1883.4 48.0 %copy-start.101 = (f32[1152]{0:T(1024)S(1)}, f32[1152]{0:T(1024)}, u32[]{:S(2)}) copy-start(f32[1152]{0:T(1024)} %get-tuple-element.853) | copy-start | bytes 13828
  1883.4 48.0 %copy-start.110 = (f32[2,256]{1,0:T(2,128)S(1)}, f32[2,256]{1,0:T(2,128)}, u32[]{:S(2)}) copy-start(f32[2,256]{1,0:T(2,128)} %copy-done.109) | copy-start | bytes 6148
  1883.4 48.0 %copy-start.117 = (f32[2,256]{1,0:T(2,128)S(1)}, f32[2,256]{1,0:T(2,128)}, u32[]{:S(2)}) copy-start(f32[2,256]{1,0:T(2,128)} %copy-done.116) | copy-start | bytes 6148
  1883.5 118.6 %all-gather.41.cloned.1.call-start = ((), (), s32[]{:S(2)}) async-start(), calls=%async_computation.30 | async-start | bytes 5898240 | tf_op jit(solution)/shard_map/all_gather | solution.py:201
  1937.1 526.8 %reduce-scatter.43.cloned.1.call-start = ((), (), s32[]{:S(2)}) async-start(), calls=%async_computation.37 | async-start | bytes 5971968 | tf_op jit(solution)/shard_map/reduce_scatter | solution.py:396
  1949.9 514.0 %reduce-scatter.41.cloned.1.call-start = ((), (), s32[]{:S(2)}) async-start(), calls=%async_computation.36 | async-start | bytes 5971968 | tf_op jit(solution)/shard_map/reduce_scatter | solution.py:396
  1962.8 506.5 %reduce-scatter.47.cloned.1.call-start = ((), (), s32[]{:S(2)}) async-start(), calls=%async_computation.39 | async-start | bytes 5971968 | tf_op jit(solution)/shard_map/reduce_scatter | solution.py:397
  1977.2 492.1 %reduce-scatter.45.cloned.1.call-start = ((), (), s32[]{:S(2)}) async-start(), calls=%async_computation.38 | async-start | bytes 5971968 | tf_op jit(solution)/shard_map/reduce_scatter | solution.py:397
  1991.3 484.1 %reduce-scatter.39.cloned.1.call-start = ((), (), s32[]{:S(2)}) async-start(), calls=%async_computation.35 | async-start | bytes 1990656 | tf_op jit(solution)/shard_map/reduce_scatter | solution.py:395
  1998.8 545.0 %reduce-scatter.37.cloned.1.call-start = ((), (), s32[]{:S(2)}) async-start(), calls=%async_computation.34 | async-start | bytes 1990656 | tf_op jit(solution)/shard_map/reduce_scatter | solution.py:395
  2008.4 773.2 %all-reduce.8.cloned.1.call-start = ((), (), s32[]{:S(2)}) async-start(), calls=%async_computation.48 | async-start | bytes 14155776
  2386.7 501.7 %reduce-scatter.35.cloned.1.call-start = ((), (), s32[]{:S(2)}) async-start(), calls=%async_computation.33 | async-start | bytes 5971968 | tf_op jit(solution)/shard_map/reduce_scatter | solution.py:393
  2398.2 598.1 %reduce-scatter.33.cloned.1.call-start = ((), (), s32[]{:S(2)}) async-start(), calls=%async_computation.32 | async-start | bytes 5971968 | tf_op jit(solution)/shard_map/reduce_scatter | solution.py:393
  2409.7 636.6 %reduce-scatter.31.cloned.1.call-start = ((), (), s32[]{:S(2)}) async-start(), calls=%async_computation.31 | async-start | bytes 5898240 | tf_op jit(solution)/shard_map/reduce_scatter | solution.py:204
  2420.6 43.3 %copy-start.136 = (f32[1152]{0:T(1024)S(1)}, f32[1152]{0:T(1024)}, u32[]{:S(2)}) copy-start(f32[1152]{0:T(1024)} %get-tuple-element.843) | copy-start | bytes 13828
  2469.3 74.5 %copy-start.69 = (f32[2,288,144]{1,2,0:T(8,128)S(1)}, f32[2,288,144]{1,2,0:T(8,128)}, u32[]{:S(2)}) copy-start(f32[2,288,144]{1,2,0:T(8,128)} %param.61) | copy-start | bytes 995332
  2469.3 74.5 %copy-start.91 = (f32[2,288,144]{1,2,0:T(8,128)S(1)}, f32[2,288,144]{1,2,0:T(8,128)}, u32[]{:S(2)}) copy-start(f32[2,288,144]{1,2,0:T(8,128)} %param.62) | copy-start | bytes 995332
  2996.2 50.0 %copy-start.16 = (bf16[2,256,1152]{2,1,0:T(8,128)(2,1)S(1)}, bf16[2,256,1152]{2,1,0:T(8,128)(2,1)}, u32[]{:S(2)}) copy-start(bf16[2,256,1152]{2,1,0:T(8,128)(2,1)} %param.43) | copy-start | bytes 3538948
  2996.2 50.0 %copy-start.106 = (f32[1152]{0:T(1024)S(1)}, f32[1152]{0:T(1024)}, u32[]{:S(2)}) copy-start(f32[1152]{0:T(1024)} %copy-done.105) | copy-start | bytes 13828
  2996.2 50.0 %copy-start.120 = (f32[2,256]{1,0:T(2,128)S(1)}, f32[2,256]{1,0:T(2,128)}, u32[]{:S(2)}) copy-start(f32[2,256]{1,0:T(2,128)} %copy-done.119) | copy-start | bytes 6148
  2996.2 50.0 %copy-start.143 = (f32[2,256]{1,0:T(2,128)S(1)}, f32[2,256]{1,0:T(2,128)}, u32[]{:S(2)}) copy-start(f32[2,256]{1,0:T(2,128)} %copy-done.142) | copy-start | bytes 6148
  (173 other events, 1189.9 us)
Sparse Core Ops, SparseCore 0:
  10.8 56.1 all-gather.44
  69.8 54.6 all-gather.42
  126.6 36.0 all-gather.26
  369.6 47.8 reduce-scatter.16
  420.3 55.0 all-gather.46
  477.5 36.0 all-gather.28
  516.5 55.0 all-gather.48
  584.7 46.3 reduce-scatter.18
  633.9 51.2 all-gather.52
  687.8 54.0 all-gather.50
  744.0 36.0 all-gather.30
  986.1 47.8 reduce-scatter.20
  1036.9 55.0 all-gather.54
  1094.0 36.0 all-gather.32
  1132.9 55.0 all-gather.56
  1190.0 36.0 all-gather.34
  1251.3 47.8 reduce-scatter.24
  1306.7 37.4 all-gather.36
  1717.0 47.8 reduce-scatter.26
  1767.4 47.8 reduce-scatter.22
  1820.9 37.4 all-gather.38
  1883.6 47.8 reduce-scatter.28
  1937.2 37.4 all-gather.40
  1978.6 104.1 reduce-scatter.42
  2086.4 103.9 reduce-scatter.40
  2194.3 103.9 reduce-scatter.46
  2301.7 103.9 reduce-scatter.44
  2409.6 65.7 reduce-scatter.38
  2478.9 64.9 reduce-scatter.36
  2548.2 233.3 all-reduce.7
  2785.2 103.0 reduce-scatter.34
  2892.4 103.8 reduce-scatter.32
  2998.6 47.5 reduce-scatter.30
where the time goes:
time: 3140 us; the launch traced here: 3120 us
  waiting for transfers between devices  1460 us (46%)
  local copies, waits for them, and re-layouts  655 us (21%)
  matrix products  421 us (13%)
  other arithmetic  404 us (13%)
  blocking collectives  154 us (5%)
    add x16, local copies, waits for them, and re-layouts, block_scores(): row_part[:, :, None, :, None] + col_bias[:, None, :, None, :]  418 us
    reduce_scatter x8, waiting for transfers between devices, row_sums(): lax.psum_scatter(partial_value.astype(jnp.bfloat16), 'mp', scatter_dimens...  359 us
    all_gather x8, waiting for transfers between devices, whole_rows(): return lax.all_gather(part_rows, 'mp', axis=1, tiled=True)  266 us
    unnamed x34, waiting for transfers between devices  238 us
    reduce_scatter x2, waiting for transfers between devices, shards(): lax.psum_scatter(grad_qkv, 'group', scatter_dimension=0, tiled=True)  205 us
    add x8, other arithmetic, block_scores(): row_part[:, :, None, :, None] + col_bias[:, None, :, None, :]  177 us
    reshape x8, local copies, waits for them, and re-layouts, attend_back(): grad_scores.astype(jnp.float32)  168 us
    all_gather x2, waiting for transfers between devices, shards(): lax.all_gather(qkv_weight[layer_index].astype(jnp.bfloat16), 'group', axi...  110 us
  transfers between devices with their start and end apart: 33, of which 28 were waited for; matrix products, arithmetic and copies ran while one was open for 18% of the time, Pallas kernels for 0%

commit v1 on v0

v1 whole, which is shorter than its diff:
```python
import functools

import jax
import jax.numpy as jnp
from jax import lax
from jax.experimental import pallas as pl
from jax.experimental.pallas import tpu as pltpu
from jax.sharding import PartitionSpec as P

STEP = 5
highest = lax.Precision.HIGHEST
norm_epsilon = 1e-05
adam_epsilon = 1e-06
beta_first = 0.5
beta_second = 0.5
decay_rate = 0.01
learn_rate = 0.5

HEAD = 72
SPARE = 256 - 3 * HEAD
LANE = 128
CHUNKS = 4
MIB = 1 << 20
MASKED = -1e30
SMALL = 6e7
BIG = 6e6
LOG2E = 1.4426950408889634
GELU_A = 0.7978845608
GELU_B = 0.044715
SCALE = HEAD**-0.5
ROOT = HEAD**0.5
EXP_SCALE = LOG2E * SCALE
SEQUENCE = (
    "i0", "i1", "unpack0", "i0", "i0", "i1", "i0", "p1",
    "i0", "i0", "i1", "p0", "i1", "i1", "i0", "unpack1",
    "p1", "i0", "i0", "i1", "p0", "i1", "i1", "i0",
    "p1", "i0", "i0", "i0", "i1", "i0", "i1", "i1",
    "i1", "up1", "i0", "i1", "i0", "down1", "i0", "i1",
    "p0", "i1", "i1", "out1", "i0", "p1", "i0", "qkv1",
    "i0", "i1", "p0", "i1", "i1", "hold_mlp1", "up0", "i0",
    "p1", "i0", "down0", "i0", "i1", "p0", "i1", "out0",
    "hold_attend1", "i1", "qkv0", "last", "i0", "i1", "i0", "i1",
    "i1", "e0", "e1",
)
bf16 = jnp.bfloat16
f32 = jnp.float32


def dot_nn(left, right):
    return lax.dot_general(left, right, (((1,), (0,)), ((), ())), preferred_element_type=f32)


def dot_nt(left, right):
    return lax.dot_general(left, right, (((1,), (1,)), ((), ())), preferred_element_type=f32)


def split_three(value):
    top = value.astype(bf16)
    rest = value - top.astype(f32)
    middle = rest.astype(bf16)
    last = (rest - middle.astype(f32)).astype(bf16)
    return top, middle, last


def lanes_of(shape):
    return lax.broadcasted_iota(jnp.int32, shape, len(shape) - 1)


def columns_spec(rows, columns, start):
    return pl.BlockSpec((pl.Element(rows), pl.Element(columns)), lambda step: (0, start))


def whole_spec(shape):
    return pl.BlockSpec(shape, lambda step: (0,) * len(shape))


class Chain:
    def __init__(self):
        self.token = None
        self.holds = []
        self.pending = None
        self.postpone = False

    def take_pair(self):
        return () if self.pending is None else self.pending.pop()

    def give_pair(self, result):
        if result:
            self.pending.append(result[0])
            self.pending = None

    def hold(self, *arrays):
        self.holds.extend(arrays)

    def call(self, body, grid, inputs, in_specs, out_specs, out_shape, scratch, flops, moved, exps, limit, name, aliases=None):
        count_in, count_out = len(in_specs), len(out_specs)
        waits = self.holds + ([] if self.token is None else [self.token])
        self.holds = []
        first = len(waits)

        def wrapped(*refs):
            ins = refs[first : first + count_in]
            outs = refs[first + count_in : first + count_in + count_out]
            token_ref = refs[first + count_in + count_out]
            rest = refs[first + count_in + count_out + 1 :]

            @pl.when(pl.program_id(0) == 0)
            def _():
                token_ref[...] = jnp.zeros(token_ref.shape, f32)

            body(*ins, *outs, *rest)

        token_spec = pl.BlockSpec((8, LANE), lambda *steps: (0, 0))
        results = pl.pallas_call(
            wrapped,
            grid=grid,
            in_specs=[pl.BlockSpec(memory_space=pl.ANY)] * first + in_specs,
            out_specs=out_specs + [token_spec],
            out_shape=out_shape + [jax.ShapeDtypeStruct((8, LANE), f32)],
            scratch_shapes=scratch,
            input_output_aliases={first + given: out for given, out in (aliases or {}).items()},
            compiler_params=pltpu.CompilerParams(vmem_limit_bytes=limit * MIB),
            cost_estimate=pl.CostEstimate(
                flops=int(flops), bytes_accessed=int(moved), transcendentals=int(exps)
            ),
            name=name,
        )(*waits, *inputs)
        self.token = results[-1]
        return results[:-1]


def put_half(half, value, keep_ref, send_ref):
    rows = keep_ref.shape[1]
    keep_ref[half] = value[:rows].astype(bf16)
    send_ref[half] = value[rows:].astype(bf16)


def row_half(own_ref, near_ref, half):
    return jnp.concatenate([own_ref[half], near_ref[half]], axis=0)


def unpack_body(packed_ref, out_ref):
    rows = packed_ref.shape[0]
    heads = out_ref.shape[1] // LANE
    lane = lanes_of((rows, LANE))
    rest = packed_ref[:, heads * 256 :].astype(f32)
    for head in range(heads):
        block = packed_ref[:, head * 256 : (head + 1) * 256].astype(f32)
        first = pltpu.roll(block, SPARE, 1)[:, :LANE]
        second = pltpu.roll(rest, (SPARE - head * (HEAD - SPARE)) % LANE, 1)
        value = jnp.where(lane < SPARE, first, jnp.where(lane < HEAD, second, 0.0))
        out_ref[:, head * LANE : (head + 1) * LANE] = value.astype(bf16)


def unpack_call(chain, packed, start, heads):
    width = packed.shape[0]
    rows = 384 if width % 384 == 0 else width
    columns = heads * (256 + HEAD - SPARE)
    return chain.call(
        unpack_body,
        (width // rows,),
        (packed,),
        [pl.BlockSpec((pl.Element(rows), pl.Element(columns)), lambda step: (step * rows, start))],
        [pl.BlockSpec((rows, heads * LANE), lambda step: (step, 0))],
        [jax.ShapeDtypeStruct((width, heads * LANE), bf16)],
        [],
        SMALL,
        1e3,
        0,
        63,
        "unpack_out",
    )[0]


def attend_body(
    own_ref, near_ref, w_ref, shift_ref, aux_ref, qpos_ref, kpos_ref, wo_ref,
    qkv_ref, mix_ref, keep_ref, send_ref,
):
    head = pl.program_id(0)
    heads = pl.num_programs(0)
    rows = own_ref.shape[1]
    seq = rows * CHUNKS
    weight = w_ref[...]

    block_rows = 2 * rows
    for half in range(2):
        where = pl.ds(half * block_rows, block_rows)
        out = dot_nn(row_half(own_ref, near_ref, half), weight) + shift_ref[0]
        lane = lanes_of((block_rows, LANE))
        keys = pltpu.roll(out, 256 - HEAD, 1)[:, :LANE]
        vals = pltpu.roll(out, 256 - 2 * HEAD, 1)[:, :LANE]
        queries = jnp.where(lane < HEAD, out[:, :LANE], jnp.where(lane == HEAD + 3, 1.0, 0.0))
        keys = jnp.where(lane < HEAD, keys, aux_ref[where, :].astype(f32))
        vals = jnp.where(lane < HEAD, vals, jnp.where(lane < HEAD + 3, 1.0, 0.0))
        qkv_ref[0, 0, where, :] = queries.astype(bf16)
        qkv_ref[0, 1, where, :] = keys.astype(bf16)
        qkv_ref[0, 2, where, :] = vals.astype(bf16)

    keyset = jnp.concatenate([qkv_ref[0, 1], kpos_ref[0]], axis=1)
    values = qkv_ref[0, 2]
    mix_lanes = pl.ds(pl.multiple_of(head * LANE, LANE), LANE)

    for start in range(0, seq, rows):
        where = pl.ds(start, rows)
        main = qkv_ref[0, 0, where, :]
        queries = jnp.concatenate([main, qpos_ref[where, :]], axis=1)
        scores = dot_nt(queries, keyset)
        top = jnp.max(scores, axis=1, keepdims=True)
        probs = jnp.exp2((scores - top) * EXP_SCALE).astype(bf16)
        mixed = dot_nn(probs, values)
        total = mixed[:, HEAD : HEAD + 1]
        lane = lanes_of((rows, LANE))
        mix_ref[where, mix_lanes] = jnp.where(lane < HEAD, mixed / total, 0.0).astype(bf16)
        hi, mid, low = split_three(-(top + jnp.log2(total) * (1.0 / EXP_SCALE)))
        main = jnp.where(lane == HEAD, hi, main)
        main = jnp.where(lane == HEAD + 1, mid, main)
        main = jnp.where(lane == HEAD + 2, low, main)
        qkv_ref[0, 0, where, :] = main

    @pl.when(head == heads - 1)
    def _():
        for half in range(2):
            where = pl.ds(half * block_rows, block_rows)
            put_half(half, dot_nt(mix_ref[where, :], wo_ref[...]), keep_ref, send_ref)


def attend_call(chain, pieces, weights, shift, aux, qpos, kpos):
    w_qkv, qkv_start = weights["attend"]
    w_out = weights["out"]
    _, rows, width = pieces[0].shape
    seq = rows * CHUNKS
    heads = kpos.shape[0]
    half = jax.ShapeDtypeStruct((2, rows, width), bf16)
    return chain.call(
        attend_body,
        (heads,),
        (*pieces, w_qkv, shift, aux, qpos, kpos, w_out),
        [whole_spec((2, rows, width))] * 2
        + [
            pl.BlockSpec((width, 256), lambda step: (0, qkv_start // 256 + step)),
            pl.BlockSpec((1, 1, 256), lambda step: (step, 0, 0)),
            whole_spec((seq, LANE)),
            whole_spec((seq, LANE)),
            pl.BlockSpec((1, seq, LANE), lambda step: (step, 0, 0)),
            whole_spec((width, heads * LANE)),
        ],
        [
            pl.BlockSpec((1, 3, seq, LANE), lambda step: (step, 0, 0, 0)),
            whole_spec((seq, heads * LANE)),
            whole_spec((2, rows, width)),
            whole_spec((2, rows, width)),
        ],
        [
            jax.ShapeDtypeStruct((heads, 3, seq, LANE), bf16),
            jax.ShapeDtypeStruct((seq, heads * LANE), bf16),
            half,
            half,
        ],
        [],
        BIG,
        1e3,
        0,
        63,
        "attend_fwd",
    )


def attend_back_body(
    own_ref, near_ref, wo_ref, qkv_ref, qpos_ref, kpos_ref, mix_ref, w_ref,
    dqkv_ref, sums_ref, rel_ref, keep_ref, send_ref,
    dmix, grad_vals, grad_keys, grad_queries,
):
    head = pl.program_id(0)
    heads = pl.num_programs(0)
    rows = own_ref.shape[1]
    seq = rows * CHUNKS
    grid_side = 32

    @pl.when(head == 0)
    def _():
        for half in range(2):
            where = pl.ds(half * 2 * rows, 2 * rows)
            dmix[where, :] = dot_nn(row_half(own_ref, near_ref, half), wo_ref[...]).astype(bf16)

    head_lanes = pl.ds(pl.multiple_of(head * LANE, LANE), LANE)
    keyset = jnp.concatenate([qkv_ref[0, 1], kpos_ref[0]], axis=1)
    keys_turned = qkv_ref[0, 1].T
    values = qkv_ref[0, 2]

    grad_vals[...] = jnp.zeros_like(grad_vals)
    grad_keys[...] = jnp.zeros_like(grad_keys)
    lane = lanes_of((rows, LANE))

    def back(pair, carry):
        val_part = None
        for half in range(2):
            where = pl.ds(pl.multiple_of((2 * pair + half) * rows, rows), rows)
            queries = jnp.concatenate([qkv_ref[0, 0, where, :], qpos_ref[where, :]], axis=1)
            grad_out = dmix[where, head_lanes]
            delta = jnp.sum(
                grad_out.astype(f32) * mix_ref[where, :].astype(f32), axis=1, keepdims=True
            )
            hi, mid, low = split_three(-delta)
            shifted = jnp.where(lane == HEAD, hi, grad_out)
            shifted = jnp.where(lane == HEAD + 1, mid, shifted)
            shifted = jnp.where(lane == HEAD + 2, low, shifted)
            probs = jnp.exp2(dot_nt(keyset, queries) * EXP_SCALE).astype(bf16)
            grad_scores = probs * dot_nt(values, shifted).astype(bf16)
            val_add = dot_nn(probs, grad_out)
            key_add = dot_nn(grad_scores, queries)
            grad_queries[:, where] = dot_nn(keys_turned, grad_scores)
            if val_part is None:
                val_part, key_part = val_add, key_add
            else:
                val_part, key_part = val_part + val_add, key_part + key_add
        grad_vals[...] += val_part
        grad_keys[...] += key_part
        return carry

    lax.fori_loop(0, CHUNKS // 2, back, 0)

    extra = grad_keys[:, LANE:].reshape(grid_side, grid_side, LANE)
    rel_ref[0, 0] = jnp.sum(extra, axis=1)
    rel_ref[0, 1] = jnp.sum(extra, axis=0)
    zeros = jnp.zeros((seq, LANE), f32)
    lane = lanes_of((seq, 256))
    d_query = jnp.concatenate([grad_queries[...].T, zeros], axis=1) * SCALE
    d_keys = pltpu.roll(jnp.concatenate([grad_keys[:, :LANE], zeros], axis=1), HEAD, 1) * SCALE
    d_vals = pltpu.roll(jnp.concatenate([grad_vals[...], zeros], axis=1), 2 * HEAD, 1)
    packed = jnp.where(
        lane < HEAD,
        d_query,
        jnp.where(lane < 2 * HEAD, d_keys, jnp.where(lane < 3 * HEAD, d_vals, 0.0)),
    ).astype(bf16)
    dqkv_ref[:, pl.ds(pl.multiple_of(head * 256, 256), 256)] = packed
    sums_ref[0] = jnp.sum(packed.astype(f32), axis=0, keepdims=True)

    @pl.when(head == heads - 1)
    def _():
        for half in range(2):
            where = pl.ds(half * 2 * rows, 2 * rows)
            put_half(half, dot_nt(dqkv_ref[where, :], w_ref[...]), keep_ref, send_ref)


def attend_back_call(chain, pieces, weights, qkv, qpos, kpos, mixed):
    w_qkv, qkv_start = weights["attend"]
    w_out = weights["out"]
    _, rows, width = pieces[0].shape
    seq = rows * CHUNKS
    heads = kpos.shape[0]
    half = jax.ShapeDtypeStruct((2, rows, width), bf16)
    return chain.call(
        attend_back_body,
        (heads,),
        (*pieces, w_out, qkv, qpos, kpos, mixed, w_qkv),
        [whole_spec((2, rows, width))] * 2
        + [
            whole_spec((width, heads * LANE)),
            pl.BlockSpec((1, 3, seq, LANE), lambda step: (step, 0, 0, 0)),
            whole_spec((seq, LANE)),
            pl.BlockSpec((1, seq, LANE), lambda step: (step, 0, 0)),
            pl.BlockSpec((seq, LANE), lambda step: (0, step)),
            columns_spec(width, heads * 256, qkv_start),
        ],
        [
            whole_spec((seq, heads * 256)),
            pl.BlockSpec((1, 1, 256), lambda step: (step, 0, 0)),
            pl.BlockSpec((1, 2, 32, LANE), lambda step: (step, 0, 0, 0)),
            whole_spec((2, rows, width)),
            whole_spec((2, rows, width)),
        ],
        [
            jax.ShapeDtypeStruct((seq, heads * 256), bf16),
            jax.ShapeDtypeStruct((heads, 1, 256), f32),
            jax.ShapeDtypeStruct((heads, 2, 32, LANE), f32),
            half,
            half,
        ],
        [
            pltpu.VMEM((seq, heads * LANE), bf16),
            pltpu.VMEM((seq, LANE), f32),
            pltpu.VMEM((seq, 256), f32),
            pltpu.VMEM((LANE, seq), f32),
        ],
        BIG,
        1e3,
        0,
        63,
        "attend_bwd",
    )


def column_chunks(hidden):
    return [pl.ds(start, min(512, hidden - start)) for start in range(0, hidden, 512)]


def mlp_body(own_ref, near_ref, up_ref, down_ref, pre_ref, act_ref, keep_ref, send_ref):
    inputs = row_half(own_ref, near_ref, 0)
    total = None
    for columns in column_chunks(up_ref.shape[1]):
        pre = dot_nn(inputs, up_ref[:, columns])
        inner = jnp.tanh(pre * (GELU_A + GELU_A * GELU_B * (pre * pre)))
        act = (0.5 * pre * (1.0 + inner)).astype(bf16)
        pre_ref[:, columns] = pre.astype(bf16)
        act_ref[:, columns] = act
        part = dot_nt(act, down_ref[:, columns])
        total = part if total is None else total + part
    put_half(0, total, keep_ref, send_ref)


def mlp_call(chain, pieces, weights, hidden):
    w_up, up_start = weights["up"]
    w_down, down_start = weights["down"]
    _, rows, width = pieces[0].shape
    seq = rows * CHUNKS
    half = jax.ShapeDtypeStruct((2, rows, width), bf16)
    half_spec = pl.BlockSpec((1, rows, width), lambda step: (step, 0, 0))
    hidden_spec = pl.BlockSpec((2 * rows, hidden), lambda step: (step, 0))
    return chain.call(
        mlp_body,
        (CHUNKS // 2,),
        (*pieces, w_up, w_down),
        [half_spec] * 2
        + [
            columns_spec(width, hidden, up_start),
            columns_spec(width, hidden, down_start),
        ],
        [hidden_spec, hidden_spec, half_spec, half_spec],
        [
            jax.ShapeDtypeStruct((seq, hidden), bf16),
            jax.ShapeDtypeStruct((seq, hidden), bf16),
            half,
            half,
        ],
        [],
        BIG,
        1e3,
        0,
        63,
        "mlp_fwd",
    )


def mlp_back_body(own_ref, near_ref, pre_ref, down_ref, up_ref, dpre_ref, keep_ref, send_ref):
    gradient = row_half(own_ref, near_ref, 0)
    total = None
    for columns in column_chunks(up_ref.shape[1]):
        grad_act = dot_nn(gradient, down_ref[:, columns])
        pre = pre_ref[:, columns].astype(f32)
        square = pre * pre
        inner = jnp.tanh(pre * (GELU_A + GELU_A * GELU_B * square))
        slope = 0.5 * (1.0 + inner) + 0.5 * pre * (1.0 - inner * inner) * (
            GELU_A + 3.0 * GELU_A * GELU_B * square
        )
        grad_pre = (slope * grad_act).astype(bf16)
        dpre_ref[:, columns] = grad_pre
        part = dot_nt(grad_pre, up_ref[:, columns])
        total = part if total is None else total + part
    put_half(0, total, keep_ref, send_ref)


def mlp_back_call(chain, pieces, pre, weights):
    w_up, up_start = weights["up"]
    w_down, down_start = weights["down"]
    _, rows, width = pieces[0].shape
    hidden = pre.shape[1]
    seq = rows * CHUNKS
    half = jax.ShapeDtypeStruct((2, rows, width), bf16)
    half_spec = pl.BlockSpec((1, rows, width), lambda step: (step, 0, 0))
    hidden_spec = pl.BlockSpec((2 * rows, hidden), lambda step: (step, 0))
    return chain.call(
        mlp_back_body,
        (CHUNKS // 2,),
        (*pieces, pre, w_down, w_up),
        [half_spec] * 2
        + [
            hidden_spec,
            columns_spec(width, hidden, down_start),
            columns_spec(width, hidden, up_start),
        ],
        [hidden_spec, half_spec, half_spec],
        [
            jax.ShapeDtypeStruct((seq, hidden), bf16),
            half,
            half,
        ],
        [],
        BIG,
        1e3,
        0,
        63,
        "mlp_bwd",
    )


def add_body(keep_ref, near_ref, out_ref):
    out_ref[...] = (keep_ref[...].astype(f32) + near_ref[...].astype(f32)).astype(bf16)


def add_both_body(keep_ref, near_ref, last_keep_ref, last_near_ref, out_ref, first_ref):
    step = pl.program_id(0)
    last = (last_keep_ref[0].astype(f32) + last_near_ref[0].astype(f32)).astype(bf16)

    @pl.when(step < 2)
    def _():
        add_body(keep_ref, near_ref, out_ref)

    @pl.when(step == 0)
    def _():
        first_ref[0] = last

    @pl.when(step == 2)
    def _():
        out_ref[0] = last


def add_both_call(chain, pair, last_pair):
    _, rows, width = pair[0].shape
    block = (1, rows, width)
    first = pl.BlockSpec(block, lambda step: (jnp.minimum(step, 1), 0, 0))
    last = pl.BlockSpec(block, lambda step: (step // 2, 0, 0))
    return chain.call(
        add_both_body,
        (3,),
        (*pair, *last_pair),
        [first, first, last, last],
        [pl.BlockSpec(block, lambda step: (step, 0, 0)), whole_spec(block)],
        [
            jax.ShapeDtypeStruct((3, rows, width), bf16),
            jax.ShapeDtypeStruct(block, bf16),
        ],
        [],
        SMALL,
        1e3,
        0,
        63,
        "add_both",
    )


def add_steps(chain, keep, near):
    if chain.postpone:
        box = [(keep, near)]
        chain.pending = box
        yield
        return box[0]
    own = add_call(chain, keep, near)
    yield
    return own


def add_call(chain, keep, near):
    _, rows, width = keep.shape
    spec = pl.BlockSpec((1, rows, width), lambda step: (step, 0, 0))
    return chain.call(
        add_body,
        (2,),
        (keep, near),
        [spec, spec],
        [spec],
        [jax.ShapeDtypeStruct(keep.shape, bf16)],
        [],
        SMALL,
        1e3,
        0,
        63,
        "add_near",
    )[0]


def normalize(value):
    average = jnp.mean(value, axis=-1, keepdims=True)
    centred = value - average
    scaling = lax.rsqrt(jnp.mean(centred * centred, axis=-1, keepdims=True) + norm_epsilon)
    return centred * scaling, scaling


def joined_sum(own, far):
    return own[0].astype(f32) + far[0].astype(f32)


def norm_body(*refs, count, extra):
    base, params = refs[0], refs[count]
    value = base[0].astype(f32)
    if count > 1:
        value = value + joined_sum(refs[1], refs[2])
    state_ref, out_ref = refs[count + 1 + extra : count + 3 + extra]
    state_ref[0] = value.astype(bf16)
    normed, _ = normalize(value)
    out_ref[0] = (normed * params[0:1, :] + params[1:2, :]).astype(bf16)
    if extra:
        add_body(refs[count + 1], refs[count + 2], refs[-1])


def chunk_specs(chunks, rows, width):
    block = (1, rows, width)
    return (
        pl.BlockSpec(block, lambda step: (step, 0, 0)),
        pl.BlockSpec(block, lambda step: (chunks - 1 - step, 0, 0)),
    )


def norm_call(chain, base, parts, params):
    chunks, rows, width = base.shape
    spec, turned = chunk_specs(chunks, rows, width)
    pair = chain.take_pair()
    results = chain.call(
        functools.partial(norm_body, count=1 + len(parts), extra=len(pair)),
        (chunks,),
        (base, *parts, params, *pair),
        [spec] + [spec, turned][: len(parts)] + [whole_spec(params.shape)] + [spec] * len(pair),
        [spec, spec] + [spec] * (len(pair) // 2),
        [jax.ShapeDtypeStruct(base.shape, bf16)] * 2
        + [jax.ShapeDtypeStruct(base.shape, bf16)] * (len(pair) // 2),
        [],
        SMALL,
        1e3,
        0,
        63,
        "norm_fwd",
    )
    chain.give_pair(results[2:])
    return results[:2]


def end_body(base_ref, own, far, out_ref):
    out_ref[...] = (base_ref[0].astype(f32) + joined_sum(own, far)).astype(bf16)


def end_call(chain, base, own, far):
    _, rows, width = base.shape
    first = pl.BlockSpec((1, rows, width), lambda step: (0, 0, 0))
    third = pl.BlockSpec((1, rows, width), lambda step: (2, 0, 0))
    return chain.call(
        end_body,
        (1,),
        (base, own, far),
        [first, first, third],
        [whole_spec((rows, width))],
        [jax.ShapeDtypeStruct((rows, width), bf16)],
        [],
        SMALL,
        1e3,
        0,
        63,
        "block_end",
    )[0]


def touch_body():
    pass


def touch_call(chain, far):
    chain.hold(far)
    chain.call(touch_body, (1,), (), [], [], [], [], SMALL, 1e3, 0, 63, "far_ready")


def gate_body(*refs):
    pass


def gate_call(chain, value, other):
    chain.hold(other)
    return chain.call(
        gate_body,
        (1,),
        (value,),
        [pl.BlockSpec(memory_space=pl.ANY)],
        [pl.BlockSpec(memory_space=pl.ANY)],
        [jax.ShapeDtypeStruct(value.shape, value.dtype)],
        [],
        SMALL,
        1e3,
        0,
        63,
        "gate",
        aliases={0: 0},
    )[0]


def norm_back_body(*refs, extra):
    own, far, grad_ref, state_ref, params = refs[:5]
    out_ref, sums_ref = refs[5 + extra : 7 + extra]
    step = pl.program_id(0)
    grad = joined_sum(own, far)
    normed, scaling = normalize(state_ref[0].astype(f32))
    scaled = grad * params[0:1, :]
    inner = scaled - jnp.mean(scaled, axis=-1, keepdims=True)
    inner = inner - normed * jnp.mean(scaled * normed, axis=-1, keepdims=True)
    out_ref[0] = (grad_ref[0].astype(f32) + inner * scaling).astype(out_ref.dtype)
    if extra:
        add_body(refs[5], refs[6], refs[-1])

    @pl.when(step == 0)
    def _():
        sums_ref[...] = jnp.concatenate(
            [
                jnp.sum(grad * normed, axis=0, keepdims=True),
                jnp.sum(grad, axis=0, keepdims=True),
            ],
            axis=0,
        )


def norm_back_call(chain, own, far, gradient, state, params, chunks=2):
    _, rows, width = state.shape
    shape = (chunks, rows, width)
    spec, turned = chunk_specs(chunks, rows, width)
    pair = chain.take_pair() if chunks == 2 else ()
    results = chain.call(
        functools.partial(norm_back_body, extra=len(pair)),
        (chunks,),
        (own, far, gradient, state, params, *pair),
        [spec, turned, spec, spec, whole_spec(params.shape)] + [spec] * len(pair),
        [spec, whole_spec((2, width))] + [spec] * (len(pair) // 2),
        [
            jax.ShapeDtypeStruct(shape, bf16 if chunks == 2 else f32),
            jax.ShapeDtypeStruct((2, width), f32),
        ]
        + [jax.ShapeDtypeStruct(shape, bf16)] * (len(pair) // 2),
        [],
        SMALL,
        1e3,
        0,
        63,
        "norm_bwd",
    )
    chain.give_pair(results[2:])
    return results[:2]


def weight_body(*refs):
    own0, near0, right0, own1, near1, right1 = refs[:6]
    out_ref, total = refs[-2], refs[-1]
    step = pl.program_id(0)
    part = dot_nn(row_half(own0, near0, 0).T, right0[...])
    part = part + dot_nn(row_half(own1, near1, 0).T, right1[...])

    @pl.when(step == 0)
    def _():
        total[...] = part

    @pl.when(step > 0)
    def _():
        out_ref[...] = (total[...] + part).astype(bf16)


def weight_call(chain, lefts, rights, buffer, all_columns, place):
    _, rows, width = lefts[0][0].shape
    columns = rights[0].shape[1]
    left = pl.BlockSpec((1, rows, width), lambda step: (step, 0, 0))
    right = pl.BlockSpec((2 * rows, columns), lambda step: (step, 0))
    inputs = [*lefts[0], rights[0], *lefts[1], rights[1]]
    in_specs = [left, left, right] * 2
    given = None
    if buffer is not None:
        given = {len(inputs): 0}
        inputs.append(buffer)
        in_specs.append(pl.BlockSpec(memory_space=pl.ANY))
    return chain.call(
        weight_body,
        (2,),
        inputs,
        in_specs,
        [pl.BlockSpec((width, columns), lambda step: (0, place))],
        [jax.ShapeDtypeStruct((width, all_columns), bf16)],
        [pltpu.VMEM((width, columns), f32)],
        BIG,
        1e3,
        0,
        63,
        "weight_grad",
        aliases=given,
    )[0]


def swap(value, axis, bit):
    size = lax.axis_size(axis)
    return lax.ppermute(value, axis, [(index, index ^ bit) for index in range(size)])


def total_over(value, axis):
    bit = 1
    while bit < lax.axis_size(axis):
        value = value + swap(value, axis, bit)
        bit *= 2
    return value


def offset_onehot(grid_side):
    places = jnp.arange(grid_side)
    offset = places[:, None] - places[None, :] + grid_side - 1
    return (offset[:, :, None] == jnp.arange(2 * grid_side - 1)[None, None, :]).astype(f32)


def lamb_moments(param, first, second, gradient):
    first_new = beta_first * first + (1.0 - beta_first) * gradient
    second_new = beta_second * second + (1.0 - beta_second) * gradient * gradient
    corrected = first_new / (1.0 - beta_first**STEP)
    update = (
        corrected / (jnp.sqrt(second_new / (1.0 - beta_second**STEP)) + adam_epsilon)
        + decay_rate * param
    )
    return (first_new, second_new, update)


def shards(
    tokens, cotangent, key_mask, group_bucket, group_count, time_table,
    ln_params, ln_first, ln_second, rel_table, rel_first, rel_second,
    qkv_weight, qkv_first, qkv_second, time_weight, time_first, time_second,
    out_weight, out_first, out_second, up_weight, up_first, up_second,
    down_weight, down_first, down_second,
):
    slots, rows, width = tokens.shape
    seq = key_mask.shape[1]
    layers = ln_params.shape[0]
    parts = lax.axis_size("mp")
    groups = lax.axis_size("group")
    heads = rel_table.shape[1] // parts
    buckets = time_table.shape[0]
    grid_side = (rel_table.shape[3] + 1) // 2
    shard_rows = qkv_weight.shape[1]
    local_width = qkv_weight.shape[3]
    place = lax.axis_index("mp")
    group = lax.axis_index("group")
    head_start = place * heads
    order = jnp.arange(CHUNKS) ^ place
    images = range(slots)

    def ready(layer):
        qkv = qkv_weight[layer].astype(bf16).reshape(shard_rows, 3, heads, HEAD)
        qkv = qkv.transpose(0, 2, 1, 3).reshape(shard_rows, heads, 3 * HEAD)
        out = out_weight[layer].astype(bf16).T.reshape(shard_rows, heads, HEAD)
        blocks = jnp.concatenate([qkv, out[:, :, :SPARE]], axis=2).reshape(shard_rows, heads * 256)
        attend = jnp.concatenate(
            [blocks, out[:, :, SPARE:].reshape(shard_rows, heads * (HEAD - SPARE))], axis=1
        )
        up = up_weight[layer].astype(bf16)
        down = down_weight[layer].astype(bf16).T
        return (attend, up, down)

    hidden = up_weight.shape[2]
    fetched = [{} for _ in range(layers)]

    def fetch_together(*wanted):
        parts = [local[layer][kind] for kind, layer in wanted]
        whole = lax.all_gather(jnp.concatenate(parts, axis=1), "group", axis=0, tiled=True)
        start = 0
        for (kind, layer), part in zip(wanted, parts):
            fetched[layer][kind] = (whole, start)
            start += part.shape[1]

    local = [dict(zip(("attend", "up", "down"), ready(layer))) for layer in range(layers)]
    for layer in range(layers):
        fetch_together(("attend", layer))
        fetch_together(("up", layer), ("down", layer))

    table_low = time_table.astype(bf16)
    own_rows = lax.dynamic_slice_in_dim(table_low, group * shard_rows, shard_rows, 1)
    time_part = jnp.einsum(
        "bd,ldf->lbf",
        own_rows,
        time_weight.astype(bf16).reshape(layers, shard_rows, 2 * local_width),
        preferred_element_type=f32,
    )
    early = jnp.concatenate(
        [
            time_part.reshape(layers * buckets, 2 * local_width),
            jnp.full((1, 2 * local_width), group_count[0].astype(f32)),
        ]
    )
    early = total_over(early, "group")
    inverse = 1.0 / early[layers * buckets, 0]
    own_shift = lax.dynamic_index_in_dim(
        early[: layers * buckets].reshape(layers, buckets, 2, heads, HEAD),
        group_bucket[0],
        1,
        keepdims=False,
    )
    zero_shift = jnp.zeros_like(own_shift[:, 0])
    shifts = jnp.concatenate([own_shift[:, 0], zero_shift, own_shift[:, 1]], axis=2)
    shifts = jnp.pad(shifts, ((0, 0), (0, 0), (0, 256 - 3 * HEAD)))[:, :, None, :]

    chunk_side = grid_side // CHUNKS
    row_of = (order[:, None] * chunk_side + jnp.arange(chunk_side)[None]).reshape(grid_side)
    side = jnp.arange(grid_side)
    row_hot = jnp.broadcast_to(
        (row_of[:, None] == side[None])[:, None], (grid_side, grid_side, grid_side)
    )
    col_hot = jnp.broadcast_to(
        (side[:, None] == side[None])[None], (grid_side, grid_side, grid_side)
    )
    hot = jnp.concatenate([row_hot, col_hot], axis=2).reshape(seq, 2 * grid_side)
    qpos = jnp.concatenate([hot, hot], axis=1).astype(bf16)
    onehot = offset_onehot(grid_side)
    own_rel = lax.dynamic_slice_in_dim(rel_table, head_start, heads, 1)
    toeplitz = jnp.einsum("abr,lhpr->lhpba", onehot, own_rel, precision=highest) * ROOT
    row_ext = toeplitz[:, :, 0].reshape(layers, heads, CHUNKS, chunk_side, grid_side)
    row_ext = jnp.take(row_ext, order, axis=2).reshape(layers, heads, grid_side, 1, grid_side)
    full = (layers, heads, grid_side, grid_side, grid_side)
    ext = jnp.concatenate(
        [jnp.broadcast_to(row_ext, full), jnp.broadcast_to(toeplitz[:, :, 1][:, :, None], full)],
        axis=4,
    ).reshape(layers, heads, seq, 2 * grid_side)
    ext_high = lax.reduce_precision(ext, 8, 7)
    kpos = jnp.concatenate([ext_high, ext - ext_high], axis=3).astype(bf16)
    lane = jnp.arange(LANE)
    live = jnp.take(key_mask.reshape(slots, CHUNKS, rows), order, axis=1).reshape(slots, seq)
    aux = jnp.where((lane >= HEAD) & (lane < HEAD + 3), 1.0, 0.0)[None, None]
    aux = jnp.where(
        lane == HEAD + 3, jnp.where(live > 0, 0.0, MASKED)[:, :, None], aux
    ).astype(bf16)

    chain = Chain()
    chain.hold(qpos, kpos, aux)
    slot_live = (jnp.arange(slots) < group_count[0]).astype(f32)
    saved = {}
    work = {}
    ends = {}

    start_rows = jnp.stack([tokens, swap(tokens, "mp", 2)], axis=1)
    start_low = cotangent.astype(f32) * slot_live[:, None, None]
    start_low = jnp.stack([start_low.astype(bf16), swap(start_low.astype(bf16), "mp", 2)], axis=1)

    def far_of(own, last):
        return swap(own[1:], "mp", 2) if last else swap(own, "mp", 2)

    def image_steps(image):
        base, parts = start_rows[image], ()
        for layer in range(layers):
            weights = fetched[layer]
            if layer == 0 and image == images[-1]:
                chain.hold(shifts)
            state, normed = norm_call(chain, base, parts, ln_params[layer, 0:2])
            pieces = (normed, swap(normed, "mp", 1))
            yield
            if layer == 0 and image == 0:
                chain.hold(start_low)
            pieces_one = pieces
            qkv, mixed, keep, send = attend_call(
                chain, pieces, weights, shifts[layer], aux[image], qpos, kpos[layer]
            )
            near = swap(send, "mp", 1)
            yield
            own = yield from add_steps(chain, keep, near)
            parts = (own, far_of(own, False))
            touch_call(chain, parts[1])
            yield
            middle, normed = norm_call(chain, state, parts, ln_params[layer, 2:4])
            pieces = (normed, swap(normed, "mp", 1))
            yield
            pre, act, keep, send = mlp_call(chain, pieces, weights, hidden)
            near = swap(send, "mp", 1)
            saved[layer, image] = (state, pieces_one, qkv, mixed, middle, pieces, pre, act)
            base = middle
            if layer < layers - 1:
                yield
                own = yield from add_steps(chain, keep, near)
                parts = (own, far_of(own, False))
                touch_call(chain, parts[1])
                yield
        yield
        low = start_low[image]
        pieces = (low, swap(low, "mp", 1))
        last_pair = (keep, near)
        for layer in reversed(range(layers)):
            weights = fetched[layer]
            state, pieces_one, qkv, mixed, middle, pieces_two, pre, act = saved[layer, image]
            dpre, keep, send = mlp_back_call(chain, pieces, pre, weights)
            near = swap(send, "mp", 1)
            work["down", layer, image] = (pieces, act)
            work["up", layer, image] = (pieces_two, dpre)
            yield
            if last_pair is not None:
                own, last_own = add_both_call(chain, (keep, near), last_pair)
                far = far_of(own, False)
                ends[image] = (base, last_own, far)
                last_pair = None
                yield
            else:
                own = yield from add_steps(chain, keep, near)
                far = far_of(own, False)
            touch_call(chain, far)
            yield
            low, sums_two = norm_back_call(
                chain, own, far, low, middle, ln_params[layer, 2:3]
            )
            pieces = (low, swap(low, "mp", 1))
            work["out", layer, image] = (pieces, mixed)
            yield
            dqkv, col_sums, rel_part, keep, send = attend_back_call(
                chain, pieces, weights, qkv, qpos, kpos[layer], mixed
            )
            near = swap(send, "mp", 1)
            work["qkv", layer, image] = (pieces_one, dqkv)
            yield
            own = yield from add_steps(chain, keep, near)
            far = far_of(own, layer == 0)
            touch_call(chain, far)
            yield
            low, sums_one = norm_back_call(
                chain, own, far, low, state, ln_params[layer, 0:1], 2 if layer else 1
            )
            pieces = (low, swap(low, "mp", 1)) if layer else None
            work["small", layer, image] = (col_sums, rel_part, sums_one, sums_two)
            yield
        ends["gradient", image] = low[0]

    buffers = {}
    sums = {}
    wholes = {"mlp": 2 * hidden, "attend": heads * (256 + LANE)}
    places = {"up": ("mlp", 0), "down": ("mlp", 1), "qkv": ("attend", 0), "out": ("attend", 2)}

    def unpack_step(layer):
        fetched[layer]["out"] = unpack_call(chain, *fetched[layer]["attend"], heads)

    def end_step(image):
        ends[image] = end_call(chain, *ends[image])

    def weight_step(kind, layer):
        lefts, rights = zip(*(work[kind, layer, image] for image in images))
        target, place = places[kind]
        buffer = buffers.pop((target, layer), None)
        whole = weight_call(chain, lefts, rights, buffer, wholes[target], place)
        if buffer is None:
            buffers[target, layer] = whole
            return
        if (target, layer) == ("attend", 0):
            buffers[target, layer] = whole
        else:
            sums[target, layer] = scatter(whole)

    def scatter(whole):
        return lax.psum_scatter(
            whole.reshape(groups, shard_rows, whole.shape[1]),
            "group",
            scatter_dimension=0,
            tiled=False,
        )

    def last_step():
        whole = gate_call(chain, buffers.pop(("attend", 0)), sums["mlp", 0])
        sums["attend", 0] = scatter(whole)

    runs = [image_steps(image) for image in images]
    for entry in SEQUENCE:
        if entry[0] in "ip":
            chain.postpone = entry[0] == "p"
            next(runs[int(entry[1:])])
        elif entry in ("e0", "e1"):
            end_step(int(entry[1:]))
        elif entry == "last":
            last_step()
        elif entry[:6] == "unpack":
            unpack_step(int(entry[-1]))
        elif entry[:5] == "hold_":
            chain.hold(sums[entry[5:-1], int(entry[-1])])
        else:
            weight_step(entry[:-1], int(entry[-1]))
    for steps in runs:
        next(steps, None)

    block_out = jnp.stack([ends[image] for image in images])
    grads = [ends["gradient", image] for image in images]
    norm_grads = [None] * layers
    rel_grads = [None] * layers
    time_sums = [None] * layers
    for layer in range(layers):

        def both(index):
            return sum(work["small", layer, image][index] for image in images)

        col_sums = both(0)[:, 0, : 3 * HEAD].reshape(heads, 3, HEAD)
        time_sums[layer] = jnp.stack([col_sums[:, 0], col_sums[:, 2]]).reshape(2 * local_width)
        rel_sum = both(1)
        row_sum = rel_sum[:, 0, :, :grid_side].reshape(heads, CHUNKS, chunk_side, grid_side)
        row_sum = jnp.take(row_sum, order, axis=1).reshape(heads, grid_side, grid_side)
        col_sum = rel_sum[:, 1, :, grid_side : 2 * grid_side]
        rel_grads[layer] = jnp.einsum(
            "abr,hpba->hpr", onehot, jnp.stack([row_sum, col_sum], axis=1), precision=highest
        )
        norm_grads[layer] = jnp.concatenate([both(2), both(3)])

    bucket_hot = (jnp.arange(buckets) == group_bucket[0]).astype(f32)
    time_buckets = bucket_hot[None, :, None] * jnp.stack(time_sums)[:, None, :]
    sizes = (time_buckets.size, layers * 4 * width, layers * heads * 2 * (2 * grid_side - 1))
    late = jnp.concatenate(
        [
            time_buckets.reshape(-1),
            jnp.stack(norm_grads).reshape(-1),
            jnp.stack(rel_grads).reshape(-1),
        ]
    )
    late = total_over(jnp.pad(late, (0, -late.size % 1024)).reshape(-1, LANE), "group").reshape(-1)
    time_total = late[: sizes[0]].reshape(layers, buckets, 2 * local_width)
    norm_own = late[sizes[0] : sizes[0] + sizes[1]]
    rel_own = late[sizes[0] + sizes[1] : sum(sizes)].reshape(layers, heads, 2, 2 * grid_side - 1)
    rel_whole = lax.dynamic_update_slice_in_dim(
        jnp.zeros(rel_table.shape, f32), rel_own, head_start, 1
    )
    mixed_sums = jnp.concatenate([norm_own, rel_whole.reshape(-1)])
    mixed_sums = total_over(
        jnp.pad(mixed_sums, (0, -mixed_sums.size % 1024)).reshape(-1, LANE), "mp"
    ).reshape(-1)
    norm_sum = mixed_sums[: sizes[1]].reshape(ln_params.shape)
    rel_sum = mixed_sums[sizes[1] : sizes[1] + rel_table.size].reshape(rel_table.shape)

    tokens_grad = (jnp.stack(grads) * inverse).astype(bf16)
    ln_first_new, ln_second_new, ln_update = lamb_moments(
        ln_params, ln_first, ln_second, norm_sum * inverse
    )
    ln_ratio = jnp.sqrt(jnp.sum(ln_params * ln_params, axis=-1, keepdims=True)) / jnp.sqrt(
        jnp.sum(ln_update * ln_update, axis=-1, keepdims=True)
    )
    ln_new = ln_params - learn_rate * ln_ratio * ln_update
    rel_first_new, rel_second_new, rel_update = lamb_moments(
        rel_table, rel_first, rel_second, rel_sum * inverse
    )
    rel_ratio = jnp.sqrt(jnp.sum(rel_table * rel_table, axis=(1, 2, 3), keepdims=True)) / jnp.sqrt(
        jnp.sum(rel_update * rel_update, axis=(1, 2, 3), keepdims=True)
    )
    rel_new = rel_table - learn_rate * rel_ratio * rel_update

    def unpack(layer):
        attend = sums["attend", layer].astype(f32)
        g_qkv, g_out = attend[:, : heads * 256], attend[:, heads * 256 :]
        g_up, g_down = jnp.split(sums["mlp", layer].astype(f32), 2, axis=1)
        g_qkv = g_qkv.reshape(shard_rows, heads, 256)[:, :, : 3 * HEAD]
        g_qkv = g_qkv.reshape(shard_rows, heads, 3, HEAD).transpose(0, 2, 1, 3)
        g_qkv = g_qkv.reshape(shard_rows, 3, local_width)
        g_time = lax.dot_general(
            own_rows.astype(f32),
            time_total[layer],
            (((0,), (0,)), ((), ())),
            precision=highest,
        ).reshape(shard_rows, 2, local_width)
        g_out = g_out.reshape(shard_rows, heads, LANE)[:, :, :HEAD].reshape(shard_rows, local_width)
        return (g_qkv, g_time, g_out.T, g_up, g_down.T)

    unpacked = [unpack(layer) for layer in range(layers)]
    masters = (qkv_weight, time_weight, out_weight, up_weight, down_weight)
    first_olds = (qkv_first, time_first, out_first, up_first, down_first)
    second_olds = (qkv_second, time_second, out_second, up_second, down_second)
    sectioned = []
    squares = []
    for index in range(5):
        master = masters[index]
        reduced = jnp.stack([unpacked[layer][index] for layer in range(layers)]) * inverse
        first_new, second_new, update = lamb_moments(
            master, first_olds[index], second_olds[index], reduced
        )
        axes = tuple(range(1, master.ndim))
        squares.append(
            jnp.stack([jnp.sum(master * master, axis=axes), jnp.sum(update * update, axis=axes)])
        )
        sectioned.append((first_new, second_new, update))

    def summed(parts):
        totals = jnp.stack(parts, axis=2)
        flat = jnp.pad(totals.reshape(-1), (0, 1024 - totals.size)).reshape(8, LANE)
        flat = total_over(total_over(flat, "group"), "mp")
        return flat.reshape(-1)[: totals.size].reshape(totals.shape)

    totals = jnp.concatenate([summed(squares[:3]), summed(squares[3:])], axis=2)
    weight_norm = jnp.sqrt(totals[0])
    update_norm = jnp.sqrt(totals[1])
    trust_ratio = weight_norm / update_norm
    results = []
    for index in range(5):
        master = masters[index]
        first_new, second_new, update = sectioned[index]
        factor = (learn_rate * trust_ratio[:, index]).reshape((layers,) + (1,) * (master.ndim - 1))
        renewed = master - factor * update
        results.extend([renewed, first_new, second_new, renewed.astype(bf16)])
    matrix_stats = jnp.stack([weight_norm, update_norm, trust_ratio])
    return (
        block_out, tokens_grad, ln_new, ln_first_new, ln_second_new,
        rel_new, rel_first_new, rel_second_new, *results, matrix_stats,
    )


def solution(mesh):
    rows = P("group", "mp", None)
    wide = P(None, "group", None, "mp")
    tall = P(None, "mp", "group")
    flat = P(None, "group", "mp")
    in_specs = (
        (rows, rows, P("group", None), P("group"), P("group"))
        + (P(),) * 7
        + (wide,) * 6
        + (tall,) * 3
        + (flat,) * 3
        + (tall,) * 3
    )
    out_specs = (
        (rows, rows) + (P(),) * 6 + (wide,) * 8 + (tall,) * 4 + (flat,) * 4 + (tall,) * 4 + (P(),)
    )
    return jax.shard_map(shards, mesh=mesh, in_specs=in_specs, out_specs=out_specs, check_vma=False)
```

time: 3140 us -> 846 us (0.27)
  waiting for transfers between devices: 1460 us -> 154 us
  local copies, waits for them, and re-layouts: 655 us -> 52.5 us
  Pallas kernels: 0 us -> 481 us
  matrix products: 421 us -> 4.17 us
  other arithmetic: 404 us -> 73.8 us
  blocking collectives: 154 us -> 0 us
  starting transfers between devices: 2.87 us -> 52.3 us
    reduce_scatter x16 -> x4, waiting for transfers between devices: 633 us -> 25.6 us  [scatter(): lax.psum_scatter(whole.reshape(groups, shard_rows, whole.shape[1]), 'grou...]
    all_gather x16 -> x4, waiting for transfers between devices: 588 us -> 17.7 us  [fetch_together(): lax.all_gather(jnp.concatenate(parts, axis=1), 'group', axis=0, tiled=True)]
    pallas_call x0 -> x63, Pallas kernels: none -> 481 us  [call(): pl.pallas_call(wrapped, grid=grid, in_specs=[pl.BlockSpec(memory_space=pl...]
    add x20 -> x1, local copies, waits for them, and re-layouts: 418 us -> 0.09 us  [shards(): order[:, None] * chunk_side + jnp.arange(chunk_side)[None]]
    dot_general x91 -> x6, matrix products: 421 us -> 4.17 us  [the longest x2 1.84 us: shards(): jnp.einsum('abr,hpba->hpr', onehot, jnp.stack([row_sum, col_sum], axis=1)...]
    unnamed x34 -> x8, waiting for transfers between devices: 238 us -> 0.13 us
    add x12 -> x24, other arithmetic: 177 us -> 4.72 us  [the longest x17 2.91 us: total_over(): value = value + swap(value, axis, bit)]
    reshape x8 -> x20, local copies, waits for them, and re-layouts: 168 us -> 3.23 us  [the longest x4 1.25 us: unpack(): g_out.reshape(shard_rows, heads, LANE)[:, :, :HEAD]]
  transfers between devices with their start and end apart: 33 -> 74, of which waited for: 28 -> 40; matrix products, arithmetic and copies ran while one was open for 18% -> 10% of each run, Pallas kernels for 0% -> 54%
where the time goes in v1:
time: 846 us; the launch traced here: 836 us
  Pallas kernels  481 us (57%)
  waiting for transfers between devices  154 us (18%)
  other arithmetic  73.8 us (9%)
  local copies, waits for them, and re-layouts  52.5 us (6%)
  starting transfers between devices  52.3 us (6%)
  between operations  18.1 us (2%)
    pallas_call x63, Pallas kernels, call(): pl.pallas_call(wrapped, grid=grid, in_specs=[pl.BlockSpec(memory_space=pl...  481 us
    ppermute x66, waiting for transfers between devices, swap(): lax.ppermute(value, axis, [(index, index ^ bit) for index in range(size)])  111 us
    ppermute x66, starting transfers between devices, swap(): lax.ppermute(value, axis, [(index, index ^ bit) for index in range(size)])  52 us
    reduce_scatter x4, waiting for transfers between devices, scatter(): lax.psum_scatter(whole.reshape(groups, shard_rows, whole.shape[1]), 'grou...  25.6 us
    unnamed x154, local copies, waits for them, and re-layouts  21.9 us
    all_gather x4, waiting for transfers between devices, fetch_together(): lax.all_gather(jnp.concatenate(parts, axis=1), 'group', axis=0, tiled=True)  17.7 us
  transfers between devices with their start and end apart: 74, of which 40 were waited for; matrix products, arithmetic and copies ran while one was open for 10% of the time, Pallas kernels for 54%

profile of v1, /device:TPU:0, one launch (start us, length us, event | category | flops | bytes accessed | tf_op | source)
XLA Modules:
  0.0 836.3 jit_solution(6386810801194477383)
XLA Ops:
  19.0 3.0 collective-permute-start.1
  38.3 4.1 pad_maximum_fusion.2.refs_1_
  47.6 9.2 %collective-permute-done.2 = f32[33,576]{1,0:T(8,128)S(1)} collective-permute-done((f32[33,576]{1,0:T(8,128)S(1)}, f32[33,576]{1,0:T(8,128)S(1)}, u32[]{:S(2)}, u32[]{:S(2)}) %collective-permute-start.2) | collective-permute-done | bytes 76064 | tf_op jit(solution)/shard_map/ppermute | solution.py:780
  57.7 2.9 fusion.11
  60.6 3.1 norm_fwd.8
  63.7 4.6 fusion.16
  71.9 2.8 norm_fwd.9
  75.0 3.3 pad_maximum_fusion.1.refs_0_
  78.3 4.0 unpack_out.2
  82.4 19.2 %attend_fwd.4 = (bf16[4,3,1024,128]{3,2,1,0:T(8,128)(2,1)}, bf16[1024,512]{1,0:T(8,128)(2,1)}, bf16[2,256,1152]{2,1,0:T(8,128)(2,1)}, bf16[2,256,1152]{2,1,0:T(8,128)(2,1)}, f32[8,128]{1,0:T(8,128)}) custom-call(bf16[2,2,256,1152]{3,2,1,0:T(8,128)(2,1)} %pad_maximum_fusion.1.refs_0_, f32[8,128]{1,0:T(8,128)} %get-tuple-element.205.refs_1_, ...), custom_call_target="tpu_custom_call" | custom-call | flops 6000000 | bytes 1000 | tf_op jit(solution)/shard_map/attend_fwd/pallas_call | solution.py:114
  108.9 18.8 %attend_fwd.5 = (bf16[4,3,1024,128]{3,2,1,0:T(8,128)(2,1)}, bf16[1024,512]{1,0:T(8,128)(2,1)}, bf16[2,256,1152]{2,1,0:T(8,128)(2,1)}, bf16[2,256,1152]{2,1,0:T(8,128)(2,1)}, f32[8,128]{1,0:T(8,128)}) custom-call(f32[8,128]{1,0:T(8,128)} %get-tuple-element.212.refs_0_, bf16[2,256,1152]{2,1,0:T(8,128)(2,1)} %get-tuple-element.213.refs_1_.refs_4_, ...), custom_call_target="tpu_custom_call" | custom-call | flops 6000000 | bytes 1000 | tf_op jit(solution)/shard_map/attend_fwd/pallas_call | solution.py:114
  127.8 8.0 collective-permute-done.7.refs_0_.refs_3_
  136.3 14.8 %norm_fwd.10 = (bf16[2,256,1152]{2,1,0:T(8,128)(2,1)}, bf16[2,256,1152]{2,1,0:T(8,128)(2,1)}, bf16[2,256,1152]{2,1,0:T(8,128)(2,1)}, f32[8,128]{1,0:T(8,128)}) custom-call(f32[8,128]{1,0:T(8,128)} %far_ready.14.refs_0_, bf16[2,256,1152]{2,1,0:T(8,128)(2,1)} %get-tuple-element.215.refs_1_.refs_4_, bf16[2,256,1152]{2,1,0:T(8,128)(2,1)} %get-tuple-element.211.refs_2_, ...), custom_call_target="tpu_custom_call" | custom-call | flops 60000000 | bytes 1000 | tf_op jit(solution)/shard_map/norm_fwd/pallas_call | solution.py:114
  154.4 7.9 all-gather.7.cloned.1.call-done.refs_3_.refs_4_.refs_5_
  162.3 11.9 %mlp_fwd.4 = (bf16[1024,1152]{1,0:T(8,128)(2,1)}, bf16[1024,1152]{1,0:T(8,128)(2,1)}, bf16[2,256,1152]{2,1,0:T(8,128)(2,1)}, bf16[2,256,1152]{2,1,0:T(8,128)(2,1)}, f32[8,128]{1,0:T(8,128)}) custom-call(f32[8,128]{1,0:T(8,128)} %get-tuple-element.219.refs_0_, bf16[2,256,1152]{2,1,0:T(8,128)(2,1)} %get-tuple-element.220.refs_1_.refs_2_, ...), custom_call_target="tpu_custom_call" | custom-call | flops 6000000 | bytes 1000 | tf_op jit(solution)/shard_map/mlp_fwd/pallas_call | solution.py:114
  175.2 4.7 collective-permute-done.10.refs_0_.refs_3_
  180.5 4.7 norm_fwd.11
  188.3 11.9 %mlp_fwd.5 = (bf16[1024,1152]{1,0:T(8,128)(2,1)}, bf16[1024,1152]{1,0:T(8,128)(2,1)}, bf16[2,256,1152]{2,1,0:T(8,128)(2,1)}, bf16[2,256,1152]{2,1,0:T(8,128)(2,1)}, f32[8,128]{1,0:T(8,128)}) custom-call(f32[8,128]{1,0:T(8,128)} %get-tuple-element.226.refs_0_, bf16[2,256,1152]{2,1,0:T(8,128)(2,1)} %get-tuple-element.227.refs_1_.refs_5_, ...), custom_call_target="tpu_custom_call" | custom-call | flops 6000000 | bytes 1000 | tf_op jit(solution)/shard_map/mlp_fwd/pallas_call | solution.py:114
  200.3 13.5 %collective-permute-done.13.refs_0_.refs_3_ = bf16[2,256,1152]{2,1,0:T(8,128)(2,1)} collective-permute-done((bf16[2,256,1152]{2,1,0:T(8,128)(2,1)}, bf16[2,256,1152]{2,1,0:T(8,128)(2,1)}, u32[]{:S(2)}, u32[]{:S(2)}) %collective-permute-start.13) | collective-permute-done | bytes 1179680 | tf_op jit(solution)/shard_map/ppermute | solution.py:780
  214.4 3.8 all-gather.9.cloned.1.call-done.refs_1_.refs_3_.refs_8_
  218.2 4.0 unpack_out.3
  222.3 4.7 norm_fwd.12
  230.2 18.9 %attend_fwd.6 = (bf16[4,3,1024,128]{3,2,1,0:T(8,128)(2,1)}, bf16[1024,512]{1,0:T(8,128)(2,1)}, bf16[2,256,1152]{2,1,0:T(8,128)(2,1)}, bf16[2,256,1152]{2,1,0:T(8,128)(2,1)}, f32[8,128]{1,0:T(8,128)}) custom-call(f32[8,128]{1,0:T(8,128)} %get-tuple-element.234.refs_0_, bf16[2,256,1152]{2,1,0:T(8,128)(2,1)} %get-tuple-element.235.refs_1_, ...), custom_call_target="tpu_custom_call" | custom-call | flops 6000000 | bytes 1000 | tf_op jit(solution)/shard_map/attend_fwd/pallas_call | solution.py:114
  249.3 6.4 collective-permute-done.16.refs_0_.refs_3_
  256.3 5.2 norm_fwd.13
  264.7 19.3 %attend_fwd.7 = (bf16[4,3,1024,128]{3,2,1,0:T(8,128)(2,1)}, bf16[1024,512]{1,0:T(8,128)(2,1)}, bf16[2,256,1152]{2,1,0:T(8,128)(2,1)}, bf16[2,256,1152]{2,1,0:T(8,128)(2,1)}, f32[8,128]{1,0:T(8,128)}) custom-call(f32[8,128]{1,0:T(8,128)} %get-tuple-element.242.refs_0_, bf16[2,256,1152]{2,1,0:T(8,128)(2,1)} %get-tuple-element.243.refs_1_.refs_4_, ...), custom_call_target="tpu_custom_call" | custom-call | flops 6000000 | bytes 1000 | tf_op jit(solution)/shard_map/attend_fwd/pallas_call | solution.py:114
  284.1 6.1 collective-permute-done.19.refs_0_.refs_3_
  290.8 4.6 norm_fwd.14
  295.4 3.3 fusion.10
  300.6 6.0 all-gather.11.cloned.1.call-done.refs_3_.refs_4_.refs_5_
  306.5 11.9 %mlp_fwd.6 = (bf16[1024,1152]{1,0:T(8,128)(2,1)}, bf16[1024,1152]{1,0:T(8,128)(2,1)}, bf16[2,256,1152]{2,1,0:T(8,128)(2,1)}, bf16[2,256,1152]{2,1,0:T(8,128)(2,1)}, f32[8,128]{1,0:T(8,128)}) custom-call(f32[8,128]{1,0:T(8,128)} %get-tuple-element.249.refs_0_, bf16[2,256,1152]{2,1,0:T(8,128)(2,1)} %get-tuple-element.250.refs_1_, ...), custom_call_target="tpu_custom_call" | custom-call | flops 6000000 | bytes 1000 | tf_op jit(solution)/shard_map/mlp_fwd/pallas_call | solution.py:114
  318.4 13.0 %mlp_bwd.4 = (bf16[1024,1152]{1,0:T(8,128)(2,1)}, bf16[2,256,1152]{2,1,0:T(8,128)(2,1)}, bf16[2,256,1152]{2,1,0:T(8,128)(2,1)}, f32[8,128]{1,0:T(8,128)}) custom-call(f32[8,128]{1,0:T(8,128)} %get-tuple-element.251.refs_0_, bf16[2,256,1152]{2,1,0:T(8,128)(2,1)} %get-tuple-element.515.refs_1_.refs_3_, bf16[2,256,1152]{2,1,0:T(8,128)(2,1)} %collective-permute-done.24.refs_2_, ...), custom_call_target="tpu_custom_call" | custom-call | flops 6000000 | bytes 1000 | tf_op jit(solution)/shard_map/mlp_bwd/pallas_call | solution.py:114
  336.2 5.2 add_both.2
  341.4 3.6 norm_fwd.15
  348.2 11.9 %mlp_fwd.7 = (bf16[1024,1152]{1,0:T(8,128)(2,1)}, bf16[1024,1152]{1,0:T(8,128)(2,1)}, bf16[2,256,1152]{2,1,0:T(8,128)(2,1)}, bf16[2,256,1152]{2,1,0:T(8,128)(2,1)}, f32[8,128]{1,0:T(8,128)}) custom-call(f32[8,128]{1,0:T(8,128)} %get-tuple-element.261.refs_0_, bf16[2,256,1152]{2,1,0:T(8,128)(2,1)} %get-tuple-element.262.refs_1_.refs_4_, ...), custom_call_target="tpu_custom_call" | custom-call | flops 6000000 | bytes 1000 | tf_op jit(solution)/shard_map/mlp_fwd/pallas_call | solution.py:114
  360.0 13.0 %mlp_bwd.5 = (bf16[1024,1152]{1,0:T(8,128)(2,1)}, bf16[2,256,1152]{2,1,0:T(8,128)(2,1)}, bf16[2,256,1152]{2,1,0:T(8,128)(2,1)}, f32[8,128]{1,0:T(8,128)}) custom-call(f32[8,128]{1,0:T(8,128)} %get-tuple-element.263.refs_0_, bf16[2,256,1152]{2,1,0:T(8,128)(2,1)} %get-tuple-element.514.refs_1_.refs_4_.refs_3_, ...), custom_call_target="tpu_custom_call" | custom-call | flops 6000000 | bytes 1000 | tf_op jit(solution)/shard_map/mlp_bwd/pallas_call | solution.py:114
  374.1 11.3 %weight_grad.8 = (bf16[1152,2304]{1,0:T(8,128)(2,1)}, f32[8,128]{1,0:T(8,128)}) custom-call(f32[8,128]{1,0:T(8,128)} %get-tuple-element.265.refs_0_, bf16[2,256,1152]{2,1,0:T(8,128)(2,1)} %get-tuple-element.250.refs_1_, bf16[2,256,1152]{2,1,0:T(8,128)(2,1)} %collective-permute-done.23.refs_2_, bf16[1024,1152]{1,0:T(8,128)(2,1)} %get-tuple-element.266.refs_3_, ...), custom_call_target="tpu_custom_call" | custom-call | flops 6000000 | bytes 1000 | tf_op jit(solution)/shard_map/weight_grad/pallas_call | solution.py:114
  387.0 5.0 add_both.3
  392.0 4.7 norm_bwd.8
  396.7 11.3 %weight_grad.9 = (bf16[1152,2304]{1,0:T(8,128)(2,1)}, f32[8,128]{1,0:T(8,128)}) custom-call(f32[8,128]{1,0:T(8,128)} %get-tuple-element.276.refs_0_, bf16[2,256,1152]{2,1,0:T(8,128)(2,1)} %get-tuple-element.515.refs_1_.refs_3_, bf16[2,256,1152]{2,1,0:T(8,128)(2,1)} %collective-permute-done.24.refs_2_, ...), custom_call_target="tpu_custom_call", output_to_operand_aliasing={{0}: (7, {})} | custom-call | flops 6000000 | bytes 1000 | tf_op jit(solution)/shard_map/weight_grad/pallas_call | solution.py:114
  413.2 25.9 %attend_bwd.4 = (bf16[1024,1024]{1,0:T(8,128)(2,1)}, f32[4,1,256]{2,1,0:T(1,128)}, f32[4,2,32,128]{3,2,1,0:T(8,128)}, bf16[2,256,1152]{2,1,0:T(8,128)(2,1)}, bf1...) custom-call(f32[8,128]{1,0:T(8,128)} %get-tuple-element.280.refs_0_, ...), custom_call_target="tpu_custom_call" | custom-call | flops 6000000 | bytes 1000 | tf_op jit(solution)/shard_map/attend_bwd/pallas_call | solution.py:114
  439.4 11.2 %collective-permute-done.32.refs_0_.refs_2_.refs_3_ = bf16[3,256,1152]{2,1,0:T(8,128)(2,1)} collective-permute-done((bf16[3,256,1152]{2,1,0:T(8,128)(2,1)}, bf16[3,256,1152]{2,1,0:T(8,128)(2,1)}, u32[]{:S(2)}, u32[]{:S(2)}) %collective-permute-start.32) | collective-permute-done | bytes 1769504 | tf_op jit(solution)/shard_map/ppermute | solution.py:780
  451.2 6.0 norm_bwd.9
  460.5 26.1 %attend_bwd.5 = (bf16[1024,1024]{1,0:T(8,128)(2,1)}, f32[4,1,256]{2,1,0:T(1,128)}, f32[4,2,32,128]{3,2,1,0:T(8,128)}, bf16[2,256,1152]{2,1,0:T(8,128)(2,1)}, bf1...) custom-call(f32[8,128]{1,0:T(8,128)} %get-tuple-element.289.refs_0_, ...), custom_call_target="tpu_custom_call" | custom-call | flops 6000000 | bytes 1000 | tf_op jit(solution)/shard_map/attend_bwd/pallas_call | solution.py:114
  486.8 6.3 weight_grad.10
  493.7 5.9 norm_bwd.10
  499.6 9.8 %weight_grad.11 = (bf16[1152,1536]{1,0:T(8,128)(2,1)}, f32[8,128]{1,0:T(8,128)}) custom-call(f32[8,128]{1,0:T(8,128)} %get-tuple-element.298.refs_0_, bf16[2,256,1152]{2,1,0:T(8,128)(2,1)} %get-tuple-element.235.refs_1_, bf16[2,256,1152]{2,1,0:T(8,128)(2,1)} %collective-permute-done.17.refs_2_, ...), custom_call_target="tpu_custom_call", output_to_operand_aliasing={{0}: (7, {})} | custom-call | flops 6000000 | bytes 1000 | tf_op jit(solution)/shard_map/weight_grad/pallas_call | solution.py:114
  514.6 13.2 %mlp_bwd.6 = (bf16[1024,1152]{1,0:T(8,128)(2,1)}, bf16[2,256,1152]{2,1,0:T(8,128)(2,1)}, bf16[2,256,1152]{2,1,0:T(8,128)(2,1)}, f32[8,128]{1,0:T(8,128)}) custom-call(f32[8,128]{1,0:T(8,128)} %get-tuple-element.302.refs_0_, bf16[2,256,1152]{2,1,0:T(8,128)(2,1)} %get-tuple-element.303.refs_1_.refs_3_, bf16[2,256,1152]{2,1,0:T(8,128)(2,1)} %copy-done.21, ...), custom_call_target="tpu_custom_call" | custom-call | flops 6000000 | bytes 1000 | tf_op jit(solution)/shard_map/mlp_bwd/pallas_call | solution.py:114
  528.1 11.3 %collective-permute-done.38.refs_0_.refs_2_ = bf16[2,256,1152]{2,1,0:T(8,128)(2,1)} collective-permute-done((bf16[2,256,1152]{2,1,0:T(8,128)(2,1)}, bf16[2,256,1152]{2,1,0:T(8,128)(2,1)}, u32[]{:S(2)}, u32[]{:S(2)}) %collective-permute-start.38) | collective-permute-done | bytes 1179680 | tf_op jit(solution)/shard_map/ppermute | solution.py:780
  540.0 6.0 norm_bwd.11
  549.2 13.1 %mlp_bwd.7 = (bf16[1024,1152]{1,0:T(8,128)(2,1)}, bf16[2,256,1152]{2,1,0:T(8,128)(2,1)}, bf16[2,256,1152]{2,1,0:T(8,128)(2,1)}, f32[8,128]{1,0:T(8,128)}) custom-call(f32[8,128]{1,0:T(8,128)} %get-tuple-element.310.refs_0_, bf16[2,256,1152]{2,1,0:T(8,128)(2,1)} %get-tuple-element.311.refs_1_.refs_4_.refs_3_, ...), custom_call_target="tpu_custom_call" | custom-call | flops 6000000 | bytes 1000 | tf_op jit(solution)/shard_map/mlp_bwd/pallas_call | solution.py:114
  562.4 11.3 %weight_grad.12 = (bf16[1152,2304]{1,0:T(8,128)(2,1)}, f32[8,128]{1,0:T(8,128)}) custom-call(bf16[144,2304]{1,0:T(8,128)(2,1)} %bitcast.297, f32[8,128]{1,0:T(8,128)} %get-tuple-element.313.refs_1_, bf16[2,256,1152]{2,1,0:T(8,128)(2,1)} %get-tuple-element.220.refs_1_.refs_2_, bf16[2,256,1152]{2,1,0:T(8,128)(2,1)} %collective-permute-done.11.refs_2_.refs_3_, ...), custom_call_target="tpu_custom_call" | custom-call | flops 6000000 | bytes 1000 | tf_op jit(solution)/shard_map/weight_grad/pallas_call | solution.py:114
  575.3 6.4 norm_bwd.12
  581.7 11.3 %weight_grad.13 = (bf16[1152,2304]{1,0:T(8,128)(2,1)}, f32[8,128]{1,0:T(8,128)}) custom-call(f32[8,128]{1,0:T(8,128)} %get-tuple-element.320.refs_0_, bf16[2,256,1152]{2,1,0:T(8,128)(2,1)} %get-tuple-element.303.refs_1_.refs_3_, bf16[2,256,1152]{2,1,0:T(8,128)(2,1)} %copy-done.21, ...), custom_call_target="tpu_custom_call", output_to_operand_aliasing={{0}: (7, {})} | custom-call | flops 6000000 | bytes 1000 | tf_op jit(solution)/shard_map/weight_grad/pallas_call | solution.py:114
  598.2 25.9 %attend_bwd.6 = (bf16[1024,1024]{1,0:T(8,128)(2,1)}, f32[4,1,256]{2,1,0:T(1,128)}, f32[4,2,32,128]{3,2,1,0:T(8,128)}, bf16[2,256,1152]{2,1,0:T(8,128)(2,1)}, bf1...) custom-call(f32[8,128]{1,0:T(8,128)} %get-tuple-element.324.refs_0_, ...), custom_call_target="tpu_custom_call" | custom-call | flops 6000000 | bytes 1000 | tf_op jit(solution)/shard_map/attend_bwd/pallas_call | solution.py:114
  628.3 6.1 norm_bwd.13
  638.7 6.3 weight_grad.14
  645.0 26.1 %attend_bwd.7 = (bf16[1024,1024]{1,0:T(8,128)(2,1)}, f32[4,1,256]{2,1,0:T(1,128)}, f32[4,2,32,128]{3,2,1,0:T(8,128)}, bf16[2,256,1152]{2,1,0:T(8,128)(2,1)}, bf1...) custom-call(bf16[144,1536]{1,0:T(8,128)(2,1)} %bitcast.302, f32[8,128]{1,0:T(8,128)} %get-tuple-element.337.refs_1_, ...), custom_call_target="tpu_custom_call" | custom-call | flops 6000000 | bytes 1000 | tf_op jit(solution)/shard_map/attend_bwd/pallas_call | solution.py:114
  675.4 10.3 %weight_grad.15 = (bf16[1152,1536]{1,0:T(8,128)(2,1)}, f32[8,128]{1,0:T(8,128)}) custom-call(f32[8,128]{1,0:T(8,128)} %get-tuple-element.339.refs_0_, bf16[2,256,1152]{2,1,0:T(8,128)(2,1)} %get-tuple-element.206.refs_2_.refs_1_, bf16[2,256,1152]{2,1,0:T(8,128)(2,1)} %collective-permute-done.5.refs_3_.refs_2_, ...), custom_call_target="tpu_custom_call", output_to_operand_aliasing={{0}: (7, {})} | custom-call | flops 6000000 | bytes 1000 | tf_op jit(solution)/shard_map/weight_grad/pallas_call | solution.py:114
  687.6 13.6 %reduce-scatter.7.cloned.1.call-done = bf16[1,144,2304]{2,1,0:T(8,128)(2,1)} async-done(((bf16[8,144,2304]{2,1,0:T(8,128)(2,1)}), bf16[1,144,2304]{2,1,0:T(8,128)(2,1)}) %reduce-scatter.7.cloned.1.call-update) | async-done | bytes 663568 | tf_op jit(solution)/shard_map/reduce_scatter | solution.py:1035
  727.7 3.6 norm_bwd.14
  733.8 3.7 norm_bwd.15
  773.7 12.1 %reduce-scatter.11.cloned.1.call-done = bf16[1,144,1536]{2,1,0:T(8,128)(2,1)} async-done(((bf16[8,144,1536]{2,1,0:T(8,128)(2,1)}), bf16[1,144,1536]{2,1,0:T(8,128)(2,1)}) %reduce-scatter.11.cloned.1.call-update) | async-done | bytes 442384 | tf_op jit(solution)/shard_map/reduce_scatter | solution.py:1035
  792.4 4.9 multiply_reduce_fusion.5
  (539 shorter events, 216.4 us)
Async XLA Ops:
  7.2 71.1 %all-gather.5.cloned.1.call-start = ((), (), s32[]{:S(2)}) async-start(), calls=%async_computation.4 | async-start | bytes 2985984 | tf_op jit(solution)/shard_map/all_gather | solution.py:848
  11.4 150.9 %all-gather.7.cloned.1.call-start = ((), (), s32[]{:S(2)}) async-start(), calls=%async_computation.5 | async-start | bytes 5971968 | tf_op jit(solution)/shard_map/all_gather | solution.py:848
  15.3 203.0 %all-gather.9.cloned.1.call-start = ((), (), s32[]{:S(2)}) async-start(), calls=%async_computation.6 | async-start | bytes 2985984 | tf_op jit(solution)/shard_map/all_gather | solution.py:848
  19.0 25.1 %collective-permute-start.1 = (f32[33,576]{1,0:T(8,128)}, f32[33,576]{1,0:T(8,128)}, u32[]{:S(2)}, u32[]{:S(2)}) collective-permute-start(f32[33,576]{1,0:T(8,128)} %concatenate.52), channel_id=1, source_target_pairs={{0,4},{4,0},{8,12},{12,8},{16,20},{20,16},{24,28},{28,24},{1,5},{5... | collective-permute-start | bytes 228104 | tf_op jit(solution)/shard_map/ppermute | solution.py:780
  22.0 35.8 %collective-permute-start.4 = (bf16[2,256,1152]{2,1,0:T(8,128)(2,1)}, bf16[2,256,1152]{2,1,0:T(8,128)(2,1)}, u32[]{:S(2)}, u32[]{:S(2)}) collective-permute-start(bf16[2,256,1152]{2,1,0:T(8,128)(2,1)} %param.29), channel_id=1, source_target_pairs={{0,2},{1,3},{2,0},{3,1},{4,6},{5,7},{6,4},{7,5},{8,10},{9,11},{10,... | collective-permute-start | bytes 3538952 | tf_op jit(solution)/shard_map/ppermute | solution.py:780
  24.8 50.1 %collective-permute-start = (bf16[2,256,1152]{2,1,0:T(8,128)(2,1)}, bf16[2,256,1152]{2,1,0:T(8,128)(2,1)}, u32[]{:S(2)}, u32[]{:S(2)}) collective-permute-start(bf16[2,256,1152]{2,1,0:T(8,128)(2,1)} %multiply_convert_fusion), channel_id=1, source_target_pairs={{0,2},{1,3},{2,0},{3,1},{4,6},{5,7},{6,4},{7,5},{8,10},{9,11},{10,... | collective-permute-start | bytes 3538952 | tf_op jit(solution)/shard_map/ppermute | solution.py:780
  27.3 279.2 %all-gather.11.cloned.1.call-start = ((), (), s32[]{:S(2)}) async-start(), calls=%async_computation.7 | async-start | bytes 5971968 | tf_op jit(solution)/shard_map/all_gather | solution.py:848
  45.0 11.8 %collective-permute-start.2 = (f32[33,576]{1,0:T(8,128)S(1)}, f32[33,576]{1,0:T(8,128)S(1)}, u32[]{:S(2)}, u32[]{:S(2)}) collective-permute-start(f32[33,576]{1,0:T(8,128)S(1)} %pad_add_fusion.1), channel_id=1, source_target_pairs={{0,8},{4,12},{8,0},{12,4},{16,24},{20,28},{24,16},{28,20},{1,9},{5... | collective-permute-start | bytes 228104 | tf_op jit(solution)/shard_map/ppermute | solution.py:780
  56.8 13.5 %collective-permute-start.3 = (f32[33,576]{1,0:T(8,128)S(1)}, f32[33,576]{1,0:T(8,128)S(1)}, u32[]{:S(2)}, u32[]{:S(2)}) collective-permute-start(f32[33,576]{1,0:T(8,128)S(1)} %add.266), channel_id=1, source_target_pairs={{0,16},{4,20},{8,24},{12,28},{16,0},{20,4},{24,8},{28,12},{1,17},{... | collective-permute-start | bytes 228104 | tf_op jit(solution)/shard_map/ppermute | solution.py:780
  63.7 18.6 %collective-permute-start.5 = (bf16[2,256,1152]{2,1,0:T(8,128)(2,1)}, bf16[2,256,1152]{2,1,0:T(8,128)(2,1)}, u32[]{:S(2)}, u32[]{:S(2)}) collective-permute-start(bf16[2,256,1152]{2,1,0:T(8,128)(2,1)} %get-tuple-element.206.refs_2_.refs_1_), channel_id=1, source_target_pairs={{0,1},{1,0},{2,3},{3,2},{4,5},{5,4},{6,7},{7,6},{8,9},{9,8},{10,11... | collective-permute-start | bytes 3538952 | tf_op jit(solution)/shard_map/ppermute | solution.py:780
  101.6 3.3 collective-permute-start.6
  101.7 7.2 collective-permute-start.8
  107.4 28.3 %collective-permute-start.7 = (bf16[2,256,1152]{2,1,0:T(8,128)(2,1)}, bf16[2,256,1152]{2,1,0:T(8,128)(2,1)}, u32[]{:S(2)}, u32[]{:S(2)}) collective-permute-start(bf16[2,256,1152]{2,1,0:T(8,128)(2,1)} %get-tuple-element.211.refs_2_), channel_id=1, source_target_pairs={{0,2},{1,3},{2,0},{3,1},{4,6},{5,7},{6,4},{7,5},{8,10},{9,11},{10,... | collective-permute-start | bytes 3538952 | tf_op jit(solution)/shard_map/ppermute | solution.py:780
  127.7 8.6 %collective-permute-start.9 = (bf16[2,256,1152]{2,1,0:T(8,128)(2,1)}, bf16[2,256,1152]{2,1,0:T(8,128)(2,1)}, u32[]{:S(2)}, u32[]{:S(2)}) collective-permute-start(bf16[2,256,1152]{2,1,0:T(8,128)(2,1)} %get-tuple-element.217), channel_id=1, source_target_pairs={{0,1},{1,0},{2,3},{3,2},{4,5},{5,4},{6,7},{7,6},{8,9},{9,8},{10,11... | collective-permute-start | bytes 3538952 | tf_op jit(solution)/shard_map/ppermute | solution.py:780
  151.2 3.2 collective-permute-start.11
  151.2 28.7 %collective-permute-start.10 = (bf16[2,256,1152]{2,1,0:T(8,128)(2,1)}, bf16[2,256,1152]{2,1,0:T(8,128)(2,1)}, u32[]{:S(2)}, u32[]{:S(2)}) collective-permute-start(bf16[2,256,1152]{2,1,0:T(8,128)(2,1)} %get-tuple-element.218.refs_2_), channel_id=1, source_target_pairs={{0,2},{1,3},{2,0},{3,1},{4,6},{5,7},{6,4},{7,5},{8,10},{9,11},{10,... | collective-permute-start | bytes 3538952 | tf_op jit(solution)/shard_map/ppermute | solution.py:780
  174.2 6.3 collective-permute-start.12
  175.1 387.3 %reduce-scatter.5.cloned.1.call-start = ((), (), s32[]{:S(2)}) async-start(), calls=%async_computation.8 | async-start | bytes 5971968 | tf_op jit(solution)/shard_map/reduce_scatter | solution.py:1035
  185.1 28.7 %collective-permute-start.13 = (bf16[2,256,1152]{2,1,0:T(8,128)(2,1)}, bf16[2,256,1152]{2,1,0:T(8,128)(2,1)}, u32[]{:S(2)}, u32[]{:S(2)}) collective-permute-start(bf16[2,256,1152]{2,1,0:T(8,128)(2,1)} %get-tuple-element.225.refs_2_), channel_id=1, source_target_pairs={{0,2},{1,3},{2,0},{3,1},{4,6},{5,7},{6,4},{7,5},{8,10},{9,11},{10,... | collective-permute-start | bytes 3538952 | tf_op jit(solution)/shard_map/ppermute | solution.py:780
  200.2 22.1 %collective-permute-start.15 = (bf16[2,256,1152]{2,1,0:T(8,128)(2,1)}, bf16[2,256,1152]{2,1,0:T(8,128)(2,1)}, u32[]{:S(2)}, u32[]{:S(2)}) collective-permute-start(bf16[2,256,1152]{2,1,0:T(8,128)(2,1)} %get-tuple-element.232), channel_id=1, source_target_pairs={{0,1},{1,0},{2,3},{3,2},{4,5},{5,4},{6,7},{7,6},{8,9},{9,8},{10,11... | collective-permute-start | bytes 3538952 | tf_op jit(solution)/shard_map/ppermute | solution.py:780
  227.0 28.7 %collective-permute-start.16 = (bf16[2,256,1152]{2,1,0:T(8,128)(2,1)}, bf16[2,256,1152]{2,1,0:T(8,128)(2,1)}, u32[]{:S(2)}, u32[]{:S(2)}) collective-permute-start(bf16[2,256,1152]{2,1,0:T(8,128)(2,1)} %get-tuple-element.233.refs_2_), channel_id=1, source_target_pairs={{0,2},{1,3},{2,0},{3,1},{4,6},{5,7},{6,4},{7,5},{8,10},{9,11},{10,... | collective-permute-start | bytes 3538952 | tf_op jit(solution)/shard_map/ppermute | solution.py:780
  249.1 7.2 collective-permute-start.18
  261.5 28.7 %collective-permute-start.19 = (bf16[2,256,1152]{2,1,0:T(8,128)(2,1)}, bf16[2,256,1152]{2,1,0:T(8,128)(2,1)}, u32[]{:S(2)}, u32[]{:S(2)}) collective-permute-start(bf16[2,256,1152]{2,1,0:T(8,128)(2,1)} %get-tuple-element.241.refs_2_), channel_id=1, source_target_pairs={{0,2},{1,3},{2,0},{3,1},{4,6},{5,7},{6,4},{7,5},{8,10},{9,11},{10,... | collective-permute-start | bytes 3538952 | tf_op jit(solution)/shard_map/ppermute | solution.py:780
  283.9 6.8 collective-permute-start.21
  295.4 11.1 %collective-permute-start.23 = (bf16[2,256,1152]{2,1,0:T(8,128)(2,1)}, bf16[2,256,1152]{2,1,0:T(8,128)(2,1)}, u32[]{:S(2)}, u32[]{:S(2)}) collective-permute-start(bf16[2,256,1152]{2,1,0:T(8,128)(2,1)} %get-tuple-element.250.refs_1_), channel_id=1, source_target_pairs={{0,1},{1,0},{2,3},{3,2},{4,5},{5,4},{6,7},{7,6},{8,9},{9,8},{10,11... | collective-permute-start | bytes 3538952 | tf_op jit(solution)/shard_map/ppermute | solution.py:780
  298.7 19.7 %collective-permute-start.24 = (bf16[2,256,1152]{2,1,0:T(8,128)(2,1)}, bf16[2,256,1152]{2,1,0:T(8,128)(2,1)}, u32[]{:S(2)}, u32[]{:S(2)}) collective-permute-start(bf16[2,256,1152]{2,1,0:T(8,128)(2,1)} %get-tuple-element.515.refs_1_.refs_3_), channel_id=1, source_target_pairs={{0,1},{1,0},{2,3},{3,2},{4,5},{5,4},{6,7},{7,6},{8,9},{9,8},{10,11... | collective-permute-start | bytes 3538952 | tf_op jit(solution)/shard_map/ppermute | solution.py:780
  299.2 32.6 %collective-permute-start.22 = (bf16[2,256,1152]{2,1,0:T(8,128)(2,1)}, bf16[2,256,1152]{2,1,0:T(8,128)(2,1)}, u32[]{:S(2)}, u32[]{:S(2)}) collective-permute-start(bf16[2,256,1152]{2,1,0:T(8,128)(2,1)} %get-tuple-element.248.refs_2_), channel_id=1, source_target_pairs={{0,2},{1,3},{2,0},{3,1},{4,6},{5,7},{6,4},{7,5},{8,10},{9,11},{10,... | collective-permute-start | bytes 3538952 | tf_op jit(solution)/shard_map/ppermute | solution.py:780
  331.4 4.9 collective-permute-start.26
  345.1 14.9 %collective-permute-start.29 = (bf16[2,256,1152]{2,1,0:T(8,128)(2,1)}, bf16[2,256,1152]{2,1,0:T(8,128)(2,1)}, u32[]{:S(2)}, u32[]{:S(2)}) collective-permute-start(bf16[2,256,1152]{2,1,0:T(8,128)(2,1)} %get-tuple-element.514.refs_1_.refs_4_.refs_3_), channel_id=1, source_target_pairs={{0,1},{1,0},{2,3},{3,2},{4,5},{5,4},{6,7},{7,6},{8,9},{9,8},{10,11... | collective-permute-start | bytes 3538952 | tf_op jit(solution)/shard_map/ppermute | solution.py:780
  345.5 41.0 %collective-permute-start.27 = (bf16[3,256,1152]{2,1,0:T(8,128)(2,1)}, bf16[3,256,1152]{2,1,0:T(8,128)(2,1)}, u32[]{:S(2)}, u32[]{:S(2)}) collective-permute-start(bf16[3,256,1152]{2,1,0:T(8,128)(2,1)} %get-tuple-element.258.refs_1_), channel_id=1, source_target_pairs={{0,2},{1,3},{2,0},{3,1},{4,6},{5,7},{6,4},{7,5},{8,10},{9,11},{10,... | collective-permute-start | bytes 5308424 | tf_op jit(solution)/shard_map/ppermute | solution.py:780
  373.0 14.1 %collective-permute-start.30 = (bf16[2,256,1152]{2,1,0:T(8,128)(2,1)}, bf16[2,256,1152]{2,1,0:T(8,128)(2,1)}, u32[]{:S(2)}, u32[]{:S(2)}) collective-permute-start(bf16[2,256,1152]{2,1,0:T(8,128)(2,1)} %get-tuple-element.270), channel_id=1, source_target_pairs={{0,1},{1,0},{2,3},{3,2},{4,5},{5,4},{6,7},{7,6},{8,9},{9,8},{10,11... | collective-permute-start | bytes 3538952 | tf_op jit(solution)/shard_map/ppermute | solution.py:780
  373.1 13.9 %collective-permute-start.31 = (bf16[2,256,1152]{2,1,0:T(8,128)(2,1)}, bf16[2,256,1152]{2,1,0:T(8,128)(2,1)}, u32[]{:S(2)}, u32[]{:S(2)}) collective-permute-start(bf16[2,256,1152]{2,1,0:T(8,128)(2,1)} %get-tuple-element.272), channel_id=1, source_target_pairs={{0,1},{1,0},{2,3},{3,2},{4,5},{5,4},{6,7},{7,6},{8,9},{9,8},{10,11... | collective-permute-start | bytes 3538952 | tf_op jit(solution)/shard_map/ppermute | solution.py:780
  408.1 236.9 %reduce-scatter.9.cloned.1.call-start = ((), (), s32[]{:S(2)}) async-start(), calls=%async_computation.10 | async-start | bytes 3981312 | tf_op jit(solution)/shard_map/reduce_scatter | solution.py:1035
  409.3 41.3 %collective-permute-start.32 = (bf16[3,256,1152]{2,1,0:T(8,128)(2,1)}, bf16[3,256,1152]{2,1,0:T(8,128)(2,1)}, u32[]{:S(2)}, u32[]{:S(2)}) collective-permute-start(bf16[3,256,1152]{2,1,0:T(8,128)(2,1)} %get-tuple-element.273.refs_1_), channel_id=1, source_target_pairs={{0,2},{1,3},{2,0},{3,1},{4,6},{5,7},{6,4},{7,5},{8,10},{9,11},{10,... | collective-permute-start | bytes 5308424 | tf_op jit(solution)/shard_map/ppermute | solution.py:780
  439.1 12.2 %collective-permute-start.34 = (bf16[2,256,1152]{2,1,0:T(8,128)(2,1)}, bf16[2,256,1152]{2,1,0:T(8,128)(2,1)}, u32[]{:S(2)}, u32[]{:S(2)}) collective-permute-start(bf16[2,256,1152]{2,1,0:T(8,128)(2,1)} %get-tuple-element.287), channel_id=1, source_target_pairs={{0,1},{1,0},{2,3},{3,2},{4,5},{5,4},{6,7},{7,6},{8,9},{9,8},{10,11... | collective-permute-start | bytes 3538952 | tf_op jit(solution)/shard_map/ppermute | solution.py:780
  457.3 3.2 collective-permute-start.36
  457.3 35.8 %collective-permute-start.35 = (bf16[2,256,1152]{2,1,0:T(8,128)(2,1)}, bf16[2,256,1152]{2,1,0:T(8,128)(2,1)}, u32[]{:S(2)}, u32[]{:S(2)}) collective-permute-start(bf16[2,256,1152]{2,1,0:T(8,128)(2,1)} %get-tuple-element.288.refs_1_), channel_id=1, source_target_pairs={{0,2},{1,3},{2,0},{3,1},{4,6},{5,7},{6,4},{7,5},{8,10},{9,11},{10,... | collective-permute-start | bytes 3538952 | tf_op jit(solution)/shard_map/ppermute | solution.py:780
  486.7 7.1 collective-permute-start.37
  509.4 191.8 %reduce-scatter.7.cloned.1.call-start = ((), (), s32[]{:S(2)}) async-start(), calls=%async_computation.9 | async-start | bytes 5971968 | tf_op jit(solution)/shard_map/reduce_scatter | solution.py:1035
  511.1 28.3 %collective-permute-start.38 = (bf16[2,256,1152]{2,1,0:T(8,128)(2,1)}, bf16[2,256,1152]{2,1,0:T(8,128)(2,1)}, u32[]{:S(2)}, u32[]{:S(2)}) collective-permute-start(bf16[2,256,1152]{2,1,0:T(8,128)(2,1)} %get-tuple-element.297.refs_1_), channel_id=1, source_target_pairs={{0,2},{1,3},{2,0},{3,1},{4,6},{5,7},{6,4},{7,5},{8,10},{9,11},{10,... | collective-permute-start | bytes 3538952 | tf_op jit(solution)/shard_map/ppermute | solution.py:780
  527.7 12.2 %collective-permute-start.40 = (bf16[2,256,1152]{2,1,0:T(8,128)(2,1)}, bf16[2,256,1152]{2,1,0:T(8,128)(2,1)}, u32[]{:S(2)}, u32[]{:S(2)}) collective-permute-start(bf16[2,256,1152]{2,1,0:T(8,128)(2,1)} %get-tuple-element.307), channel_id=1, source_target_pairs={{0,1},{1,0},{2,3},{3,2},{4,5},{5,4},{6,7},{7,6},{8,9},{9,8},{10,11... | collective-permute-start | bytes 3538952 | tf_op jit(solution)/shard_map/ppermute | solution.py:780
  545.9 3.2 collective-permute-start.42
  546.0 28.7 %collective-permute-start.41 = (bf16[2,256,1152]{2,1,0:T(8,128)(2,1)}, bf16[2,256,1152]{2,1,0:T(8,128)(2,1)}, u32[]{:S(2)}, u32[]{:S(2)}) collective-permute-start(bf16[2,256,1152]{2,1,0:T(8,128)(2,1)} %get-tuple-element.308.refs_1_), channel_id=1, source_target_pairs={{0,2},{1,3},{2,0},{3,1},{4,6},{5,7},{6,4},{7,5},{8,10},{9,11},{10,... | collective-permute-start | bytes 3538952 | tf_op jit(solution)/shard_map/ppermute | solution.py:780
  562.3 13.0 %collective-permute-start.43 = (bf16[2,256,1152]{2,1,0:T(8,128)(2,1)}, bf16[2,256,1152]{2,1,0:T(8,128)(2,1)}, u32[]{:S(2)}, u32[]{:S(2)}) collective-permute-start(bf16[2,256,1152]{2,1,0:T(8,128)(2,1)} %get-tuple-element.318), channel_id=1, source_target_pairs={{0,1},{1,0},{2,3},{3,2},{4,5},{5,4},{6,7},{7,6},{8,9},{9,8},{10,11... | collective-permute-start | bytes 3538952 | tf_op jit(solution)/shard_map/ppermute | solution.py:780
  593.0 192.7 %reduce-scatter.11.cloned.1.call-start = ((), (), s32[]{:S(2)}) async-start(), calls=%async_computation.11 | async-start | bytes 3981312 | tf_op jit(solution)/shard_map/reduce_scatter | solution.py:1035
  594.3 33.4 %collective-permute-start.44 = (bf16[2,256,1152]{2,1,0:T(8,128)(2,1)}, bf16[2,256,1152]{2,1,0:T(8,128)(2,1)}, u32[]{:S(2)}, u32[]{:S(2)}) collective-permute-start(bf16[2,256,1152]{2,1,0:T(8,128)(2,1)} %get-tuple-element.319.refs_1_), channel_id=1, source_target_pairs={{0,2},{1,3},{2,0},{3,1},{4,6},{5,7},{6,4},{7,5},{8,10},{9,11},{10,... | collective-permute-start | bytes 3538952 | tf_op jit(solution)/shard_map/ppermute | solution.py:780
  624.1 4.3 collective-permute-start.46
  634.4 4.3 collective-permute-start.48
  637.2 74.9 %collective-permute-start.47 = (bf16[1,256,1152]{2,1,0:T(8,128)(2,1)}, bf16[1,256,1152]{2,1,0:T(8,128)(2,1)}, u32[]{:S(2)}, u32[]{:S(2)}) collective-permute-start(bf16[1,256,1152]{2,1,0:T(8,128)(2,1)} %slice.288), channel_id=1, source_target_pairs={{0,2},{1,3},{2,0},{3,1},{4,6},{5,7},{6,4},{7,5},{8,10},{9,11},{10,... | collective-permute-start | bytes 1769480 | tf_op jit(solution)/shard_map/ppermute | solution.py:780
  672.0 40.7 %collective-permute-start.49 = (bf16[2,256,1152]{2,1,0:T(8,128)(2,1)}, bf16[2,256,1152]{2,1,0:T(8,128)(2,1)}, u32[]{:S(2)}, u32[]{:S(2)}) collective-permute-start(bf16[2,256,1152]{2,1,0:T(8,128)(2,1)} %get-tuple-element.347), channel_id=1, source_target_pairs={{0,1},{1,0},{2,3},{3,2},{4,5},{5,4},{6,7},{7,6},{8,9},{9,8},{10,11... | collective-permute-start | bytes 3538952 | tf_op jit(solution)/shard_map/ppermute | solution.py:780
  710.7 8.2 collective-permute-start.61
  717.5 14.9 %collective-permute-start.50 = (bf16[1,256,1152]{2,1,0:T(8,128)(2,1)}, bf16[1,256,1152]{2,1,0:T(8,128)(2,1)S(1)}, u32[]{:S(2)}, u32[]{:S(2)}) collective-permute-start(bf16[1,256,1152]{2,1,0:T(8,128)(2,1)} %slice.289), channel_id=1, source_target_pairs={{0,2},{1,3},{2,0},{3,1},{4,6},{5,7},{6,4},{7,5},{8,10},{9,11},{10,... | collective-permute-start | bytes 1769480 | tf_op jit(solution)/shard_map/ppermute | solution.py:780
  718.9 3.8 collective-permute-start.62
  722.8 4.9 collective-permute-start.63
  727.7 3.7 collective-permute-start.64
  731.4 12.1 %collective-permute-start.65 = (f32[8,128]{1,0:T(8,128)S(1)}, f32[8,128]{1,0:T(8,128)S(1)}, u32[]{:S(2)}, u32[]{:S(2)}) collective-permute-start(f32[8,128]{1,0:T(8,128)S(1)} %add.332), channel_id=1, source_target_pairs={{0,2},{1,3},{2,0},{3,1},{4,6},{5,7},{6,4},{7,5},{8,10},{9,11},{10,... | collective-permute-start | bytes 12296 | tf_op jit(solution)/shard_map/ppermute | solution.py:780
  738.9 7.7 collective-permute-start.51
  747.4 8.8 %collective-permute-start.52 = (f32[224,128]{1,0:T(8,128)S(1)}, f32[224,128]{1,0:T(8,128)S(1)}, u32[]{:S(2)}, u32[]{:S(2)}) collective-permute-start(f32[224,128]{1,0:T(8,128)S(1)} %fusion.45), channel_id=1, source_target_pairs={{0,8},{4,12},{8,0},{12,4},{16,24},{20,28},{24,16},{28,20},{1,9},{5... | collective-permute-start | bytes 344072 | tf_op jit(solution)/shard_map/ppermute | solution.py:780
  757.2 7.0 collective-permute-start.53
  767.5 4.9 collective-permute-start.55
  798.9 3.6 collective-permute-start.56
  802.6 3.6 collective-permute-start.57
  806.2 4.5 collective-permute-start.58
  811.9 3.6 collective-permute-start.60
  (87 other events, 571.1 us)
Sparse Core Ops, SparseCore 0:
  11.5 62.3 all-gather.4
  76.6 85.5 all-gather.6
  165.0 53.1 all-gather.8
  220.9 85.6 all-gather.10
  408.2 102.3 reduce-scatter.4
  514.5 78.9 reduce-scatter.8
  597.4 103.7 reduce-scatter.6
  704.8 80.8 reduce-scatter.10

commit v2 on v1

--- a/solution.py
+++ b/solution.py
@@ -287,37 +287,30 @@
     keys_turned = qkv_ref[0, 1].T
     values = qkv_ref[0, 2]
 
-    grad_vals[...] = jnp.zeros_like(grad_vals)
-    grad_keys[...] = jnp.zeros_like(grad_keys)
     lane = lanes_of((rows, LANE))
-
-    def back(pair, carry):
-        val_part = None
-        for half in range(2):
-            where = pl.ds(pl.multiple_of((2 * pair + half) * rows, rows), rows)
-            queries = jnp.concatenate([qkv_ref[0, 0, where, :], qpos_ref[where, :]], axis=1)
-            grad_out = dmix[where, head_lanes]
-            delta = jnp.sum(
-                grad_out.astype(f32) * mix_ref[where, :].astype(f32), axis=1, keepdims=True
-            )
-            hi, mid, low = split_three(-delta)
-            shifted = jnp.where(lane == HEAD, hi, grad_out)
-            shifted = jnp.where(lane == HEAD + 1, mid, shifted)
-            shifted = jnp.where(lane == HEAD + 2, low, shifted)
-            probs = jnp.exp2(dot_nt(keyset, queries) * EXP_SCALE).astype(bf16)
-            grad_scores = probs * dot_nt(values, shifted).astype(bf16)
-            val_add = dot_nn(probs, grad_out)
-            key_add = dot_nn(grad_scores, queries)
-            grad_queries[:, where] = dot_nn(keys_turned, grad_scores)
-            if val_part is None:
-                val_part, key_part = val_add, key_add
-            else:
-                val_part, key_part = val_part + val_add, key_part + key_add
-        grad_vals[...] += val_part
-        grad_keys[...] += key_part
-        return carry
-
-    lax.fori_loop(0, CHUNKS // 2, back, 0)
+    val_part = None
+    for start in range(0, seq, rows):
+        where = pl.ds(start, rows)
+        queries = jnp.concatenate([qkv_ref[0, 0, where, :], qpos_ref[where, :]], axis=1)
+        grad_out = dmix[where, head_lanes]
+        delta = jnp.sum(
+            grad_out.astype(f32) * mix_ref[where, :].astype(f32), axis=1, keepdims=True
+        )
+        hi, mid, low = split_three(-delta)
+        shifted = jnp.where(lane == HEAD, hi, grad_out)
+        shifted = jnp.where(lane == HEAD + 1, mid, shifted)
+        shifted = jnp.where(lane == HEAD + 2, low, shifted)
+        probs = jnp.exp2(dot_nt(keyset, queries) * EXP_SCALE).astype(bf16)
+        grad_scores = probs * dot_nt(values, shifted).astype(bf16)
+        val_add = dot_nn(probs, grad_out)
+        key_add = dot_nn(grad_scores, queries)
+        grad_queries[:, where] = dot_nn(keys_turned, grad_scores)
+        if val_part is None:
+            val_part, key_part = val_add, key_add
+        else:
+            val_part, key_part = val_part + val_add, key_part + key_add
+    grad_vals[...] = val_part
+    grad_keys[...] = key_part
 
     extra = grad_keys[:, LANE:].reshape(grid_side, grid_side, LANE)
     rel_ref[0, 0] = jnp.sum(extra, axis=1)
@@ -391,7 +384,8 @@
 
 
 def column_chunks(hidden):
-    return [pl.ds(start, min(512, hidden - start)) for start in range(0, hidden, 512)]
+    first = (hidden // 2 + LANE - 1) // LANE * LANE
+    return [pl.ds(0, first), pl.ds(first, hidden - first)]
 
 
 def mlp_body(own_ref, near_ref, up_ref, down_ref, pre_ref, act_ref, keep_ref, send_ref):
@@ -734,8 +728,8 @@
     own0, near0, right0, own1, near1, right1 = refs[:6]
     out_ref, total = refs[-2], refs[-1]
     step = pl.program_id(0)
-    part = dot_nn(row_half(own0, near0, 0).T, right0[...])
-    part = part + dot_nn(row_half(own1, near1, 0).T, right1[...])
+    left = jnp.concatenate([own0[0], near0[0], own1[0], near1[0]], axis=0)
+    part = dot_nn(left.T, jnp.concatenate([right0[...], right1[...]], axis=0))
 
     @pl.when(step == 0)
     def _():

time: 846 us -> 846 us (level)
  waiting for transfers between devices: 154 us -> 178 us
  Pallas kernels: 481 us -> 458 us
    pallas_call x63, Pallas kernels: 481 us -> 458 us  [call(): pl.pallas_call(wrapped, grid=grid, in_specs=[pl.BlockSpec(memory_space=pl...]
    all_gather x4, waiting for transfers between devices: 17.7 us -> 30.4 us  [fetch_together(): lax.all_gather(jnp.concatenate(parts, axis=1), 'group', axis=0, tiled=True)]
    reduce_scatter x4, waiting for transfers between devices: 25.6 us -> 37.9 us  [scatter(): lax.psum_scatter(whole.reshape(groups, shard_rows, whole.shape[1]), 'grou...]
  transfers between devices with their start and end apart: 74 -> 74, of which waited for: 40 -> 40; matrix products, arithmetic and copies ran while one was open for 10% -> 10% of each run, Pallas kernels for 54% -> 51%
where the time goes in v2:
time: 846 us; the launch traced here: 837 us
  Pallas kernels  458 us (54%)
  waiting for transfers between devices  178 us (21%)
  other arithmetic  73.8 us (9%)
  local copies, waits for them, and re-layouts  52.4 us (6%)
  starting transfers between devices  52.4 us (6%)
  between operations  17.9 us (2%)
    pallas_call x63, Pallas kernels, call(): pl.pallas_call(wrapped, grid=grid, in_specs=[pl.BlockSpec(memory_space=pl...  458 us
    ppermute x66, waiting for transfers between devices, swap(): lax.ppermute(value, axis, [(index, index ^ bit) for index in range(size)])  110 us
    ppermute x66, starting transfers between devices, swap(): lax.ppermute(value, axis, [(index, index ^ bit) for index in range(size)])  52 us
    reduce_scatter x4, waiting for transfers between devices, scatter(): lax.psum_scatter(whole.reshape(groups, shard_rows, whole.shape[1]), 'grou...  37.9 us
    all_gather x4, waiting for transfers between devices, fetch_together(): lax.all_gather(jnp.concatenate(parts, axis=1), 'group', axis=0, tiled=True)  30.4 us
    unnamed x154, local copies, waits for them, and re-layouts  21.9 us
  transfers between devices with their start and end apart: 74, of which 40 were waited for; matrix products, arithmetic and copies ran while one was open for 10% of the time, Pallas kernels for 51%

profile of v2, /device:TPU:0, one launch (start us, length us, event | category | flops | bytes accessed | tf_op | source)
XLA Modules:
  0.0 837.0 jit_solution(7041397865221542851)
XLA Ops:
  19.0 3.0 collective-permute-start.1
  38.3 4.1 pad_maximum_fusion.2.refs_1_
  47.6 9.2 %collective-permute-done.2 = f32[33,576]{1,0:T(8,128)S(1)} collective-permute-done((f32[33,576]{1,0:T(8,128)S(1)}, f32[33,576]{1,0:T(8,128)S(1)}, u32[]{:S(2)}, u32[]{:S(2)}) %collective-permute-start.2) | collective-permute-done | bytes 76064 | tf_op jit(solution)/shard_map/ppermute | solution.py:774
  57.7 2.9 fusion.11
  60.6 3.3 norm_fwd.8
  63.9 4.6 fusion.16
  71.9 2.8 norm_fwd.9
  75.0 3.3 pad_maximum_fusion.1.refs_0_
  78.3 4.0 unpack_out.2
  82.4 19.2 %attend_fwd.4 = (bf16[4,3,1024,128]{3,2,1,0:T(8,128)(2,1)}, bf16[1024,512]{1,0:T(8,128)(2,1)}, bf16[2,256,1152]{2,1,0:T(8,128)(2,1)}, bf16[2,256,1152]{2,1,0:T(8,128)(2,1)}, f32[8,128]{1,0:T(8,128)}) custom-call(bf16[2,2,256,1152]{3,2,1,0:T(8,128)(2,1)} %pad_maximum_fusion.1.refs_0_, f32[8,128]{1,0:T(8,128)} %get-tuple-element.205.refs_1_, ...), custom_call_target="tpu_custom_call" | custom-call | flops 6000000 | bytes 1000 | tf_op jit(solution)/shard_map/attend_fwd/pallas_call | solution.py:114
  108.9 18.8 %attend_fwd.5 = (bf16[4,3,1024,128]{3,2,1,0:T(8,128)(2,1)}, bf16[1024,512]{1,0:T(8,128)(2,1)}, bf16[2,256,1152]{2,1,0:T(8,128)(2,1)}, bf16[2,256,1152]{2,1,0:T(8,128)(2,1)}, f32[8,128]{1,0:T(8,128)}) custom-call(f32[8,128]{1,0:T(8,128)} %get-tuple-element.212.refs_0_, bf16[2,256,1152]{2,1,0:T(8,128)(2,1)} %get-tuple-element.213.refs_1_.refs_4_, ...), custom_call_target="tpu_custom_call" | custom-call | flops 6000000 | bytes 1000 | tf_op jit(solution)/shard_map/attend_fwd/pallas_call | solution.py:114
  127.8 8.0 collective-permute-done.7.refs_0_.refs_3_
  136.3 4.8 norm_fwd.10
  144.4 17.9 %all-gather.7.cloned.1.call-done.refs_3_.refs_4_.refs_5_ = bf16[1152,2304]{1,0:T(8,128)(2,1)} async-done(((bf16[144,2304]{1,0:T(8,128)(2,1)}), bf16[1152,2304]{1,0:T(8,128)(2,1)}) %all-gather.7.cloned.1.call-update) | async-done | bytes 5308432 | tf_op jit(solution)/shard_map/all_gather | solution.py:842
  162.3 12.3 %mlp_fwd.4 = (bf16[1024,1152]{1,0:T(8,128)(2,1)}, bf16[1024,1152]{1,0:T(8,128)(2,1)}, bf16[2,256,1152]{2,1,0:T(8,128)(2,1)}, bf16[2,256,1152]{2,1,0:T(8,128)(2,1)}, f32[8,128]{1,0:T(8,128)}) custom-call(f32[8,128]{1,0:T(8,128)} %get-tuple-element.219.refs_0_, bf16[2,256,1152]{2,1,0:T(8,128)(2,1)} %get-tuple-element.220.refs_1_.refs_2_, ...), custom_call_target="tpu_custom_call" | custom-call | flops 6000000 | bytes 1000 | tf_op jit(solution)/shard_map/mlp_fwd/pallas_call | solution.py:114
  177.7 4.7 norm_fwd.11
  185.6 12.2 %mlp_fwd.5 = (bf16[1024,1152]{1,0:T(8,128)(2,1)}, bf16[1024,1152]{1,0:T(8,128)(2,1)}, bf16[2,256,1152]{2,1,0:T(8,128)(2,1)}, bf16[2,256,1152]{2,1,0:T(8,128)(2,1)}, f32[8,128]{1,0:T(8,128)}) custom-call(f32[8,128]{1,0:T(8,128)} %get-tuple-element.226.refs_0_, bf16[2,256,1152]{2,1,0:T(8,128)(2,1)} %get-tuple-element.227.refs_1_.refs_5_, ...), custom_call_target="tpu_custom_call" | custom-call | flops 6000000 | bytes 1000 | tf_op jit(solution)/shard_map/mlp_fwd/pallas_call | solution.py:114
  198.0 13.1 %collective-permute-done.13.refs_0_.refs_3_ = bf16[2,256,1152]{2,1,0:T(8,128)(2,1)} collective-permute-done((bf16[2,256,1152]{2,1,0:T(8,128)(2,1)}, bf16[2,256,1152]{2,1,0:T(8,128)(2,1)}, u32[]{:S(2)}, u32[]{:S(2)}) %collective-permute-start.13) | collective-permute-done | bytes 1179680 | tf_op jit(solution)/shard_map/ppermute | solution.py:774
  211.7 6.5 all-gather.9.cloned.1.call-done.refs_1_.refs_3_.refs_8_
  218.2 4.0 unpack_out.3
  222.3 4.7 norm_fwd.12
  230.2 18.9 %attend_fwd.6 = (bf16[4,3,1024,128]{3,2,1,0:T(8,128)(2,1)}, bf16[1024,512]{1,0:T(8,128)(2,1)}, bf16[2,256,1152]{2,1,0:T(8,128)(2,1)}, bf16[2,256,1152]{2,1,0:T(8,128)(2,1)}, f32[8,128]{1,0:T(8,128)}) custom-call(f32[8,128]{1,0:T(8,128)} %get-tuple-element.234.refs_0_, bf16[2,256,1152]{2,1,0:T(8,128)(2,1)} %get-tuple-element.235.refs_1_, ...), custom_call_target="tpu_custom_call" | custom-call | flops 6000000 | bytes 1000 | tf_op jit(solution)/shard_map/attend_fwd/pallas_call | solution.py:114
  249.3 6.4 collective-permute-done.16.refs_0_.refs_3_
  256.3 5.2 norm_fwd.13
  264.7 19.3 %attend_fwd.7 = (bf16[4,3,1024,128]{3,2,1,0:T(8,128)(2,1)}, bf16[1024,512]{1,0:T(8,128)(2,1)}, bf16[2,256,1152]{2,1,0:T(8,128)(2,1)}, bf16[2,256,1152]{2,1,0:T(8,128)(2,1)}, f32[8,128]{1,0:T(8,128)}) custom-call(f32[8,128]{1,0:T(8,128)} %get-tuple-element.242.refs_0_, bf16[2,256,1152]{2,1,0:T(8,128)(2,1)} %get-tuple-element.243.refs_1_.refs_4_, ...), custom_call_target="tpu_custom_call" | custom-call | flops 6000000 | bytes 1000 | tf_op jit(solution)/shard_map/attend_fwd/pallas_call | solution.py:114
  284.1 6.1 collective-permute-done.19.refs_0_.refs_3_
  290.8 4.6 norm_fwd.14
  295.4 3.3 fusion.10
  300.6 6.0 all-gather.11.cloned.1.call-done.refs_3_.refs_4_.refs_5_
  306.5 12.3 %mlp_fwd.6 = (bf16[1024,1152]{1,0:T(8,128)(2,1)}, bf16[1024,1152]{1,0:T(8,128)(2,1)}, bf16[2,256,1152]{2,1,0:T(8,128)(2,1)}, bf16[2,256,1152]{2,1,0:T(8,128)(2,1)}, f32[8,128]{1,0:T(8,128)}) custom-call(f32[8,128]{1,0:T(8,128)} %get-tuple-element.249.refs_0_, bf16[2,256,1152]{2,1,0:T(8,128)(2,1)} %get-tuple-element.250.refs_1_, ...), custom_call_target="tpu_custom_call" | custom-call | flops 6000000 | bytes 1000 | tf_op jit(solution)/shard_map/mlp_fwd/pallas_call | solution.py:114
  318.8 13.5 %mlp_bwd.4 = (bf16[1024,1152]{1,0:T(8,128)(2,1)}, bf16[2,256,1152]{2,1,0:T(8,128)(2,1)}, bf16[2,256,1152]{2,1,0:T(8,128)(2,1)}, f32[8,128]{1,0:T(8,128)}) custom-call(f32[8,128]{1,0:T(8,128)} %get-tuple-element.251.refs_0_, bf16[2,256,1152]{2,1,0:T(8,128)(2,1)} %get-tuple-element.515.refs_1_.refs_3_, bf16[2,256,1152]{2,1,0:T(8,128)(2,1)} %collective-permute-done.24.refs_2_, ...), custom_call_target="tpu_custom_call" | custom-call | flops 6000000 | bytes 1000 | tf_op jit(solution)/shard_map/mlp_bwd/pallas_call | solution.py:114
  337.3 5.0 add_both.2
  342.3 3.6 norm_fwd.15
  349.0 12.2 %mlp_fwd.7 = (bf16[1024,1152]{1,0:T(8,128)(2,1)}, bf16[1024,1152]{1,0:T(8,128)(2,1)}, bf16[2,256,1152]{2,1,0:T(8,128)(2,1)}, bf16[2,256,1152]{2,1,0:T(8,128)(2,1)}, f32[8,128]{1,0:T(8,128)}) custom-call(f32[8,128]{1,0:T(8,128)} %get-tuple-element.261.refs_0_, bf16[2,256,1152]{2,1,0:T(8,128)(2,1)} %get-tuple-element.262.refs_1_.refs_4_, ...), custom_call_target="tpu_custom_call" | custom-call | flops 6000000 | bytes 1000 | tf_op jit(solution)/shard_map/mlp_fwd/pallas_call | solution.py:114
  361.3 13.4 %mlp_bwd.5 = (bf16[1024,1152]{1,0:T(8,128)(2,1)}, bf16[2,256,1152]{2,1,0:T(8,128)(2,1)}, bf16[2,256,1152]{2,1,0:T(8,128)(2,1)}, f32[8,128]{1,0:T(8,128)}) custom-call(f32[8,128]{1,0:T(8,128)} %get-tuple-element.263.refs_0_, bf16[2,256,1152]{2,1,0:T(8,128)(2,1)} %get-tuple-element.514.refs_1_.refs_4_.refs_3_, ...), custom_call_target="tpu_custom_call" | custom-call | flops 6000000 | bytes 1000 | tf_op jit(solution)/shard_map/mlp_bwd/pallas_call | solution.py:114
  375.7 11.3 %weight_grad.8 = (bf16[1152,2304]{1,0:T(8,128)(2,1)}, f32[8,128]{1,0:T(8,128)}) custom-call(f32[8,128]{1,0:T(8,128)} %get-tuple-element.265.refs_0_, bf16[2,256,1152]{2,1,0:T(8,128)(2,1)} %get-tuple-element.250.refs_1_, bf16[2,256,1152]{2,1,0:T(8,128)(2,1)} %collective-permute-done.23.refs_2_, bf16[1024,1152]{1,0:T(8,128)(2,1)} %get-tuple-element.266.refs_3_, ...), custom_call_target="tpu_custom_call" | custom-call | flops 6000000 | bytes 1000 | tf_op jit(solution)/shard_map/weight_grad/pallas_call | solution.py:114
  387.9 5.4 add_both.3
  393.3 4.5 norm_bwd.8
  397.8 11.3 %weight_grad.9 = (bf16[1152,2304]{1,0:T(8,128)(2,1)}, f32[8,128]{1,0:T(8,128)}) custom-call(f32[8,128]{1,0:T(8,128)} %get-tuple-element.276.refs_0_, bf16[2,256,1152]{2,1,0:T(8,128)(2,1)} %get-tuple-element.515.refs_1_.refs_3_, bf16[2,256,1152]{2,1,0:T(8,128)(2,1)} %collective-permute-done.24.refs_2_, ...), custom_call_target="tpu_custom_call", output_to_operand_aliasing={{0}: (7, {})} | custom-call | flops 6000000 | bytes 1000 | tf_op jit(solution)/shard_map/weight_grad/pallas_call | solution.py:114
  414.3 22.0 %attend_bwd.4 = (bf16[1024,1024]{1,0:T(8,128)(2,1)}, f32[4,1,256]{2,1,0:T(1,128)}, f32[4,2,32,128]{3,2,1,0:T(8,128)}, bf16[2,256,1152]{2,1,0:T(8,128)(2,1)}, bf1...) custom-call(f32[8,128]{1,0:T(8,128)} %get-tuple-element.280.refs_0_, ...), custom_call_target="tpu_custom_call" | custom-call | flops 6000000 | bytes 1000 | tf_op jit(solution)/shard_map/attend_bwd/pallas_call | solution.py:114
  436.6 15.2 %collective-permute-done.32.refs_0_.refs_2_.refs_3_ = bf16[3,256,1152]{2,1,0:T(8,128)(2,1)} collective-permute-done((bf16[3,256,1152]{2,1,0:T(8,128)(2,1)}, bf16[3,256,1152]{2,1,0:T(8,128)(2,1)}, u32[]{:S(2)}, u32[]{:S(2)}) %collective-permute-start.32) | collective-permute-done | bytes 1769504 | tf_op jit(solution)/shard_map/ppermute | solution.py:774
  452.3 6.0 norm_bwd.9
  461.6 22.0 %attend_bwd.5 = (bf16[1024,1024]{1,0:T(8,128)(2,1)}, f32[4,1,256]{2,1,0:T(1,128)}, f32[4,2,32,128]{3,2,1,0:T(8,128)}, bf16[2,256,1152]{2,1,0:T(8,128)(2,1)}, bf1...) custom-call(f32[8,128]{1,0:T(8,128)} %get-tuple-element.289.refs_0_, ...), custom_call_target="tpu_custom_call" | custom-call | flops 6000000 | bytes 1000 | tf_op jit(solution)/shard_map/attend_bwd/pallas_call | solution.py:114
  483.8 6.3 weight_grad.10
  490.6 5.9 norm_bwd.10
  496.5 9.7 %weight_grad.11 = (bf16[1152,1536]{1,0:T(8,128)(2,1)}, f32[8,128]{1,0:T(8,128)}) custom-call(f32[8,128]{1,0:T(8,128)} %get-tuple-element.298.refs_0_, bf16[2,256,1152]{2,1,0:T(8,128)(2,1)} %get-tuple-element.235.refs_1_, bf16[2,256,1152]{2,1,0:T(8,128)(2,1)} %collective-permute-done.17.refs_2_, ...), custom_call_target="tpu_custom_call", output_to_operand_aliasing={{0}: (7, {})} | custom-call | flops 6000000 | bytes 1000 | tf_op jit(solution)/shard_map/weight_grad/pallas_call | solution.py:114
  511.4 13.6 %mlp_bwd.6 = (bf16[1024,1152]{1,0:T(8,128)(2,1)}, bf16[2,256,1152]{2,1,0:T(8,128)(2,1)}, bf16[2,256,1152]{2,1,0:T(8,128)(2,1)}, f32[8,128]{1,0:T(8,128)}) custom-call(f32[8,128]{1,0:T(8,128)} %get-tuple-element.302.refs_0_, bf16[2,256,1152]{2,1,0:T(8,128)(2,1)} %get-tuple-element.303.refs_1_.refs_3_, bf16[2,256,1152]{2,1,0:T(8,128)(2,1)} %copy-done.21, ...), custom_call_target="tpu_custom_call" | custom-call | flops 6000000 | bytes 1000 | tf_op jit(solution)/shard_map/mlp_bwd/pallas_call | solution.py:114
  525.4 10.8 %collective-permute-done.38.refs_0_.refs_2_ = bf16[2,256,1152]{2,1,0:T(8,128)(2,1)} collective-permute-done((bf16[2,256,1152]{2,1,0:T(8,128)(2,1)}, bf16[2,256,1152]{2,1,0:T(8,128)(2,1)}, u32[]{:S(2)}, u32[]{:S(2)}) %collective-permute-start.38) | collective-permute-done | bytes 1179680 | tf_op jit(solution)/shard_map/ppermute | solution.py:774
  536.8 6.1 norm_bwd.11
  546.1 13.4 %mlp_bwd.7 = (bf16[1024,1152]{1,0:T(8,128)(2,1)}, bf16[2,256,1152]{2,1,0:T(8,128)(2,1)}, bf16[2,256,1152]{2,1,0:T(8,128)(2,1)}, f32[8,128]{1,0:T(8,128)}) custom-call(f32[8,128]{1,0:T(8,128)} %get-tuple-element.310.refs_0_, bf16[2,256,1152]{2,1,0:T(8,128)(2,1)} %get-tuple-element.311.refs_1_.refs_4_.refs_3_, ...), custom_call_target="tpu_custom_call" | custom-call | flops 6000000 | bytes 1000 | tf_op jit(solution)/shard_map/mlp_bwd/pallas_call | solution.py:114
  559.7 11.8 %weight_grad.12 = (bf16[1152,2304]{1,0:T(8,128)(2,1)}, f32[8,128]{1,0:T(8,128)}) custom-call(bf16[144,2304]{1,0:T(8,128)(2,1)} %bitcast.297, f32[8,128]{1,0:T(8,128)} %get-tuple-element.313.refs_1_, bf16[2,256,1152]{2,1,0:T(8,128)(2,1)} %get-tuple-element.220.refs_1_.refs_2_, bf16[2,256,1152]{2,1,0:T(8,128)(2,1)} %collective-permute-done.11.refs_2_.refs_3_, ...), custom_call_target="tpu_custom_call" | custom-call | flops 6000000 | bytes 1000 | tf_op jit(solution)/shard_map/weight_grad/pallas_call | solution.py:114
  572.2 6.0 norm_bwd.12
  578.2 11.4 %weight_grad.13 = (bf16[1152,2304]{1,0:T(8,128)(2,1)}, f32[8,128]{1,0:T(8,128)}) custom-call(f32[8,128]{1,0:T(8,128)} %get-tuple-element.320.refs_0_, bf16[2,256,1152]{2,1,0:T(8,128)(2,1)} %get-tuple-element.303.refs_1_.refs_3_, bf16[2,256,1152]{2,1,0:T(8,128)(2,1)} %copy-done.21, ...), custom_call_target="tpu_custom_call", output_to_operand_aliasing={{0}: (7, {})} | custom-call | flops 6000000 | bytes 1000 | tf_op jit(solution)/shard_map/weight_grad/pallas_call | solution.py:114
  594.8 22.0 %attend_bwd.6 = (bf16[1024,1024]{1,0:T(8,128)(2,1)}, f32[4,1,256]{2,1,0:T(1,128)}, f32[4,2,32,128]{3,2,1,0:T(8,128)}, bf16[2,256,1152]{2,1,0:T(8,128)(2,1)}, bf1...) custom-call(f32[8,128]{1,0:T(8,128)} %get-tuple-element.324.refs_0_, ...), custom_call_target="tpu_custom_call" | custom-call | flops 6000000 | bytes 1000 | tf_op jit(solution)/shard_map/attend_bwd/pallas_call | solution.py:114
  621.2 6.0 norm_bwd.13
  631.4 6.2 weight_grad.14
  637.7 22.2 %attend_bwd.7 = (bf16[1024,1024]{1,0:T(8,128)(2,1)}, f32[4,1,256]{2,1,0:T(1,128)}, f32[4,2,32,128]{3,2,1,0:T(8,128)}, bf16[2,256,1152]{2,1,0:T(8,128)(2,1)}, bf1...) custom-call(bf16[144,1536]{1,0:T(8,128)(2,1)} %bitcast.302, f32[8,128]{1,0:T(8,128)} %get-tuple-element.337.refs_1_, ...), custom_call_target="tpu_custom_call" | custom-call | flops 6000000 | bytes 1000 | tf_op jit(solution)/shard_map/attend_bwd/pallas_call | solution.py:114
  664.3 9.9 %weight_grad.15 = (bf16[1152,1536]{1,0:T(8,128)(2,1)}, f32[8,128]{1,0:T(8,128)}) custom-call(f32[8,128]{1,0:T(8,128)} %get-tuple-element.339.refs_0_, bf16[2,256,1152]{2,1,0:T(8,128)(2,1)} %get-tuple-element.206.refs_2_.refs_1_, bf16[2,256,1152]{2,1,0:T(8,128)(2,1)} %collective-permute-done.5.refs_3_.refs_2_, ...), custom_call_target="tpu_custom_call", output_to_operand_aliasing={{0}: (7, {})} | custom-call | flops 6000000 | bytes 1000 | tf_op jit(solution)/shard_map/weight_grad/pallas_call | solution.py:114
  676.0 26.4 %reduce-scatter.7.cloned.1.call-done = bf16[1,144,2304]{2,1,0:T(8,128)(2,1)} async-done(((bf16[8,144,2304]{2,1,0:T(8,128)(2,1)}), bf16[1,144,2304]{2,1,0:T(8,128)(2,1)}) %reduce-scatter.7.cloned.1.call-update) | async-done | bytes 663568 | tf_op jit(solution)/shard_map/reduce_scatter | solution.py:1029
  713.9 2.9 add_near.3
  729.3 3.6 norm_bwd.14
  735.1 3.7 norm_bwd.15
  775.3 11.5 %reduce-scatter.11.cloned.1.call-done = bf16[1,144,1536]{2,1,0:T(8,128)(2,1)} async-done(((bf16[8,144,1536]{2,1,0:T(8,128)(2,1)}), bf16[1,144,1536]{2,1,0:T(8,128)(2,1)}) %reduce-scatter.11.cloned.1.call-update) | async-done | bytes 442384 | tf_op jit(solution)/shard_map/reduce_scatter | solution.py:1029
  793.4 4.9 multiply_reduce_fusion.5
  (539 shorter events, 213.8 us)
Async XLA Ops:
  7.2 71.1 %all-gather.5.cloned.1.call-start = ((), (), s32[]{:S(2)}) async-start(), calls=%async_computation.4 | async-start | bytes 2985984 | tf_op jit(solution)/shard_map/all_gather | solution.py:842
  11.4 150.9 %all-gather.7.cloned.1.call-start = ((), (), s32[]{:S(2)}) async-start(), calls=%async_computation.5 | async-start | bytes 5971968 | tf_op jit(solution)/shard_map/all_gather | solution.py:842
  15.3 203.0 %all-gather.9.cloned.1.call-start = ((), (), s32[]{:S(2)}) async-start(), calls=%async_computation.6 | async-start | bytes 2985984 | tf_op jit(solution)/shard_map/all_gather | solution.py:842
  19.0 25.1 %collective-permute-start.1 = (f32[33,576]{1,0:T(8,128)}, f32[33,576]{1,0:T(8,128)}, u32[]{:S(2)}, u32[]{:S(2)}) collective-permute-start(f32[33,576]{1,0:T(8,128)} %concatenate.52), channel_id=1, source_target_pairs={{0,4},{4,0},{8,12},{12,8},{16,20},{20,16},{24,28},{28,24},{1,5},{5... | collective-permute-start | bytes 228104 | tf_op jit(solution)/shard_map/ppermute | solution.py:774
  22.0 35.8 %collective-permute-start.4 = (bf16[2,256,1152]{2,1,0:T(8,128)(2,1)}, bf16[2,256,1152]{2,1,0:T(8,128)(2,1)}, u32[]{:S(2)}, u32[]{:S(2)}) collective-permute-start(bf16[2,256,1152]{2,1,0:T(8,128)(2,1)} %param.29), channel_id=1, source_target_pairs={{0,2},{1,3},{2,0},{3,1},{4,6},{5,7},{6,4},{7,5},{8,10},{9,11},{10,... | collective-permute-start | bytes 3538952 | tf_op jit(solution)/shard_map/ppermute | solution.py:774
  24.8 50.1 %collective-permute-start = (bf16[2,256,1152]{2,1,0:T(8,128)(2,1)}, bf16[2,256,1152]{2,1,0:T(8,128)(2,1)}, u32[]{:S(2)}, u32[]{:S(2)}) collective-permute-start(bf16[2,256,1152]{2,1,0:T(8,128)(2,1)} %multiply_convert_fusion), channel_id=1, source_target_pairs={{0,2},{1,3},{2,0},{3,1},{4,6},{5,7},{6,4},{7,5},{8,10},{9,11},{10,... | collective-permute-start | bytes 3538952 | tf_op jit(solution)/shard_map/ppermute | solution.py:774
  27.3 279.2 %all-gather.11.cloned.1.call-start = ((), (), s32[]{:S(2)}) async-start(), calls=%async_computation.7 | async-start | bytes 5971968 | tf_op jit(solution)/shard_map/all_gather | solution.py:842
  45.0 11.8 %collective-permute-start.2 = (f32[33,576]{1,0:T(8,128)S(1)}, f32[33,576]{1,0:T(8,128)S(1)}, u32[]{:S(2)}, u32[]{:S(2)}) collective-permute-start(f32[33,576]{1,0:T(8,128)S(1)} %pad_add_fusion.1), channel_id=1, source_target_pairs={{0,8},{4,12},{8,0},{12,4},{16,24},{20,28},{24,16},{28,20},{1,9},{5... | collective-permute-start | bytes 228104 | tf_op jit(solution)/shard_map/ppermute | solution.py:774
  56.8 13.5 %collective-permute-start.3 = (f32[33,576]{1,0:T(8,128)S(1)}, f32[33,576]{1,0:T(8,128)S(1)}, u32[]{:S(2)}, u32[]{:S(2)}) collective-permute-start(f32[33,576]{1,0:T(8,128)S(1)} %add.266), channel_id=1, source_target_pairs={{0,16},{4,20},{8,24},{12,28},{16,0},{20,4},{24,8},{28,12},{1,17},{... | collective-permute-start | bytes 228104 | tf_op jit(solution)/shard_map/ppermute | solution.py:774
  63.9 18.4 %collective-permute-start.5 = (bf16[2,256,1152]{2,1,0:T(8,128)(2,1)}, bf16[2,256,1152]{2,1,0:T(8,128)(2,1)}, u32[]{:S(2)}, u32[]{:S(2)}) collective-permute-start(bf16[2,256,1152]{2,1,0:T(8,128)(2,1)} %get-tuple-element.206.refs_2_.refs_1_), channel_id=1, source_target_pairs={{0,1},{1,0},{2,3},{3,2},{4,5},{5,4},{6,7},{7,6},{8,9},{9,8},{10,11... | collective-permute-start | bytes 3538952 | tf_op jit(solution)/shard_map/ppermute | solution.py:774
  101.6 3.3 collective-permute-start.6
  101.7 7.2 collective-permute-start.8
  107.4 28.3 %collective-permute-start.7 = (bf16[2,256,1152]{2,1,0:T(8,128)(2,1)}, bf16[2,256,1152]{2,1,0:T(8,128)(2,1)}, u32[]{:S(2)}, u32[]{:S(2)}) collective-permute-start(bf16[2,256,1152]{2,1,0:T(8,128)(2,1)} %get-tuple-element.211.refs_2_), channel_id=1, source_target_pairs={{0,2},{1,3},{2,0},{3,1},{4,6},{5,7},{6,4},{7,5},{8,10},{9,11},{10,... | collective-permute-start | bytes 3538952 | tf_op jit(solution)/shard_map/ppermute | solution.py:774
  127.7 8.6 %collective-permute-start.9 = (bf16[2,256,1152]{2,1,0:T(8,128)(2,1)}, bf16[2,256,1152]{2,1,0:T(8,128)(2,1)}, u32[]{:S(2)}, u32[]{:S(2)}) collective-permute-start(bf16[2,256,1152]{2,1,0:T(8,128)(2,1)} %get-tuple-element.217), channel_id=1, source_target_pairs={{0,1},{1,0},{2,3},{3,2},{4,5},{5,4},{6,7},{7,6},{8,9},{9,8},{10,11... | collective-permute-start | bytes 3538952 | tf_op jit(solution)/shard_map/ppermute | solution.py:774
  141.2 3.2 collective-permute-start.11
  141.2 34.4 %collective-permute-start.10 = (bf16[2,256,1152]{2,1,0:T(8,128)(2,1)}, bf16[2,256,1152]{2,1,0:T(8,128)(2,1)}, u32[]{:S(2)}, u32[]{:S(2)}) collective-permute-start(bf16[2,256,1152]{2,1,0:T(8,128)(2,1)} %get-tuple-element.218.refs_2_), channel_id=1, source_target_pairs={{0,2},{1,3},{2,0},{3,1},{4,6},{5,7},{6,4},{7,5},{8,10},{9,11},{10,... | collective-permute-start | bytes 3538952 | tf_op jit(solution)/shard_map/ppermute | solution.py:774
  175.5 384.2 %reduce-scatter.5.cloned.1.call-start = ((), (), s32[]{:S(2)}) async-start(), calls=%async_computation.8 | async-start | bytes 5971968 | tf_op jit(solution)/shard_map/reduce_scatter | solution.py:1029
  182.5 28.6 %collective-permute-start.13 = (bf16[2,256,1152]{2,1,0:T(8,128)(2,1)}, bf16[2,256,1152]{2,1,0:T(8,128)(2,1)}, u32[]{:S(2)}, u32[]{:S(2)}) collective-permute-start(bf16[2,256,1152]{2,1,0:T(8,128)(2,1)} %get-tuple-element.225.refs_2_), channel_id=1, source_target_pairs={{0,2},{1,3},{2,0},{3,1},{4,6},{5,7},{6,4},{7,5},{8,10},{9,11},{10,... | collective-permute-start | bytes 3538952 | tf_op jit(solution)/shard_map/ppermute | solution.py:774
  197.8 24.4 %collective-permute-start.15 = (bf16[2,256,1152]{2,1,0:T(8,128)(2,1)}, bf16[2,256,1152]{2,1,0:T(8,128)(2,1)}, u32[]{:S(2)}, u32[]{:S(2)}) collective-permute-start(bf16[2,256,1152]{2,1,0:T(8,128)(2,1)} %get-tuple-element.232), channel_id=1, source_target_pairs={{0,1},{1,0},{2,3},{3,2},{4,5},{5,4},{6,7},{7,6},{8,9},{9,8},{10,11... | collective-permute-start | bytes 3538952 | tf_op jit(solution)/shard_map/ppermute | solution.py:774
  227.0 28.7 %collective-permute-start.16 = (bf16[2,256,1152]{2,1,0:T(8,128)(2,1)}, bf16[2,256,1152]{2,1,0:T(8,128)(2,1)}, u32[]{:S(2)}, u32[]{:S(2)}) collective-permute-start(bf16[2,256,1152]{2,1,0:T(8,128)(2,1)} %get-tuple-element.233.refs_2_), channel_id=1, source_target_pairs={{0,2},{1,3},{2,0},{3,1},{4,6},{5,7},{6,4},{7,5},{8,10},{9,11},{10,... | collective-permute-start | bytes 3538952 | tf_op jit(solution)/shard_map/ppermute | solution.py:774
  249.1 7.2 collective-permute-start.18
  261.5 28.7 %collective-permute-start.19 = (bf16[2,256,1152]{2,1,0:T(8,128)(2,1)}, bf16[2,256,1152]{2,1,0:T(8,128)(2,1)}, u32[]{:S(2)}, u32[]{:S(2)}) collective-permute-start(bf16[2,256,1152]{2,1,0:T(8,128)(2,1)} %get-tuple-element.241.refs_2_), channel_id=1, source_target_pairs={{0,2},{1,3},{2,0},{3,1},{4,6},{5,7},{6,4},{7,5},{8,10},{9,11},{10,... | collective-permute-start | bytes 3538952 | tf_op jit(solution)/shard_map/ppermute | solution.py:774
  284.0 6.8 collective-permute-start.21
  295.4 11.1 %collective-permute-start.23 = (bf16[2,256,1152]{2,1,0:T(8,128)(2,1)}, bf16[2,256,1152]{2,1,0:T(8,128)(2,1)}, u32[]{:S(2)}, u32[]{:S(2)}) collective-permute-start(bf16[2,256,1152]{2,1,0:T(8,128)(2,1)} %get-tuple-element.250.refs_1_), channel_id=1, source_target_pairs={{0,1},{1,0},{2,3},{3,2},{4,5},{5,4},{6,7},{7,6},{8,9},{9,8},{10,11... | collective-permute-start | bytes 3538952 | tf_op jit(solution)/shard_map/ppermute | solution.py:774
  298.7 20.1 %collective-permute-start.24 = (bf16[2,256,1152]{2,1,0:T(8,128)(2,1)}, bf16[2,256,1152]{2,1,0:T(8,128)(2,1)}, u32[]{:S(2)}, u32[]{:S(2)}) collective-permute-start(bf16[2,256,1152]{2,1,0:T(8,128)(2,1)} %get-tuple-element.515.refs_1_.refs_3_), channel_id=1, source_target_pairs={{0,1},{1,0},{2,3},{3,2},{4,5},{5,4},{6,7},{7,6},{8,9},{9,8},{10,11... | collective-permute-start | bytes 3538952 | tf_op jit(solution)/shard_map/ppermute | solution.py:774
  299.2 33.7 %collective-permute-start.22 = (bf16[2,256,1152]{2,1,0:T(8,128)(2,1)}, bf16[2,256,1152]{2,1,0:T(8,128)(2,1)}, u32[]{:S(2)}, u32[]{:S(2)}) collective-permute-start(bf16[2,256,1152]{2,1,0:T(8,128)(2,1)} %get-tuple-element.248.refs_2_), channel_id=1, source_target_pairs={{0,2},{1,3},{2,0},{3,1},{4,6},{5,7},{6,4},{7,5},{8,10},{9,11},{10,... | collective-permute-start | bytes 3538952 | tf_op jit(solution)/shard_map/ppermute | solution.py:774
  332.3 3.3 collective-permute-start.25
  332.4 4.9 collective-permute-start.26
  346.0 15.3 %collective-permute-start.29 = (bf16[2,256,1152]{2,1,0:T(8,128)(2,1)}, bf16[2,256,1152]{2,1,0:T(8,128)(2,1)}, u32[]{:S(2)}, u32[]{:S(2)}) collective-permute-start(bf16[2,256,1152]{2,1,0:T(8,128)(2,1)} %get-tuple-element.514.refs_1_.refs_4_.refs_3_), channel_id=1, source_target_pairs={{0,1},{1,0},{2,3},{3,2},{4,5},{5,4},{6,7},{7,6},{8,9},{9,8},{10,11... | collective-permute-start | bytes 3538952 | tf_op jit(solution)/shard_map/ppermute | solution.py:774
  346.3 41.0 %collective-permute-start.27 = (bf16[3,256,1152]{2,1,0:T(8,128)(2,1)}, bf16[3,256,1152]{2,1,0:T(8,128)(2,1)}, u32[]{:S(2)}, u32[]{:S(2)}) collective-permute-start(bf16[3,256,1152]{2,1,0:T(8,128)(2,1)} %get-tuple-element.258.refs_1_), channel_id=1, source_target_pairs={{0,2},{1,3},{2,0},{3,1},{4,6},{5,7},{6,4},{7,5},{8,10},{9,11},{10,... | collective-permute-start | bytes 5308424 | tf_op jit(solution)/shard_map/ppermute | solution.py:774
  374.6 13.3 %collective-permute-start.30 = (bf16[2,256,1152]{2,1,0:T(8,128)(2,1)}, bf16[2,256,1152]{2,1,0:T(8,128)(2,1)}, u32[]{:S(2)}, u32[]{:S(2)}) collective-permute-start(bf16[2,256,1152]{2,1,0:T(8,128)(2,1)} %get-tuple-element.270), channel_id=1, source_target_pairs={{0,1},{1,0},{2,3},{3,2},{4,5},{5,4},{6,7},{7,6},{8,9},{9,8},{10,11... | collective-permute-start | bytes 3538952 | tf_op jit(solution)/shard_map/ppermute | solution.py:774
  374.7 13.1 %collective-permute-start.31 = (bf16[2,256,1152]{2,1,0:T(8,128)(2,1)}, bf16[2,256,1152]{2,1,0:T(8,128)(2,1)}, u32[]{:S(2)}, u32[]{:S(2)}) collective-permute-start(bf16[2,256,1152]{2,1,0:T(8,128)(2,1)} %get-tuple-element.272), channel_id=1, source_target_pairs={{0,1},{1,0},{2,3},{3,2},{4,5},{5,4},{6,7},{7,6},{8,9},{9,8},{10,11... | collective-permute-start | bytes 3538952 | tf_op jit(solution)/shard_map/ppermute | solution.py:774
  409.1 228.6 %reduce-scatter.9.cloned.1.call-start = ((), (), s32[]{:S(2)}) async-start(), calls=%async_computation.10 | async-start | bytes 3981312 | tf_op jit(solution)/shard_map/reduce_scatter | solution.py:1029
  410.4 41.3 %collective-permute-start.32 = (bf16[3,256,1152]{2,1,0:T(8,128)(2,1)}, bf16[3,256,1152]{2,1,0:T(8,128)(2,1)}, u32[]{:S(2)}, u32[]{:S(2)}) collective-permute-start(bf16[3,256,1152]{2,1,0:T(8,128)(2,1)} %get-tuple-element.273.refs_1_), channel_id=1, source_target_pairs={{0,2},{1,3},{2,0},{3,1},{4,6},{5,7},{6,4},{7,5},{8,10},{9,11},{10,... | collective-permute-start | bytes 5308424 | tf_op jit(solution)/shard_map/ppermute | solution.py:774
  436.2 16.1 %collective-permute-start.34 = (bf16[2,256,1152]{2,1,0:T(8,128)(2,1)}, bf16[2,256,1152]{2,1,0:T(8,128)(2,1)}, u32[]{:S(2)}, u32[]{:S(2)}) collective-permute-start(bf16[2,256,1152]{2,1,0:T(8,128)(2,1)} %get-tuple-element.287), channel_id=1, source_target_pairs={{0,1},{1,0},{2,3},{3,2},{4,5},{5,4},{6,7},{7,6},{8,9},{9,8},{10,11... | collective-permute-start | bytes 3538952 | tf_op jit(solution)/shard_map/ppermute | solution.py:774
  458.4 3.2 collective-permute-start.36
  458.4 31.6 %collective-permute-start.35 = (bf16[2,256,1152]{2,1,0:T(8,128)(2,1)}, bf16[2,256,1152]{2,1,0:T(8,128)(2,1)}, u32[]{:S(2)}, u32[]{:S(2)}) collective-permute-start(bf16[2,256,1152]{2,1,0:T(8,128)(2,1)} %get-tuple-element.288.refs_1_), channel_id=1, source_target_pairs={{0,2},{1,3},{2,0},{3,1},{4,6},{5,7},{6,4},{7,5},{8,10},{9,11},{10,... | collective-permute-start | bytes 3538952 | tf_op jit(solution)/shard_map/ppermute | solution.py:774
  483.6 7.1 collective-permute-start.37
  506.2 196.1 %reduce-scatter.7.cloned.1.call-start = ((), (), s32[]{:S(2)}) async-start(), calls=%async_computation.9 | async-start | bytes 5971968 | tf_op jit(solution)/shard_map/reduce_scatter | solution.py:1029
  508.0 28.2 %collective-permute-start.38 = (bf16[2,256,1152]{2,1,0:T(8,128)(2,1)}, bf16[2,256,1152]{2,1,0:T(8,128)(2,1)}, u32[]{:S(2)}, u32[]{:S(2)}) collective-permute-start(bf16[2,256,1152]{2,1,0:T(8,128)(2,1)} %get-tuple-element.297.refs_1_), channel_id=1, source_target_pairs={{0,2},{1,3},{2,0},{3,1},{4,6},{5,7},{6,4},{7,5},{8,10},{9,11},{10,... | collective-permute-start | bytes 3538952 | tf_op jit(solution)/shard_map/ppermute | solution.py:774
  525.0 11.8 %collective-permute-start.40 = (bf16[2,256,1152]{2,1,0:T(8,128)(2,1)}, bf16[2,256,1152]{2,1,0:T(8,128)(2,1)}, u32[]{:S(2)}, u32[]{:S(2)}) collective-permute-start(bf16[2,256,1152]{2,1,0:T(8,128)(2,1)} %get-tuple-element.307), channel_id=1, source_target_pairs={{0,1},{1,0},{2,3},{3,2},{4,5},{5,4},{6,7},{7,6},{8,9},{9,8},{10,11... | collective-permute-start | bytes 3538952 | tf_op jit(solution)/shard_map/ppermute | solution.py:774
  542.9 3.2 collective-permute-start.42
  542.9 28.7 %collective-permute-start.41 = (bf16[2,256,1152]{2,1,0:T(8,128)(2,1)}, bf16[2,256,1152]{2,1,0:T(8,128)(2,1)}, u32[]{:S(2)}, u32[]{:S(2)}) collective-permute-start(bf16[2,256,1152]{2,1,0:T(8,128)(2,1)} %get-tuple-element.308.refs_1_), channel_id=1, source_target_pairs={{0,2},{1,3},{2,0},{3,1},{4,6},{5,7},{6,4},{7,5},{8,10},{9,11},{10,... | collective-permute-start | bytes 3538952 | tf_op jit(solution)/shard_map/ppermute | solution.py:774
  559.5 12.7 %collective-permute-start.43 = (bf16[2,256,1152]{2,1,0:T(8,128)(2,1)}, bf16[2,256,1152]{2,1,0:T(8,128)(2,1)}, u32[]{:S(2)}, u32[]{:S(2)}) collective-permute-start(bf16[2,256,1152]{2,1,0:T(8,128)(2,1)} %get-tuple-element.318), channel_id=1, source_target_pairs={{0,1},{1,0},{2,3},{3,2},{4,5},{5,4},{6,7},{7,6},{8,9},{9,8},{10,11... | collective-permute-start | bytes 3538952 | tf_op jit(solution)/shard_map/ppermute | solution.py:774
  589.6 197.2 %reduce-scatter.11.cloned.1.call-start = ((), (), s32[]{:S(2)}) async-start(), calls=%async_computation.11 | async-start | bytes 3981312 | tf_op jit(solution)/shard_map/reduce_scatter | solution.py:1029
  591.1 29.5 %collective-permute-start.44 = (bf16[2,256,1152]{2,1,0:T(8,128)(2,1)}, bf16[2,256,1152]{2,1,0:T(8,128)(2,1)}, u32[]{:S(2)}, u32[]{:S(2)}) collective-permute-start(bf16[2,256,1152]{2,1,0:T(8,128)(2,1)} %get-tuple-element.319.refs_1_), channel_id=1, source_target_pairs={{0,2},{1,3},{2,0},{3,1},{4,6},{5,7},{6,4},{7,5},{8,10},{9,11},{10,... | collective-permute-start | bytes 3538952 | tf_op jit(solution)/shard_map/ppermute | solution.py:774
  616.8 4.4 collective-permute-start.46
  627.2 4.3 collective-permute-start.48
  629.9 83.4 %collective-permute-start.47 = (bf16[1,256,1152]{2,1,0:T(8,128)(2,1)}, bf16[1,256,1152]{2,1,0:T(8,128)(2,1)}, u32[]{:S(2)}, u32[]{:S(2)}) collective-permute-start(bf16[1,256,1152]{2,1,0:T(8,128)(2,1)} %slice.288), channel_id=1, source_target_pairs={{0,2},{1,3},{2,0},{3,1},{4,6},{5,7},{6,4},{7,5},{8,10},{9,11},{10,... | collective-permute-start | bytes 1769480 | tf_op jit(solution)/shard_map/ppermute | solution.py:774
  660.8 53.1 %collective-permute-start.49 = (bf16[2,256,1152]{2,1,0:T(8,128)(2,1)}, bf16[2,256,1152]{2,1,0:T(8,128)(2,1)}, u32[]{:S(2)}, u32[]{:S(2)}) collective-permute-start(bf16[2,256,1152]{2,1,0:T(8,128)(2,1)} %get-tuple-element.347), channel_id=1, source_target_pairs={{0,1},{1,0},{2,3},{3,2},{4,5},{5,4},{6,7},{7,6},{8,9},{9,8},{10,11... | collective-permute-start | bytes 3538952 | tf_op jit(solution)/shard_map/ppermute | solution.py:774
  711.9 8.4 %collective-permute-start.61 = (f32[8,128]{1,0:T(8,128)S(1)}, f32[8,128]{1,0:T(8,128)S(1)}, u32[]{:S(2)}, u32[]{:S(2)}) collective-permute-start(f32[8,128]{1,0:T(8,128)S(1)} %pad_bitcast_fusion.1), channel_id=1, source_target_pairs={{0,4},{4,0},{8,12},{12,8},{16,20},{20,16},{24,28},{28,24},{1,5},{5... | collective-permute-start | bytes 12296 | tf_op jit(solution)/shard_map/ppermute | solution.py:774
  718.8 14.9 %collective-permute-start.50 = (bf16[1,256,1152]{2,1,0:T(8,128)(2,1)}, bf16[1,256,1152]{2,1,0:T(8,128)(2,1)S(1)}, u32[]{:S(2)}, u32[]{:S(2)}) collective-permute-start(bf16[1,256,1152]{2,1,0:T(8,128)(2,1)} %slice.289), channel_id=1, source_target_pairs={{0,2},{1,3},{2,0},{3,1},{4,6},{5,7},{6,4},{7,5},{8,10},{9,11},{10,... | collective-permute-start | bytes 1769480 | tf_op jit(solution)/shard_map/ppermute | solution.py:774
  720.3 3.8 collective-permute-start.62
  724.1 5.2 collective-permute-start.63
  729.3 3.6 collective-permute-start.64
  732.9 11.9 %collective-permute-start.65 = (f32[8,128]{1,0:T(8,128)S(1)}, f32[8,128]{1,0:T(8,128)S(1)}, u32[]{:S(2)}, u32[]{:S(2)}) collective-permute-start(f32[8,128]{1,0:T(8,128)S(1)} %add.332), channel_id=1, source_target_pairs={{0,2},{1,3},{2,0},{3,1},{4,6},{5,7},{6,4},{7,5},{8,10},{9,11},{10,... | collective-permute-start | bytes 12296 | tf_op jit(solution)/shard_map/ppermute | solution.py:774
  740.2 7.8 collective-permute-start.51
  748.9 8.9 %collective-permute-start.52 = (f32[224,128]{1,0:T(8,128)S(1)}, f32[224,128]{1,0:T(8,128)S(1)}, u32[]{:S(2)}, u32[]{:S(2)}) collective-permute-start(f32[224,128]{1,0:T(8,128)S(1)} %fusion.45), channel_id=1, source_target_pairs={{0,8},{4,12},{8,0},{12,4},{16,24},{20,28},{24,16},{28,20},{1,9},{5... | collective-permute-start | bytes 344072 | tf_op jit(solution)/shard_map/ppermute | solution.py:774
  758.8 7.0 collective-permute-start.53
  769.1 4.8 collective-permute-start.55
  799.9 3.6 collective-permute-start.56
  803.5 3.6 collective-permute-start.57
  807.1 4.5 collective-permute-start.58
  812.8 3.6 collective-permute-start.60
  (87 other events, 539.1 us)
Sparse Core Ops, SparseCore 0:
  11.5 62.3 all-gather.4
  76.6 85.5 all-gather.6
  165.0 53.1 all-gather.8
  220.9 85.6 all-gather.10
  409.2 102.3 reduce-scatter.4
  515.6 78.8 reduce-scatter.8
  598.6 103.7 reduce-scatter.6
  706.0 80.7 reduce-scatter.10

commit v3 on v2

--- a/solution.py
+++ b/solution.py
@@ -384,8 +384,7 @@
 
 
 def column_chunks(hidden):
-    first = (hidden // 2 + LANE - 1) // LANE * LANE
-    return [pl.ds(0, first), pl.ds(first, hidden - first)]
+    return [pl.ds(start, min(512, hidden - start)) for start in range(0, hidden, 512)]
 
 
 def mlp_body(own_ref, near_ref, up_ref, down_ref, pre_ref, act_ref, keep_ref, send_ref):
@@ -724,12 +723,12 @@
     return results[:2]
 
 
-def weight_body(*refs):
+def weight_body(*refs, packed):
     own0, near0, right0, own1, near1, right1 = refs[:6]
     out_ref, total = refs[-2], refs[-1]
     step = pl.program_id(0)
-    left = jnp.concatenate([own0[0], near0[0], own1[0], near1[0]], axis=0)
-    part = dot_nn(left.T, jnp.concatenate([right0[...], right1[...]], axis=0))
+    part = dot_nn(row_half(own0, near0, 0).T, right0[...])
+    part = part + dot_nn(row_half(own1, near1, 0).T, right1[...])
 
     @pl.when(step == 0)
     def _():
@@ -737,10 +736,27 @@
 
     @pl.when(step > 0)
     def _():
-        out_ref[...] = (total[...] + part).astype(bf16)
-
-
-def weight_call(chain, lefts, rights, buffer, all_columns, place):
+        value = total[...] + part
+        if not packed:
+            out_ref[...] = value.astype(bf16)
+            return
+        other_ref = refs[6]
+        width, columns = value.shape
+        lane, wide = lanes_of((width, LANE)), lanes_of((width, 256))
+        rest = jnp.zeros((width, LANE), f32)
+        for head in range(columns // 256):
+            other = other_ref[:, head * LANE : (head + 1) * LANE].astype(f32)
+            shifted = pltpu.roll(jnp.concatenate([other, jnp.zeros_like(other)], axis=1), 3 * HEAD, 1)
+            block = value[:, head * 256 : (head + 1) * 256]
+            block = jnp.where(wide < 3 * HEAD, block, shifted)
+            out_ref[:, head * 256 : (head + 1) * 256] = block.astype(bf16)
+            size = HEAD - SPARE
+            moved = pltpu.roll(other, (head * size - SPARE) % LANE, 1)
+            rest = jnp.where((lane >= head * size) & (lane < (head + 1) * size), moved, rest)
+        out_ref[:, columns:] = rest.astype(bf16)
+
+
+def weight_call(chain, lefts, rights, buffer, all_columns, place, packed=False):
     _, rows, width = lefts[0][0].shape
     columns = rights[0].shape[1]
     left = pl.BlockSpec((1, rows, width), lambda step: (step, 0, 0))
@@ -748,16 +764,21 @@
     inputs = [*lefts[0], rights[0], *lefts[1], rights[1]]
     in_specs = [left, left, right] * 2
     given = None
-    if buffer is not None:
+    out_spec = pl.BlockSpec((width, columns), lambda step: (0, place))
+    if packed:
+        inputs.append(buffer)
+        in_specs.append(whole_spec(buffer.shape))
+        out_spec = whole_spec((width, all_columns))
+    elif buffer is not None:
         given = {len(inputs): 0}
         inputs.append(buffer)
         in_specs.append(pl.BlockSpec(memory_space=pl.ANY))
     return chain.call(
-        weight_body,
+        functools.partial(weight_body, packed=packed),
         (2,),
         inputs,
         in_specs,
-        [pl.BlockSpec((width, columns), lambda step: (0, place))],
+        [out_spec],
         [jax.ShapeDtypeStruct((width, all_columns), bf16)],
         [pltpu.VMEM((width, columns), f32)],
         BIG,
@@ -1003,8 +1024,8 @@
 
     buffers = {}
     sums = {}
-    wholes = {"mlp": 2 * hidden, "attend": heads * (256 + LANE)}
-    places = {"up": ("mlp", 0), "down": ("mlp", 1), "qkv": ("attend", 0), "out": ("attend", 2)}
+    wholes = {"mlp": 2 * hidden, "attend": heads * (256 + HEAD - SPARE)}
+    places = {"up": ("mlp", 0), "down": ("mlp", 1), "qkv": ("attend", 0), "out": ("attend", 0)}
 
     def unpack_step(layer):
         fetched[layer]["out"] = unpack_call(chain, *fetched[layer]["attend"], heads)
@@ -1016,7 +1037,12 @@
         lefts, rights = zip(*(work[kind, layer, image] for image in images))
         target, place = places[kind]
         buffer = buffers.pop((target, layer), None)
-        whole = weight_call(chain, lefts, rights, buffer, wholes[target], place)
+        if target == "mlp":
+            whole = weight_call(chain, lefts, rights, buffer, wholes[target], place)
+        elif buffer is None:
+            whole = weight_call(chain, lefts, rights, None, heads * LANE, 0)
+        else:
+            whole = weight_call(chain, lefts, rights, buffer, wholes[target], 0, True)
         if buffer is None:
             buffers[target, layer] = whole
             return
@@ -1118,10 +1144,11 @@
 
     def unpack(layer):
         attend = sums["attend", layer].astype(f32)
-        g_qkv, g_out = attend[:, : heads * 256], attend[:, heads * 256 :]
+        blocks = attend[:, : heads * 256].reshape(shard_rows, heads, 256)
+        rest = attend[:, heads * 256 :].reshape(shard_rows, heads, HEAD - SPARE)
+        g_out = jnp.concatenate([blocks[:, :, 3 * HEAD :], rest], axis=2)
         g_up, g_down = jnp.split(sums["mlp", layer].astype(f32), 2, axis=1)
-        g_qkv = g_qkv.reshape(shard_rows, heads, 256)[:, :, : 3 * HEAD]
-        g_qkv = g_qkv.reshape(shard_rows, heads, 3, HEAD).transpose(0, 2, 1, 3)
+        g_qkv = blocks[:, :, : 3 * HEAD].reshape(shard_rows, heads, 3, HEAD).transpose(0, 2, 1, 3)
         g_qkv = g_qkv.reshape(shard_rows, 3, local_width)
         g_time = lax.dot_general(
             own_rows.astype(f32),
@@ -1129,7 +1156,7 @@
             (((0,), (0,)), ((), ())),
             precision=highest,
         ).reshape(shard_rows, 2, local_width)
-        g_out = g_out.reshape(shard_rows, heads, LANE)[:, :, :HEAD].reshape(shard_rows, local_width)
+        g_out = g_out.reshape(shard_rows, local_width)
         return (g_qkv, g_time, g_out.T, g_up, g_down.T)
 
     unpacked = [unpack(layer) for layer in range(layers)]

time: 846 us -> 856 us (1.012)
  other arithmetic: 73.8 us -> 84.2 us
  waiting for transfers between devices: 178 us -> 169 us
    reduce_scatter x4, waiting for transfers between devices: 37.9 us -> 28.6 us  [scatter(): lax.psum_scatter(whole.reshape(groups, shard_rows, whole.shape[1]), 'grou...]
    unnamed x154 -> x175, local copies, waits for them, and re-layouts: 21.9 us -> 21.1 us
  transfers between devices with their start and end apart: 74 -> 74, of which waited for: 40 -> 38; matrix products, arithmetic and copies ran while one was open for 10% -> 13% of each run, Pallas kernels for 51% -> 51%
where the time goes in v3:
time: 856 us; the launch traced here: 846 us
  Pallas kernels  458 us (54%)
  waiting for transfers between devices  169 us (20%)
  other arithmetic  84.2 us (10%)
  local copies, waits for them, and re-layouts  60.2 us (7%)
  starting transfers between devices  50.7 us (6%)
  between operations  17.9 us (2%)
    pallas_call x63, Pallas kernels, call(): pl.pallas_call(wrapped, grid=grid, in_specs=[pl.BlockSpec(memory_space=pl...  458 us
    ppermute x66, waiting for transfers between devices, swap(): lax.ppermute(value, axis, [(index, index ^ bit) for index in range(size)])  109 us
    ppermute x66, starting transfers between devices, swap(): lax.ppermute(value, axis, [(index, index ^ bit) for index in range(size)])  50.3 us
    all_gather x4, waiting for transfers between devices, fetch_together(): lax.all_gather(jnp.concatenate(parts, axis=1), 'group', axis=0, tiled=True)  30.4 us
    reduce_scatter x4, waiting for transfers between devices, scatter(): lax.psum_scatter(whole.reshape(groups, shard_rows, whole.shape[1]), 'grou...  28.6 us
    unnamed x175, local copies, waits for them, and re-layouts  21.1 us
  transfers between devices with their start and end apart: 74, of which 38 were waited for; matrix products, arithmetic and copies ran while one was open for 13% of the time, Pallas kernels for 51%

profile of v3, /device:TPU:0, one launch (start us, length us, event | category | flops | bytes accessed | tf_op | source)
XLA Modules:
  0.0 846.0 jit_solution(10159680741977822168)
XLA Ops:
  19.0 3.0 collective-permute-start.1
  38.3 4.1 pad_maximum_fusion.2.refs_1_
  47.5 9.1 %collective-permute-done.2 = f32[33,576]{1,0:T(8,128)S(1)} collective-permute-done((f32[33,576]{1,0:T(8,128)S(1)}, f32[33,576]{1,0:T(8,128)S(1)}, u32[]{:S(2)}, u32[]{:S(2)}) %collective-permute-start.2) | collective-permute-done | bytes 76064 | tf_op jit(solution)/shard_map/ppermute | solution.py:795
  57.6 2.9 fusion.11
  60.5 3.0 norm_fwd.8
  63.5 4.7 fusion.16
  71.9 2.8 norm_fwd.9
  75.0 3.3 pad_maximum_fusion.1.refs_0_
  78.3 4.0 unpack_out.2
  82.3 19.2 %attend_fwd.4 = (bf16[4,3,1024,128]{3,2,1,0:T(8,128)(2,1)}, bf16[1024,512]{1,0:T(8,128)(2,1)}, bf16[2,256,1152]{2,1,0:T(8,128)(2,1)}, bf16[2,256,1152]{2,1,0:T(8,128)(2,1)}, f32[8,128]{1,0:T(8,128)}) custom-call(bf16[2,2,256,1152]{3,2,1,0:T(8,128)(2,1)} %pad_maximum_fusion.1.refs_0_, f32[8,128]{1,0:T(8,128)} %get-tuple-element.205.refs_1_, ...), custom_call_target="tpu_custom_call" | custom-call | flops 6000000 | bytes 1000 | tf_op jit(solution)/shard_map/attend_fwd/pallas_call | solution.py:114
  108.8 18.8 %attend_fwd.5 = (bf16[4,3,1024,128]{3,2,1,0:T(8,128)(2,1)}, bf16[1024,512]{1,0:T(8,128)(2,1)}, bf16[2,256,1152]{2,1,0:T(8,128)(2,1)}, bf16[2,256,1152]{2,1,0:T(8,128)(2,1)}, f32[8,128]{1,0:T(8,128)}) custom-call(f32[8,128]{1,0:T(8,128)} %get-tuple-element.212.refs_0_, bf16[2,256,1152]{2,1,0:T(8,128)(2,1)} %get-tuple-element.213.refs_1_.refs_4_, ...), custom_call_target="tpu_custom_call" | custom-call | flops 6000000 | bytes 1000 | tf_op jit(solution)/shard_map/attend_fwd/pallas_call | solution.py:114
  127.8 7.9 collective-permute-done.7.refs_0_.refs_3_
  136.3 5.1 norm_fwd.10
  144.5 17.5 %all-gather.7.cloned.1.call-done.refs_3_.refs_4_.refs_5_ = bf16[1152,2304]{1,0:T(8,128)(2,1)} async-done(((bf16[144,2304]{1,0:T(8,128)(2,1)}), bf16[1152,2304]{1,0:T(8,128)(2,1)}) %all-gather.7.cloned.1.call-update) | async-done | bytes 5308432 | tf_op jit(solution)/shard_map/all_gather | solution.py:863
  162.0 11.9 %mlp_fwd.4 = (bf16[1024,1152]{1,0:T(8,128)(2,1)}, bf16[1024,1152]{1,0:T(8,128)(2,1)}, bf16[2,256,1152]{2,1,0:T(8,128)(2,1)}, bf16[2,256,1152]{2,1,0:T(8,128)(2,1)}, f32[8,128]{1,0:T(8,128)}) custom-call(f32[8,128]{1,0:T(8,128)} %get-tuple-element.219.refs_0_, bf16[2,256,1152]{2,1,0:T(8,128)(2,1)} %get-tuple-element.220.refs_1_.refs_2_, ...), custom_call_target="tpu_custom_call" | custom-call | flops 6000000 | bytes 1000 | tf_op jit(solution)/shard_map/mlp_fwd/pallas_call | solution.py:114
  177.1 4.7 norm_fwd.11
  185.0 11.9 %mlp_fwd.5 = (bf16[1024,1152]{1,0:T(8,128)(2,1)}, bf16[1024,1152]{1,0:T(8,128)(2,1)}, bf16[2,256,1152]{2,1,0:T(8,128)(2,1)}, bf16[2,256,1152]{2,1,0:T(8,128)(2,1)}, f32[8,128]{1,0:T(8,128)}) custom-call(f32[8,128]{1,0:T(8,128)} %get-tuple-element.226.refs_0_, bf16[2,256,1152]{2,1,0:T(8,128)(2,1)} %get-tuple-element.227.refs_1_.refs_5_, ...), custom_call_target="tpu_custom_call" | custom-call | flops 6000000 | bytes 1000 | tf_op jit(solution)/shard_map/mlp_fwd/pallas_call | solution.py:114
  197.0 13.5 %collective-permute-done.13.refs_0_.refs_3_ = bf16[2,256,1152]{2,1,0:T(8,128)(2,1)} collective-permute-done((bf16[2,256,1152]{2,1,0:T(8,128)(2,1)}, bf16[2,256,1152]{2,1,0:T(8,128)(2,1)}, u32[]{:S(2)}, u32[]{:S(2)}) %collective-permute-start.13) | collective-permute-done | bytes 1179680 | tf_op jit(solution)/shard_map/ppermute | solution.py:795
  211.1 6.9 all-gather.9.cloned.1.call-done.refs_1_.refs_3_.refs_8_
  218.0 4.0 unpack_out.3
  222.0 4.7 norm_fwd.12
  229.9 18.9 %attend_fwd.6 = (bf16[4,3,1024,128]{3,2,1,0:T(8,128)(2,1)}, bf16[1024,512]{1,0:T(8,128)(2,1)}, bf16[2,256,1152]{2,1,0:T(8,128)(2,1)}, bf16[2,256,1152]{2,1,0:T(8,128)(2,1)}, f32[8,128]{1,0:T(8,128)}) custom-call(f32[8,128]{1,0:T(8,128)} %get-tuple-element.234.refs_0_, bf16[2,256,1152]{2,1,0:T(8,128)(2,1)} %get-tuple-element.235.refs_1_, ...), custom_call_target="tpu_custom_call" | custom-call | flops 6000000 | bytes 1000 | tf_op jit(solution)/shard_map/attend_fwd/pallas_call | solution.py:114
  248.9 6.4 collective-permute-done.16.refs_0_.refs_3_
  256.0 5.2 norm_fwd.13
  264.4 19.0 %attend_fwd.7 = (bf16[4,3,1024,128]{3,2,1,0:T(8,128)(2,1)}, bf16[1024,512]{1,0:T(8,128)(2,1)}, bf16[2,256,1152]{2,1,0:T(8,128)(2,1)}, bf16[2,256,1152]{2,1,0:T(8,128)(2,1)}, f32[8,128]{1,0:T(8,128)}) custom-call(f32[8,128]{1,0:T(8,128)} %get-tuple-element.242.refs_0_, bf16[2,256,1152]{2,1,0:T(8,128)(2,1)} %get-tuple-element.243.refs_1_.refs_4_, ...), custom_call_target="tpu_custom_call" | custom-call | flops 6000000 | bytes 1000 | tf_op jit(solution)/shard_map/attend_fwd/pallas_call | solution.py:114
  283.6 6.3 collective-permute-done.19.refs_0_.refs_3_
  290.5 4.7 norm_fwd.14
  295.1 3.3 fusion.10
  300.2 6.0 all-gather.11.cloned.1.call-done.refs_3_.refs_4_.refs_5_
  306.3 11.9 %mlp_fwd.6 = (bf16[1024,1152]{1,0:T(8,128)(2,1)}, bf16[1024,1152]{1,0:T(8,128)(2,1)}, bf16[2,256,1152]{2,1,0:T(8,128)(2,1)}, bf16[2,256,1152]{2,1,0:T(8,128)(2,1)}, f32[8,128]{1,0:T(8,128)}) custom-call(f32[8,128]{1,0:T(8,128)} %get-tuple-element.249.refs_0_, bf16[2,256,1152]{2,1,0:T(8,128)(2,1)} %get-tuple-element.250.refs_1_, ...), custom_call_target="tpu_custom_call" | custom-call | flops 6000000 | bytes 1000 | tf_op jit(solution)/shard_map/mlp_fwd/pallas_call | solution.py:114
  318.2 13.0 %mlp_bwd.4 = (bf16[1024,1152]{1,0:T(8,128)(2,1)}, bf16[2,256,1152]{2,1,0:T(8,128)(2,1)}, bf16[2,256,1152]{2,1,0:T(8,128)(2,1)}, f32[8,128]{1,0:T(8,128)}) custom-call(f32[8,128]{1,0:T(8,128)} %get-tuple-element.251.refs_0_, bf16[2,256,1152]{2,1,0:T(8,128)(2,1)} %get-tuple-element.515.refs_1_.refs_3_, bf16[2,256,1152]{2,1,0:T(8,128)(2,1)} %collective-permute-done.24.refs_2_, ...), custom_call_target="tpu_custom_call" | custom-call | flops 6000000 | bytes 1000 | tf_op jit(solution)/shard_map/mlp_bwd/pallas_call | solution.py:114
  336.0 5.2 add_both.2
  341.2 3.6 norm_fwd.15
  348.0 11.9 %mlp_fwd.7 = (bf16[1024,1152]{1,0:T(8,128)(2,1)}, bf16[1024,1152]{1,0:T(8,128)(2,1)}, bf16[2,256,1152]{2,1,0:T(8,128)(2,1)}, bf16[2,256,1152]{2,1,0:T(8,128)(2,1)}, f32[8,128]{1,0:T(8,128)}) custom-call(f32[8,128]{1,0:T(8,128)} %get-tuple-element.261.refs_0_, bf16[2,256,1152]{2,1,0:T(8,128)(2,1)} %get-tuple-element.262.refs_1_.refs_4_, ...), custom_call_target="tpu_custom_call" | custom-call | flops 6000000 | bytes 1000 | tf_op jit(solution)/shard_map/mlp_fwd/pallas_call | solution.py:114
  359.9 13.0 %mlp_bwd.5 = (bf16[1024,1152]{1,0:T(8,128)(2,1)}, bf16[2,256,1152]{2,1,0:T(8,128)(2,1)}, bf16[2,256,1152]{2,1,0:T(8,128)(2,1)}, f32[8,128]{1,0:T(8,128)}) custom-call(f32[8,128]{1,0:T(8,128)} %get-tuple-element.263.refs_0_, bf16[2,256,1152]{2,1,0:T(8,128)(2,1)} %get-tuple-element.514.refs_1_.refs_4_.refs_3_, ...), custom_call_target="tpu_custom_call" | custom-call | flops 6000000 | bytes 1000 | tf_op jit(solution)/shard_map/mlp_bwd/pallas_call | solution.py:114
  373.9 11.4 %weight_grad.8 = (bf16[1152,2304]{1,0:T(8,128)(2,1)}, f32[8,128]{1,0:T(8,128)}) custom-call(f32[8,128]{1,0:T(8,128)} %get-tuple-element.265.refs_0_, bf16[2,256,1152]{2,1,0:T(8,128)(2,1)} %get-tuple-element.250.refs_1_, bf16[2,256,1152]{2,1,0:T(8,128)(2,1)} %collective-permute-done.23.refs_2_, bf16[1024,1152]{1,0:T(8,128)(2,1)} %get-tuple-element.266.refs_3_, ...), custom_call_target="tpu_custom_call" | custom-call | flops 6000000 | bytes 1000 | tf_op jit(solution)/shard_map/weight_grad/pallas_call | solution.py:114
  386.9 5.0 add_both.3
  391.9 5.0 norm_bwd.8
  396.9 11.3 %weight_grad.9 = (bf16[1152,2304]{1,0:T(8,128)(2,1)}, f32[8,128]{1,0:T(8,128)}) custom-call(f32[8,128]{1,0:T(8,128)} %get-tuple-element.276.refs_0_, bf16[2,256,1152]{2,1,0:T(8,128)(2,1)} %get-tuple-element.515.refs_1_.refs_3_, bf16[2,256,1152]{2,1,0:T(8,128)(2,1)} %collective-permute-done.24.refs_2_, ...), custom_call_target="tpu_custom_call", output_to_operand_aliasing={{0}: (7, {})} | custom-call | flops 6000000 | bytes 1000 | tf_op jit(solution)/shard_map/weight_grad/pallas_call | solution.py:114
  413.3 21.9 %attend_bwd.4 = (bf16[1024,1024]{1,0:T(8,128)(2,1)}, f32[4,1,256]{2,1,0:T(1,128)}, f32[4,2,32,128]{3,2,1,0:T(8,128)}, bf16[2,256,1152]{2,1,0:T(8,128)(2,1)}, bf1...) custom-call(f32[8,128]{1,0:T(8,128)} %get-tuple-element.280.refs_0_, ...), custom_call_target="tpu_custom_call" | custom-call | flops 6000000 | bytes 1000 | tf_op jit(solution)/shard_map/attend_bwd/pallas_call | solution.py:114
  435.6 15.2 %collective-permute-done.32.refs_0_.refs_2_.refs_3_ = bf16[3,256,1152]{2,1,0:T(8,128)(2,1)} collective-permute-done((bf16[3,256,1152]{2,1,0:T(8,128)(2,1)}, bf16[3,256,1152]{2,1,0:T(8,128)(2,1)}, u32[]{:S(2)}, u32[]{:S(2)}) %collective-permute-start.32) | collective-permute-done | bytes 1769504 | tf_op jit(solution)/shard_map/ppermute | solution.py:795
  451.4 5.9 norm_bwd.9
  460.6 22.0 %attend_bwd.5 = (bf16[1024,1024]{1,0:T(8,128)(2,1)}, f32[4,1,256]{2,1,0:T(1,128)}, f32[4,2,32,128]{3,2,1,0:T(8,128)}, bf16[2,256,1152]{2,1,0:T(8,128)(2,1)}, bf1...) custom-call(f32[8,128]{1,0:T(8,128)} %get-tuple-element.289.refs_0_, ...), custom_call_target="tpu_custom_call" | custom-call | flops 6000000 | bytes 1000 | tf_op jit(solution)/shard_map/attend_bwd/pallas_call | solution.py:114
  482.8 6.2 weight_grad.10
  489.6 5.9 norm_bwd.10
  495.5 11.5 %weight_grad.11 = (bf16[1152,1152]{1,0:T(8,128)(2,1)}, f32[8,128]{1,0:T(8,128)}) custom-call(f32[8,128]{1,0:T(8,128)} %get-tuple-element.298.refs_0_, bf16[2,256,1152]{2,1,0:T(8,128)(2,1)} %get-tuple-element.235.refs_1_, bf16[2,256,1152]{2,1,0:T(8,128)(2,1)} %collective-permute-done.17.refs_2_, bf16[1024,1024]{1,0:T(8,128)(2,1)} %get-tuple-element.299.refs_3_, ...), custom_call_target="tpu_custom_call" | custom-call | flops 6000000 | bytes 1000 | tf_op jit(solution)/shard_map/weight_grad/pallas_call | solution.py:114
  512.2 13.4 %mlp_bwd.6 = (bf16[1024,1152]{1,0:T(8,128)(2,1)}, bf16[2,256,1152]{2,1,0:T(8,128)(2,1)}, bf16[2,256,1152]{2,1,0:T(8,128)(2,1)}, f32[8,128]{1,0:T(8,128)}) custom-call(f32[8,128]{1,0:T(8,128)} %get-tuple-element.302.refs_0_, bf16[2,256,1152]{2,1,0:T(8,128)(2,1)} %get-tuple-element.303.refs_1_.refs_3_, bf16[2,256,1152]{2,1,0:T(8,128)(2,1)} %copy-done.21, ...), custom_call_target="tpu_custom_call" | custom-call | flops 6000000 | bytes 1000 | tf_op jit(solution)/shard_map/mlp_bwd/pallas_call | solution.py:114
  525.9 11.0 %collective-permute-done.38.refs_0_.refs_2_ = bf16[2,256,1152]{2,1,0:T(8,128)(2,1)} collective-permute-done((bf16[2,256,1152]{2,1,0:T(8,128)(2,1)}, bf16[2,256,1152]{2,1,0:T(8,128)(2,1)}, u32[]{:S(2)}, u32[]{:S(2)}) %collective-permute-start.38) | collective-permute-done | bytes 1179680 | tf_op jit(solution)/shard_map/ppermute | solution.py:795
  537.6 6.0 norm_bwd.11
  546.8 13.1 %mlp_bwd.7 = (bf16[1024,1152]{1,0:T(8,128)(2,1)}, bf16[2,256,1152]{2,1,0:T(8,128)(2,1)}, bf16[2,256,1152]{2,1,0:T(8,128)(2,1)}, f32[8,128]{1,0:T(8,128)}) custom-call(f32[8,128]{1,0:T(8,128)} %get-tuple-element.310.refs_0_, bf16[2,256,1152]{2,1,0:T(8,128)(2,1)} %get-tuple-element.311.refs_1_.refs_4_.refs_3_, ...), custom_call_target="tpu_custom_call" | custom-call | flops 6000000 | bytes 1000 | tf_op jit(solution)/shard_map/mlp_bwd/pallas_call | solution.py:114
  560.0 11.3 %weight_grad.12 = (bf16[1152,2304]{1,0:T(8,128)(2,1)}, f32[8,128]{1,0:T(8,128)}) custom-call(bf16[144,2304]{1,0:T(8,128)(2,1)} %bitcast.300, f32[8,128]{1,0:T(8,128)} %get-tuple-element.313.refs_1_, bf16[2,256,1152]{2,1,0:T(8,128)(2,1)} %get-tuple-element.220.refs_1_.refs_2_, bf16[2,256,1152]{2,1,0:T(8,128)(2,1)} %collective-permute-done.11.refs_2_.refs_3_, ...), custom_call_target="tpu_custom_call" | custom-call | flops 6000000 | bytes 1000 | tf_op jit(solution)/shard_map/weight_grad/pallas_call | solution.py:114
  572.9 6.1 norm_bwd.12
  579.0 11.4 %weight_grad.13 = (bf16[1152,2304]{1,0:T(8,128)(2,1)}, f32[8,128]{1,0:T(8,128)}) custom-call(f32[8,128]{1,0:T(8,128)} %get-tuple-element.320.refs_0_, bf16[2,256,1152]{2,1,0:T(8,128)(2,1)} %get-tuple-element.303.refs_1_.refs_3_, bf16[2,256,1152]{2,1,0:T(8,128)(2,1)} %copy-done.21, ...), custom_call_target="tpu_custom_call", output_to_operand_aliasing={{0}: (7, {})} | custom-call | flops 6000000 | bytes 1000 | tf_op jit(solution)/shard_map/weight_grad/pallas_call | solution.py:114
  596.0 21.9 %attend_bwd.6 = (bf16[1024,1024]{1,0:T(8,128)(2,1)}, f32[4,1,256]{2,1,0:T(1,128)}, f32[4,2,32,128]{3,2,1,0:T(8,128)}, bf16[2,256,1152]{2,1,0:T(8,128)(2,1)}, bf1...) custom-call(f32[8,128]{1,0:T(8,128)} %get-tuple-element.324.refs_0_, ...), custom_call_target="tpu_custom_call" | custom-call | flops 6000000 | bytes 1000 | tf_op jit(solution)/shard_map/attend_bwd/pallas_call | solution.py:114
  623.6 6.0 norm_bwd.13
  635.6 6.2 weight_grad.14
  641.8 22.3 %attend_bwd.7 = (bf16[1024,1024]{1,0:T(8,128)(2,1)}, f32[4,1,256]{2,1,0:T(1,128)}, f32[4,2,32,128]{3,2,1,0:T(8,128)}, bf16[2,256,1152]{2,1,0:T(8,128)(2,1)}, bf1...) custom-call(bf16[144,1152]{1,0:T(8,128)(2,1)} %bitcast.305, f32[8,128]{1,0:T(8,128)} %get-tuple-element.337.refs_1_, ...), custom_call_target="tpu_custom_call" | custom-call | flops 6000000 | bytes 1000 | tf_op jit(solution)/shard_map/attend_bwd/pallas_call | solution.py:114
  669.9 11.5 %weight_grad.15 = (bf16[1152,1152]{1,0:T(8,128)(2,1)}, f32[8,128]{1,0:T(8,128)}) custom-call(f32[8,128]{1,0:T(8,128)} %get-tuple-element.339.refs_0_, bf16[2,256,1152]{2,1,0:T(8,128)(2,1)} %get-tuple-element.206.refs_2_.refs_1_, bf16[2,256,1152]{2,1,0:T(8,128)(2,1)} %collective-permute-done.5.refs_3_.refs_2_, bf16[1024,1024]{1,0:T(8,128)(2,1)} %get-tuple-element.340.refs_3_, ...), custom_call_target="tpu_custom_call" | custom-call | flops 6000000 | bytes 1000 | tf_op jit(solution)/shard_map/weight_grad/pallas_call | solution.py:114
  686.7 6.2 reduce-scatter.7.cloned.1.call-done
  693.5 6.0 copy.143
  729.1 3.8 norm_bwd.14
  735.1 3.6 norm_bwd.15
  775.0 22.3 %reduce-scatter.11.cloned.1.call-done = bf16[1,144,1152]{1,2,0:T(8,128)(2,1)} async-done(((bf16[8,144,1152]{1,2,0:T(8,128)(2,1)}), bf16[1,144,1152]{1,2,0:T(8,128)(2,1)}) %reduce-scatter.11.cloned.1.call-update) | async-done | bytes 331792 | tf_op jit(solution)/shard_map/reduce_scatter | solution.py:1055
  802.4 4.7 multiply_reduce_fusion.5
  (562 shorter events, 228.6 us)
Async XLA Ops:
  7.2 71.0 %all-gather.5.cloned.1.call-start = ((), (), s32[]{:S(2)}) async-start(), calls=%async_computation.4 | async-start | bytes 2985984 | tf_op jit(solution)/shard_map/all_gather | solution.py:863
  11.4 150.6 %all-gather.7.cloned.1.call-start = ((), (), s32[]{:S(2)}) async-start(), calls=%async_computation.5 | async-start | bytes 5971968 | tf_op jit(solution)/shard_map/all_gather | solution.py:863
  15.3 202.7 %all-gather.9.cloned.1.call-start = ((), (), s32[]{:S(2)}) async-start(), calls=%async_computation.6 | async-start | bytes 2985984 | tf_op jit(solution)/shard_map/all_gather | solution.py:863
  19.0 25.1 %collective-permute-start.1 = (f32[33,576]{1,0:T(8,128)}, f32[33,576]{1,0:T(8,128)}, u32[]{:S(2)}, u32[]{:S(2)}) collective-permute-start(f32[33,576]{1,0:T(8,128)} %concatenate.58), channel_id=1, source_target_pairs={{0,4},{4,0},{8,12},{12,8},{16,20},{20,16},{24,28},{28,24},{1,5},{5... | collective-permute-start | bytes 228104 | tf_op jit(solution)/shard_map/ppermute | solution.py:795
  21.9 35.7 %collective-permute-start.4 = (bf16[2,256,1152]{2,1,0:T(8,128)(2,1)}, bf16[2,256,1152]{2,1,0:T(8,128)(2,1)}, u32[]{:S(2)}, u32[]{:S(2)}) collective-permute-start(bf16[2,256,1152]{2,1,0:T(8,128)(2,1)} %param.29), channel_id=1, source_target_pairs={{0,2},{1,3},{2,0},{3,1},{4,6},{5,7},{6,4},{7,5},{8,10},{9,11},{10,... | collective-permute-start | bytes 3538952 | tf_op jit(solution)/shard_map/ppermute | solution.py:795
  24.8 50.1 %collective-permute-start = (bf16[2,256,1152]{2,1,0:T(8,128)(2,1)}, bf16[2,256,1152]{2,1,0:T(8,128)(2,1)}, u32[]{:S(2)}, u32[]{:S(2)}) collective-permute-start(bf16[2,256,1152]{2,1,0:T(8,128)(2,1)} %multiply_convert_fusion), channel_id=1, source_target_pairs={{0,2},{1,3},{2,0},{3,1},{4,6},{5,7},{6,4},{7,5},{8,10},{9,11},{10,... | collective-permute-start | bytes 3538952 | tf_op jit(solution)/shard_map/ppermute | solution.py:795
  27.3 279.0 %all-gather.11.cloned.1.call-start = ((), (), s32[]{:S(2)}) async-start(), calls=%async_computation.7 | async-start | bytes 5971968 | tf_op jit(solution)/shard_map/all_gather | solution.py:863
  45.0 11.6 %collective-permute-start.2 = (f32[33,576]{1,0:T(8,128)S(1)}, f32[33,576]{1,0:T(8,128)S(1)}, u32[]{:S(2)}, u32[]{:S(2)}) collective-permute-start(f32[33,576]{1,0:T(8,128)S(1)} %pad_add_fusion.1), channel_id=1, source_target_pairs={{0,8},{4,12},{8,0},{12,4},{16,24},{20,28},{24,16},{28,20},{1,9},{5... | collective-permute-start | bytes 228104 | tf_op jit(solution)/shard_map/ppermute | solution.py:795
  56.6 13.7 %collective-permute-start.3 = (f32[33,576]{1,0:T(8,128)S(1)}, f32[33,576]{1,0:T(8,128)S(1)}, u32[]{:S(2)}, u32[]{:S(2)}) collective-permute-start(f32[33,576]{1,0:T(8,128)S(1)} %add.266), channel_id=1, source_target_pairs={{0,16},{4,20},{8,24},{12,28},{16,0},{20,4},{24,8},{28,12},{1,17},{... | collective-permute-start | bytes 228104 | tf_op jit(solution)/shard_map/ppermute | solution.py:795
  63.5 18.8 %collective-permute-start.5 = (bf16[2,256,1152]{2,1,0:T(8,128)(2,1)}, bf16[2,256,1152]{2,1,0:T(8,128)(2,1)}, u32[]{:S(2)}, u32[]{:S(2)}) collective-permute-start(bf16[2,256,1152]{2,1,0:T(8,128)(2,1)} %get-tuple-element.206.refs_2_.refs_1_), channel_id=1, source_target_pairs={{0,1},{1,0},{2,3},{3,2},{4,5},{5,4},{6,7},{7,6},{8,9},{9,8},{10,11... | collective-permute-start | bytes 3538952 | tf_op jit(solution)/shard_map/ppermute | solution.py:795
  101.5 3.3 collective-permute-start.6
  101.6 7.2 collective-permute-start.8
  107.3 28.3 %collective-permute-start.7 = (bf16[2,256,1152]{2,1,0:T(8,128)(2,1)}, bf16[2,256,1152]{2,1,0:T(8,128)(2,1)}, u32[]{:S(2)}, u32[]{:S(2)}) collective-permute-start(bf16[2,256,1152]{2,1,0:T(8,128)(2,1)} %get-tuple-element.211.refs_2_), channel_id=1, source_target_pairs={{0,2},{1,3},{2,0},{3,1},{4,6},{5,7},{6,4},{7,5},{8,10},{9,11},{10,... | collective-permute-start | bytes 3538952 | tf_op jit(solution)/shard_map/ppermute | solution.py:795
  127.7 8.6 %collective-permute-start.9 = (bf16[2,256,1152]{2,1,0:T(8,128)(2,1)}, bf16[2,256,1152]{2,1,0:T(8,128)(2,1)}, u32[]{:S(2)}, u32[]{:S(2)}) collective-permute-start(bf16[2,256,1152]{2,1,0:T(8,128)(2,1)} %get-tuple-element.217), channel_id=1, source_target_pairs={{0,1},{1,0},{2,3},{3,2},{4,5},{5,4},{6,7},{7,6},{8,9},{9,8},{10,11... | collective-permute-start | bytes 3538952 | tf_op jit(solution)/shard_map/ppermute | solution.py:795
  141.3 3.2 collective-permute-start.11
  141.3 33.6 %collective-permute-start.10 = (bf16[2,256,1152]{2,1,0:T(8,128)(2,1)}, bf16[2,256,1152]{2,1,0:T(8,128)(2,1)}, u32[]{:S(2)}, u32[]{:S(2)}) collective-permute-start(bf16[2,256,1152]{2,1,0:T(8,128)(2,1)} %get-tuple-element.218.refs_2_), channel_id=1, source_target_pairs={{0,2},{1,3},{2,0},{3,1},{4,6},{5,7},{6,4},{7,5},{8,10},{9,11},{10,... | collective-permute-start | bytes 3538952 | tf_op jit(solution)/shard_map/ppermute | solution.py:795
  174.9 385.1 %reduce-scatter.5.cloned.1.call-start = ((), (), s32[]{:S(2)}) async-start(), calls=%async_computation.8 | async-start | bytes 5971968 | tf_op jit(solution)/shard_map/reduce_scatter | solution.py:1055
  181.9 28.6 %collective-permute-start.13 = (bf16[2,256,1152]{2,1,0:T(8,128)(2,1)}, bf16[2,256,1152]{2,1,0:T(8,128)(2,1)}, u32[]{:S(2)}, u32[]{:S(2)}) collective-permute-start(bf16[2,256,1152]{2,1,0:T(8,128)(2,1)} %get-tuple-element.225.refs_2_), channel_id=1, source_target_pairs={{0,2},{1,3},{2,0},{3,1},{4,6},{5,7},{6,4},{7,5},{8,10},{9,11},{10,... | collective-permute-start | bytes 3538952 | tf_op jit(solution)/shard_map/ppermute | solution.py:795
  196.8 25.2 %collective-permute-start.15 = (bf16[2,256,1152]{2,1,0:T(8,128)(2,1)}, bf16[2,256,1152]{2,1,0:T(8,128)(2,1)}, u32[]{:S(2)}, u32[]{:S(2)}) collective-permute-start(bf16[2,256,1152]{2,1,0:T(8,128)(2,1)} %get-tuple-element.232), channel_id=1, source_target_pairs={{0,1},{1,0},{2,3},{3,2},{4,5},{5,4},{6,7},{7,6},{8,9},{9,8},{10,11... | collective-permute-start | bytes 3538952 | tf_op jit(solution)/shard_map/ppermute | solution.py:795
  226.7 28.7 %collective-permute-start.16 = (bf16[2,256,1152]{2,1,0:T(8,128)(2,1)}, bf16[2,256,1152]{2,1,0:T(8,128)(2,1)}, u32[]{:S(2)}, u32[]{:S(2)}) collective-permute-start(bf16[2,256,1152]{2,1,0:T(8,128)(2,1)} %get-tuple-element.233.refs_2_), channel_id=1, source_target_pairs={{0,2},{1,3},{2,0},{3,1},{4,6},{5,7},{6,4},{7,5},{8,10},{9,11},{10,... | collective-permute-start | bytes 3538952 | tf_op jit(solution)/shard_map/ppermute | solution.py:795
  248.7 7.2 collective-permute-start.18
  261.2 28.7 %collective-permute-start.19 = (bf16[2,256,1152]{2,1,0:T(8,128)(2,1)}, bf16[2,256,1152]{2,1,0:T(8,128)(2,1)}, u32[]{:S(2)}, u32[]{:S(2)}) collective-permute-start(bf16[2,256,1152]{2,1,0:T(8,128)(2,1)} %get-tuple-element.241.refs_2_), channel_id=1, source_target_pairs={{0,2},{1,3},{2,0},{3,1},{4,6},{5,7},{6,4},{7,5},{8,10},{9,11},{10,... | collective-permute-start | bytes 3538952 | tf_op jit(solution)/shard_map/ppermute | solution.py:795
  283.4 7.1 collective-permute-start.21
  295.1 11.1 %collective-permute-start.23 = (bf16[2,256,1152]{2,1,0:T(8,128)(2,1)}, bf16[2,256,1152]{2,1,0:T(8,128)(2,1)}, u32[]{:S(2)}, u32[]{:S(2)}) collective-permute-start(bf16[2,256,1152]{2,1,0:T(8,128)(2,1)} %get-tuple-element.250.refs_1_), channel_id=1, source_target_pairs={{0,1},{1,0},{2,3},{3,2},{4,5},{5,4},{6,7},{7,6},{8,9},{9,8},{10,11... | collective-permute-start | bytes 3538952 | tf_op jit(solution)/shard_map/ppermute | solution.py:795
  298.5 19.7 %collective-permute-start.24 = (bf16[2,256,1152]{2,1,0:T(8,128)(2,1)}, bf16[2,256,1152]{2,1,0:T(8,128)(2,1)}, u32[]{:S(2)}, u32[]{:S(2)}) collective-permute-start(bf16[2,256,1152]{2,1,0:T(8,128)(2,1)} %get-tuple-element.515.refs_1_.refs_3_), channel_id=1, source_target_pairs={{0,1},{1,0},{2,3},{3,2},{4,5},{5,4},{6,7},{7,6},{8,9},{9,8},{10,11... | collective-permute-start | bytes 3538952 | tf_op jit(solution)/shard_map/ppermute | solution.py:795
  299.0 32.7 %collective-permute-start.22 = (bf16[2,256,1152]{2,1,0:T(8,128)(2,1)}, bf16[2,256,1152]{2,1,0:T(8,128)(2,1)}, u32[]{:S(2)}, u32[]{:S(2)}) collective-permute-start(bf16[2,256,1152]{2,1,0:T(8,128)(2,1)} %get-tuple-element.248.refs_2_), channel_id=1, source_target_pairs={{0,2},{1,3},{2,0},{3,1},{4,6},{5,7},{6,4},{7,5},{8,10},{9,11},{10,... | collective-permute-start | bytes 3538952 | tf_op jit(solution)/shard_map/ppermute | solution.py:795
  331.2 4.9 collective-permute-start.26
  344.9 14.9 %collective-permute-start.29 = (bf16[2,256,1152]{2,1,0:T(8,128)(2,1)}, bf16[2,256,1152]{2,1,0:T(8,128)(2,1)}, u32[]{:S(2)}, u32[]{:S(2)}) collective-permute-start(bf16[2,256,1152]{2,1,0:T(8,128)(2,1)} %get-tuple-element.514.refs_1_.refs_4_.refs_3_), channel_id=1, source_target_pairs={{0,1},{1,0},{2,3},{3,2},{4,5},{5,4},{6,7},{7,6},{8,9},{9,8},{10,11... | collective-permute-start | bytes 3538952 | tf_op jit(solution)/shard_map/ppermute | solution.py:795
  345.3 41.0 %collective-permute-start.27 = (bf16[3,256,1152]{2,1,0:T(8,128)(2,1)}, bf16[3,256,1152]{2,1,0:T(8,128)(2,1)}, u32[]{:S(2)}, u32[]{:S(2)}) collective-permute-start(bf16[3,256,1152]{2,1,0:T(8,128)(2,1)} %get-tuple-element.258.refs_1_), channel_id=1, source_target_pairs={{0,2},{1,3},{2,0},{3,1},{4,6},{5,7},{6,4},{7,5},{8,10},{9,11},{10,... | collective-permute-start | bytes 5308424 | tf_op jit(solution)/shard_map/ppermute | solution.py:795
  372.8 14.1 %collective-permute-start.30 = (bf16[2,256,1152]{2,1,0:T(8,128)(2,1)}, bf16[2,256,1152]{2,1,0:T(8,128)(2,1)}, u32[]{:S(2)}, u32[]{:S(2)}) collective-permute-start(bf16[2,256,1152]{2,1,0:T(8,128)(2,1)} %get-tuple-element.270), channel_id=1, source_target_pairs={{0,1},{1,0},{2,3},{3,2},{4,5},{5,4},{6,7},{7,6},{8,9},{9,8},{10,11... | collective-permute-start | bytes 3538952 | tf_op jit(solution)/shard_map/ppermute | solution.py:795
  372.9 13.9 %collective-permute-start.31 = (bf16[2,256,1152]{2,1,0:T(8,128)(2,1)}, bf16[2,256,1152]{2,1,0:T(8,128)(2,1)}, u32[]{:S(2)}, u32[]{:S(2)}) collective-permute-start(bf16[2,256,1152]{2,1,0:T(8,128)(2,1)} %get-tuple-element.272), channel_id=1, source_target_pairs={{0,1},{1,0},{2,3},{3,2},{4,5},{5,4},{6,7},{7,6},{8,9},{9,8},{10,11... | collective-permute-start | bytes 3538952 | tf_op jit(solution)/shard_map/ppermute | solution.py:795
  408.2 212.2 %reduce-scatter.9.cloned.1.call-start = ((), (), s32[]{:S(2)}) async-start(), calls=%async_computation.10 | async-start | bytes 2985984 | tf_op jit(solution)/shard_map/reduce_scatter | solution.py:1055
  409.4 41.3 %collective-permute-start.32 = (bf16[3,256,1152]{2,1,0:T(8,128)(2,1)}, bf16[3,256,1152]{2,1,0:T(8,128)(2,1)}, u32[]{:S(2)}, u32[]{:S(2)}) collective-permute-start(bf16[3,256,1152]{2,1,0:T(8,128)(2,1)} %get-tuple-element.273.refs_1_), channel_id=1, source_target_pairs={{0,2},{1,3},{2,0},{3,1},{4,6},{5,7},{6,4},{7,5},{8,10},{9,11},{10,... | collective-permute-start | bytes 5308424 | tf_op jit(solution)/shard_map/ppermute | solution.py:795
  435.2 16.1 %collective-permute-start.34 = (bf16[2,256,1152]{2,1,0:T(8,128)(2,1)}, bf16[2,256,1152]{2,1,0:T(8,128)(2,1)}, u32[]{:S(2)}, u32[]{:S(2)}) collective-permute-start(bf16[2,256,1152]{2,1,0:T(8,128)(2,1)} %get-tuple-element.287), channel_id=1, source_target_pairs={{0,1},{1,0},{2,3},{3,2},{4,5},{5,4},{6,7},{7,6},{8,9},{9,8},{10,11... | collective-permute-start | bytes 3538952 | tf_op jit(solution)/shard_map/ppermute | solution.py:795
  457.3 3.2 collective-permute-start.36
  457.4 31.6 %collective-permute-start.35 = (bf16[2,256,1152]{2,1,0:T(8,128)(2,1)}, bf16[2,256,1152]{2,1,0:T(8,128)(2,1)}, u32[]{:S(2)}, u32[]{:S(2)}) collective-permute-start(bf16[2,256,1152]{2,1,0:T(8,128)(2,1)} %get-tuple-element.288.refs_1_), channel_id=1, source_target_pairs={{0,2},{1,3},{2,0},{3,1},{4,6},{5,7},{6,4},{7,5},{8,10},{9,11},{10,... | collective-permute-start | bytes 3538952 | tf_op jit(solution)/shard_map/ppermute | solution.py:795
  482.6 7.0 collective-permute-start.37
  507.0 185.9 %reduce-scatter.7.cloned.1.call-start = ((), (), s32[]{:S(2)}) async-start(), calls=%async_computation.9 | async-start | bytes 5971968 | tf_op jit(solution)/shard_map/reduce_scatter | solution.py:1055
  508.7 28.2 %collective-permute-start.38 = (bf16[2,256,1152]{2,1,0:T(8,128)(2,1)}, bf16[2,256,1152]{2,1,0:T(8,128)(2,1)}, u32[]{:S(2)}, u32[]{:S(2)}) collective-permute-start(bf16[2,256,1152]{2,1,0:T(8,128)(2,1)} %get-tuple-element.297.refs_1_), channel_id=1, source_target_pairs={{0,2},{1,3},{2,0},{3,1},{4,6},{5,7},{6,4},{7,5},{8,10},{9,11},{10,... | collective-permute-start | bytes 3538952 | tf_op jit(solution)/shard_map/ppermute | solution.py:795
  525.6 12.0 %collective-permute-start.40 = (bf16[2,256,1152]{2,1,0:T(8,128)(2,1)}, bf16[2,256,1152]{2,1,0:T(8,128)(2,1)}, u32[]{:S(2)}, u32[]{:S(2)}) collective-permute-start(bf16[2,256,1152]{2,1,0:T(8,128)(2,1)} %get-tuple-element.307), channel_id=1, source_target_pairs={{0,1},{1,0},{2,3},{3,2},{4,5},{5,4},{6,7},{7,6},{8,9},{9,8},{10,11... | collective-permute-start | bytes 3538952 | tf_op jit(solution)/shard_map/ppermute | solution.py:795
  543.5 3.2 collective-permute-start.42
  543.6 28.7 %collective-permute-start.41 = (bf16[2,256,1152]{2,1,0:T(8,128)(2,1)}, bf16[2,256,1152]{2,1,0:T(8,128)(2,1)}, u32[]{:S(2)}, u32[]{:S(2)}) collective-permute-start(bf16[2,256,1152]{2,1,0:T(8,128)(2,1)} %get-tuple-element.308.refs_1_), channel_id=1, source_target_pairs={{0,2},{1,3},{2,0},{3,1},{4,6},{5,7},{6,4},{7,5},{8,10},{9,11},{10,... | collective-permute-start | bytes 3538952 | tf_op jit(solution)/shard_map/ppermute | solution.py:795
  559.9 13.0 %collective-permute-start.43 = (bf16[2,256,1152]{2,1,0:T(8,128)(2,1)}, bf16[2,256,1152]{2,1,0:T(8,128)(2,1)}, u32[]{:S(2)}, u32[]{:S(2)}) collective-permute-start(bf16[2,256,1152]{2,1,0:T(8,128)(2,1)} %get-tuple-element.318), channel_id=1, source_target_pairs={{0,1},{1,0},{2,3},{3,2},{4,5},{5,4},{6,7},{7,6},{8,9},{9,8},{10,11... | collective-permute-start | bytes 3538952 | tf_op jit(solution)/shard_map/ppermute | solution.py:795
  590.4 206.8 %reduce-scatter.11.cloned.1.call-start = ((), (), s32[]{:S(2)}) async-start(), calls=%async_computation.11 | async-start | bytes 5308416 | tf_op jit(solution)/shard_map/reduce_scatter | solution.py:1055
  591.6 3.4 collective-permute-start.45
  593.6 29.4 %collective-permute-start.44 = (bf16[2,256,1152]{2,1,0:T(8,128)(2,1)}, bf16[2,256,1152]{2,1,0:T(8,128)(2,1)}, u32[]{:S(2)}, u32[]{:S(2)}) collective-permute-start(bf16[2,256,1152]{2,1,0:T(8,128)(2,1)} %get-tuple-element.319.refs_1_), channel_id=1, source_target_pairs={{0,2},{1,3},{2,0},{3,1},{4,6},{5,7},{6,4},{7,5},{8,10},{9,11},{10,... | collective-permute-start | bytes 3538952 | tf_op jit(solution)/shard_map/ppermute | solution.py:795
  618.0 5.6 collective-permute-start.46
  629.6 6.1 collective-permute-start.48
  633.7 77.5 %collective-permute-start.47 = (bf16[1,256,1152]{2,1,0:T(8,128)(2,1)}, bf16[1,256,1152]{2,1,0:T(8,128)(2,1)}, u32[]{:S(2)}, u32[]{:S(2)}) collective-permute-start(bf16[1,256,1152]{2,1,0:T(8,128)(2,1)} %slice.288), channel_id=1, source_target_pairs={{0,2},{1,3},{2,0},{3,1},{4,6},{5,7},{6,4},{7,5},{8,10},{9,11},{10,... | collective-permute-start | bytes 1769480 | tf_op jit(solution)/shard_map/ppermute | solution.py:795
  665.6 46.2 %collective-permute-start.49 = (bf16[2,256,1152]{2,1,0:T(8,128)(2,1)}, bf16[2,256,1152]{2,1,0:T(8,128)(2,1)}, u32[]{:S(2)}, u32[]{:S(2)}) collective-permute-start(bf16[2,256,1152]{2,1,0:T(8,128)(2,1)} %get-tuple-element.347), channel_id=1, source_target_pairs={{0,1},{1,0},{2,3},{3,2},{4,5},{5,4},{6,7},{7,6},{8,9},{9,8},{10,11... | collective-permute-start | bytes 3538952 | tf_op jit(solution)/shard_map/ppermute | solution.py:795
  709.7 8.2 collective-permute-start.61
  716.5 18.1 %collective-permute-start.50 = (bf16[1,256,1152]{2,1,0:T(8,128)(2,1)}, bf16[1,256,1152]{2,1,0:T(8,128)(2,1)}, u32[]{:S(2)}, u32[]{:S(2)}) collective-permute-start(bf16[1,256,1152]{2,1,0:T(8,128)(2,1)} %slice.289), channel_id=1, source_target_pairs={{0,2},{1,3},{2,0},{3,1},{4,6},{5,7},{6,4},{7,5},{8,10},{9,11},{10,... | collective-permute-start | bytes 1769480 | tf_op jit(solution)/shard_map/ppermute | solution.py:795
  718.6 4.4 collective-permute-start.62
  723.7 4.9 collective-permute-start.63
  729.1 3.8 collective-permute-start.64
  734.2 12.0 %collective-permute-start.65 = (f32[8,128]{1,0:T(8,128)}, f32[8,128]{1,0:T(8,128)}, u32[]{:S(2)}, u32[]{:S(2)}) collective-permute-start(f32[8,128]{1,0:T(8,128)} %add.332), channel_id=1, source_target_pairs={{0,2},{1,3},{2,0},{3,1},{4,6},{5,7},{6,4},{7,5},{8,10},{9,11},{10,... | collective-permute-start | bytes 12296 | tf_op jit(solution)/shard_map/ppermute | solution.py:795
  741.8 7.7 collective-permute-start.51
  749.6 8.8 %collective-permute-start.52 = (f32[224,128]{1,0:T(8,128)S(1)}, f32[224,128]{1,0:T(8,128)S(1)}, u32[]{:S(2)}, u32[]{:S(2)}) collective-permute-start(f32[224,128]{1,0:T(8,128)S(1)} %fusion.45), channel_id=1, source_target_pairs={{0,8},{4,12},{8,0},{12,4},{16,24},{20,28},{24,16},{28,20},{1,9},{5... | collective-permute-start | bytes 344072 | tf_op jit(solution)/shard_map/ppermute | solution.py:795
  758.4 7.0 collective-permute-start.53
  768.8 4.8 collective-permute-start.55
  808.6 3.6 collective-permute-start.56
  812.2 3.6 collective-permute-start.57
  815.9 4.7 collective-permute-start.58
  821.8 3.6 collective-permute-start.60
  (96 other events, 507.1 us)
Sparse Core Ops, SparseCore 0:
  11.5 62.1 all-gather.4
  76.5 85.4 all-gather.6
  164.7 53.2 all-gather.8
  220.6 85.6 all-gather.10
  408.3 102.2 reduce-scatter.4
  514.5 70.0 reduce-scatter.8
  590.6 102.2 reduce-scatter.6
  699.7 97.5 reduce-scatter.10
